TPU v7x, 256 devices: a whole 4x4x8 slice. The times are simulated.
256 devices in a mesh: rep: 8 (over z_hi, core), ep: 32 (over z_lo, x, y).
Axes of the slice: x: 4, y: 4, z: 8 (z_hi: 4, z_lo: 2; z = z_hi * 2 + z_lo), core: 2. Of those that a mesh axis runs over, the one named last changes fastest.
Arguments:
- expert_inputs: bfloat16 [32, 1024, 1024], P('ep', 'rep'), may hold values from -6 to 6
- expert_cotangent: bfloat16 [32, 1024, 3584], P('ep', 'rep'), may hold values from -0.29882812 to 0.29882812
- row_counts: int32 [32, 8], P('ep', 'rep'), may hold values from 1 to 128, as said below
- expert_master: float32 [32, 1024, 3584], P('ep', 'rep'), may hold values from -6 to 6
- expert_moment: float32 [32, 1024, 3584], P('ep', 'rep'), may hold values from -0.6 to 0.6
- expert_variance: float32 [32, 1024, 3584], P('ep', 'rep'), may hold values from 0.0001 to 1
- layer_inputs: bfloat16 [32768, 7168], P(('rep', 'ep')), may hold values from -24 to 24
- layer_cotangent: bfloat16 [32768, 576], P(('rep', 'ep')), may hold values from -0.059814453 to 0.059814453
- dense_master: float32 [7168, 576], P(('rep', 'ep')), may hold values from -6 to 6
- dense_moment: float32 [7168, 576], P(('rep', 'ep')), may hold values from -0.6 to 0.6
- dense_variance: float32 [7168, 576], P(('rep', 'ep')), may hold values from 0.0001 to 1
Outputs:
- expert_updated: float32 [32, 1024, 3584], P('ep', 'rep')
- dense_updated: float32 [7168, 576], P(('rep', 'ep'))
Inputs may be any that keep to these rules, and one draw needn't show every extreme that they name: `row_counts`: live slots of each expert from each replica; some pair has exactly 128 live slots and some pair exactly one.
All inputs are finite; a program needn't handle non-finite values.
Results may differ from a plain program's by a relative error of at most 0.0023.
Values may be sent and summed in bfloat16 or wider, within the bound.
No kernel may reach another device: no remote copies, remote signals or barrier semaphores. Data moves between devices by JAX's collectives and lax.ppermute only.
A program may use at most 128 MiB of HBM per device.

v0:
```python
import jax
import jax.numpy as jnp
from jax import lax
from jax.sharding import PartitionSpec as P

beta_first = 0.9
beta_second = 0.999
step_count = 1000.0
learn_rate = 0.05
weight_decay = 0.1
epsilon = 1e-08


def adam_step(master, moment, variance, gradient):
    moment_new = beta_first * moment + (1.0 - beta_first) * gradient
    variance_new = beta_second * variance + (1.0 - beta_second) * gradient * gradient
    first_fix = 1.0 - beta_first**step_count
    second_fix = 1.0 - beta_second**step_count
    update = moment_new / first_fix / (jnp.sqrt(variance_new / second_fix) + epsilon)
    return master - learn_rate * (update + weight_decay * master)


def transpose_product(left, right):
    return lax.dot_general(
        left, right, (((0,), (0,)), ((), ())), preferred_element_type=jnp.float32
    )


def on_device(
    expert_inputs,
    expert_cotangent,
    row_counts,
    expert_master,
    expert_moment,
    expert_variance,
    layer_inputs,
    layer_cotangent,
    dense_master,
    dense_moment,
    dense_variance,
):
    inputs_local = expert_inputs[0]
    cotangent_local = expert_cotangent[0]
    slot_count = inputs_local.shape[0]
    live_rows = jnp.arange(slot_count) < row_counts[0, 0]
    masked = jnp.where(live_rows[:, None], cotangent_local, jnp.zeros_like(cotangent_local))
    columns = inputs_local
    expert_grad = lax.psum_scatter(
        transpose_product(columns, masked).astype(jnp.bfloat16),
        "rep",
        scatter_dimension=0,
        tiled=True,
    ).astype(jnp.float32)
    expert_updated = adam_step(expert_master[0], expert_moment[0], expert_variance[0], expert_grad)[
        None
    ]
    columns = layer_inputs
    dense_grad = lax.psum_scatter(
        transpose_product(columns, layer_cotangent), ("rep", "ep"), scatter_dimension=0, tiled=True
    )
    dense_updated = adam_step(dense_master, dense_moment, dense_variance, dense_grad)
    return (expert_updated, dense_updated)


def solution(mesh):
    in_specs = (
        P("ep", "rep", None),
        P("ep", "rep", None),
        P("ep", "rep"),
        P("ep", "rep", None),
        P("ep", "rep", None),
        P("ep", "rep", None),
        P(("rep", "ep"), None),
        P(("rep", "ep"), None),
        P(("rep", "ep"), None),
        P(("rep", "ep"), None),
        P(("rep", "ep"), None),
    )
    out_specs = (P("ep", "rep", None), P(("rep", "ep"), None))
    return jax.shard_map(
        on_device, mesh=mesh, in_specs=in_specs, out_specs=out_specs, check_vma=False
    )
```

profile of v0, /device:TPU:8, one launch (start us, length us, event | category | flops | bytes accessed | tf_op | source)
XLA Modules:
  0.0 968.2 jit_solution(1420209636016464006)
XLA Ops:
  7.2 0.0 copy-start
  7.2 0.0 reduce-scatter.6.cloned.1.call-start
  8.0 6.3 fusion.1
  14.3 10.0 %copy.21 = bf16[1024,3584]{1,0:T(8,128)(2,1)} copy(bf16[1024,3584]{0,1:T(8,128)(2,1)} %fusion.1) | data formatting | bytes 14680064
  24.3 0.0 reduce-scatter.6.cloned.1.call-update
  24.4 0.9 copy-done.1
  25.2 7.7 fusion.24
  32.9 750.8 %fusion = f32[32,576]{1,0:T(8,128)S(1)} fusion(f32[7168,576]{1,0:T(8,128)} %fusion.24), kind=kCustom, calls=%all-reduce-scatter | all-reduce-scatter fusion | flops 4718593 | bytes 16588800
  783.8 4.3 collective-permute-start
  788.0 1.3 collective-permute-start.31
  789.4 1.3 collective-permute-start.1
  790.7 2.5 collective-permute-start.10
  793.1 6.5 collective-permute-start.11
  799.6 1.3 collective-permute-start.12
  800.9 5.6 collective-permute-start.13
  806.5 3.7 collective-permute-start.14
  810.2 4.7 collective-permute-start.15
  814.9 1.4 collective-permute-start.16
  816.3 7.2 collective-permute-start.17
  823.5 6.2 collective-permute-start.18
  829.7 3.7 collective-permute-start.19
  833.4 4.6 collective-permute-start.2
  838.0 2.2 collective-permute-start.20
  840.2 2.9 collective-permute-start.21
  843.1 4.5 collective-permute-start.22
  847.6 2.3 collective-permute-start.23
  850.0 2.5 collective-permute-start.24
  852.5 4.8 collective-permute-start.25
  857.4 1.3 collective-permute-start.26
  858.7 2.5 collective-permute-start.27
  861.3 3.1 collective-permute-start.28
  864.5 2.2 collective-permute-start.29
  866.7 2.5 collective-permute-start.3
  869.2 1.3 collective-permute-start.30
  870.5 1.3 collective-permute-start.4
  871.9 7.0 collective-permute-start.5
  878.9 3.1 collective-permute-start.6
  882.0 2.8 collective-permute-start.7
  884.8 6.0 collective-permute-start.8
  890.7 3.4 collective-permute-start.9
  894.2 2.7 copy.17
  896.9 2.8 copy.18
  899.7 2.8 copy.19
  902.5 47.7 %concatenate = f32[1052,576]{1,0:T(8,128)} concatenate(f32[28,576]{1,0:T(8,128)S(1)} %collective-permute-done.31, f32[32,576]{1,0:T(8,128)} %copy-done.13, f32[32,576]{1,0:T(8,128)} %copy-done.11, f32[32,576]{1,0:T(8,128)} %copy-done.10, f32[32,576]{1,0:T(8,128)} %copy-done.9, f32[32,576]{1,0:T(8,128)} %copy-done.8, f32[32,576]{1,0:T(8,128)} %copy-done.7, f32[32,576]{1,0:T(8,128)} %copy-done.6, ...), dimensions={0} | concatenate | bytes 4847616
  950.2 1.6 multiply_subtract_fusion
  951.8 1.5 copy.22
  953.4 5.2 fusion.7
  958.6 2.7 copy.20
  (63 shorter events, 0.2 us)
Async XLA Ops:
  7.2 17.2 %copy-start = (bf16[128,7168]{1,0:T(8,128)(2,1)S(1)}, bf16[128,7168]{1,0:T(8,128)(2,1)}, u32[]{:S(2)}) copy-start(bf16[128,7168]{1,0:T(8,128)(2,1)} %param.17) | copy-start | bytes 5505028
  7.2 944.6 %reduce-scatter.6.cloned.1.call-start = ((), (), s32[]{:S(2)}) async-start(), calls=%async_computation.1 | async-start | bytes 8257536
  24.3 0.9 copy-start.1
  783.8 17.1 %collective-permute-start = (f32[32,576]{1,0:T(8,128)S(1)}, f32[32,576]{1,0:T(8,128)S(1)}, u32[]{:S(2)}, u32[]{:S(2)}) collective-permute-start(f32[32,576]{1,0:T(8,128)S(1)} %fusion), channel_id=1, source_target_pairs={{0,1},{1,2},{2,3},{3,4},{4,5},{5,6},{6,7},{7,8},{8,9},{9,10},{10,1... | collective-permute-start | bytes 221192
  788.0 11.5 %collective-permute-start.31 = (f32[28,576]{1,0:T(8,128)S(1)}, f32[28,576]{1,0:T(8,128)S(1)}, u32[]{:S(2)}, u32[]{:S(2)}) collective-permute-start(f32[28,576]{1,0:T(8,128)S(1)} %slice), channel_id=1, source_target_pairs={{0,32},{1,33},{2,34},{3,35},{4,36},{5,37},{6,38},{7,39},{8,40},{9,... | collective-permute-start | bytes 193544
  789.4 17.2 %collective-permute-start.1 = (f32[32,576]{1,0:T(8,128)S(1)}, f32[32,576]{1,0:T(8,128)S(1)}, u32[]{:S(2)}, u32[]{:S(2)}) collective-permute-start(f32[32,576]{1,0:T(8,128)S(1)} %fusion), channel_id=1, source_target_pairs={{0,2},{1,3},{2,4},{3,5},{4,6},{5,7},{6,8},{7,9},{8,10},{9,11},{10,... | collective-permute-start | bytes 221192
  790.7 19.6 %collective-permute-start.10 = (f32[32,576]{1,0:T(8,128)S(1)}, f32[32,576]{1,0:T(8,128)S(1)}, u32[]{:S(2)}, u32[]{:S(2)}) collective-permute-start(f32[32,576]{1,0:T(8,128)S(1)} %fusion), channel_id=1, source_target_pairs={{0,11},{1,12},{2,13},{3,14},{4,15},{5,16},{6,17},{7,18},{8,19},{9,... | collective-permute-start | bytes 221192
  793.1 21.8 %collective-permute-start.11 = (f32[32,576]{1,0:T(8,128)S(1)}, f32[32,576]{1,0:T(8,128)S(1)}, u32[]{:S(2)}, u32[]{:S(2)}) collective-permute-start(f32[32,576]{1,0:T(8,128)S(1)} %fusion), channel_id=1, source_target_pairs={{0,12},{1,13},{2,14},{3,15},{4,16},{5,17},{6,18},{7,19},{8,20},{9,... | collective-permute-start | bytes 221192
  799.6 16.7 %collective-permute-start.12 = (f32[32,576]{1,0:T(8,128)S(1)}, f32[32,576]{1,0:T(8,128)S(1)}, u32[]{:S(2)}, u32[]{:S(2)}) collective-permute-start(f32[32,576]{1,0:T(8,128)S(1)} %fusion), channel_id=1, source_target_pairs={{0,13},{1,14},{2,15},{3,16},{4,17},{5,18},{6,19},{7,20},{8,21},{9,... | collective-permute-start | bytes 221192
  800.9 22.6 %collective-permute-start.13 = (f32[32,576]{1,0:T(8,128)S(1)}, f32[32,576]{1,0:T(8,128)S(1)}, u32[]{:S(2)}, u32[]{:S(2)}) collective-permute-start(f32[32,576]{1,0:T(8,128)S(1)} %fusion), channel_id=1, source_target_pairs={{0,14},{1,15},{2,16},{3,17},{4,18},{5,19},{6,20},{7,21},{8,22},{9,... | collective-permute-start | bytes 221192
  806.5 23.2 %collective-permute-start.14 = (f32[32,576]{1,0:T(8,128)S(1)}, f32[32,576]{1,0:T(8,128)S(1)}, u32[]{:S(2)}, u32[]{:S(2)}) collective-permute-start(f32[32,576]{1,0:T(8,128)S(1)} %fusion), channel_id=1, source_target_pairs={{0,15},{1,16},{2,17},{3,18},{4,19},{5,20},{6,21},{7,22},{8,23},{9,... | collective-permute-start | bytes 221192
  810.2 23.1 %collective-permute-start.15 = (f32[32,576]{1,0:T(8,128)S(1)}, f32[32,576]{1,0:T(8,128)S(1)}, u32[]{:S(2)}, u32[]{:S(2)}) collective-permute-start(f32[32,576]{1,0:T(8,128)S(1)} %fusion), channel_id=1, source_target_pairs={{0,16},{1,17},{2,18},{3,19},{4,20},{5,21},{6,22},{7,23},{8,24},{9,... | collective-permute-start | bytes 221192
  814.9 23.1 %collective-permute-start.16 = (f32[32,576]{1,0:T(8,128)S(1)}, f32[32,576]{1,0:T(8,128)S(1)}, u32[]{:S(2)}, u32[]{:S(2)}) collective-permute-start(f32[32,576]{1,0:T(8,128)S(1)} %fusion), channel_id=1, source_target_pairs={{0,17},{1,18},{2,19},{3,20},{4,21},{5,22},{6,23},{7,24},{8,25},{9,... | collective-permute-start | bytes 221192
  816.3 23.9 %collective-permute-start.17 = (f32[32,576]{1,0:T(8,128)S(1)}, f32[32,576]{1,0:T(8,128)S(1)}, u32[]{:S(2)}, u32[]{:S(2)}) collective-permute-start(f32[32,576]{1,0:T(8,128)S(1)} %fusion), channel_id=1, source_target_pairs={{0,18},{1,19},{2,20},{3,21},{4,22},{5,23},{6,24},{7,25},{8,26},{9,... | collective-permute-start | bytes 221192
  823.5 19.6 %collective-permute-start.18 = (f32[32,576]{1,0:T(8,128)S(1)}, f32[32,576]{1,0:T(8,128)S(1)}, u32[]{:S(2)}, u32[]{:S(2)}) collective-permute-start(f32[32,576]{1,0:T(8,128)S(1)} %fusion), channel_id=1, source_target_pairs={{0,19},{1,20},{2,21},{3,22},{4,23},{5,24},{6,25},{7,26},{8,27},{9,... | collective-permute-start | bytes 221192
  829.7 17.9 %collective-permute-start.19 = (f32[32,576]{1,0:T(8,128)S(1)}, f32[32,576]{1,0:T(8,128)S(1)}, u32[]{:S(2)}, u32[]{:S(2)}) collective-permute-start(f32[32,576]{1,0:T(8,128)S(1)} %fusion), channel_id=1, source_target_pairs={{0,20},{1,21},{2,22},{3,23},{4,24},{5,25},{6,26},{7,27},{8,28},{9,... | collective-permute-start | bytes 221192
  833.4 16.6 %collective-permute-start.2 = (f32[32,576]{1,0:T(8,128)S(1)}, f32[32,576]{1,0:T(8,128)S(1)}, u32[]{:S(2)}, u32[]{:S(2)}) collective-permute-start(f32[32,576]{1,0:T(8,128)S(1)} %fusion), channel_id=1, source_target_pairs={{0,3},{1,4},{2,5},{3,6},{4,7},{5,8},{6,9},{7,10},{8,11},{9,12},{10... | collective-permute-start | bytes 221192
  838.0 14.6 %collective-permute-start.20 = (f32[32,576]{1,0:T(8,128)S(1)}, f32[32,576]{1,0:T(8,128)S(1)}, u32[]{:S(2)}, u32[]{:S(2)}) collective-permute-start(f32[32,576]{1,0:T(8,128)S(1)} %fusion), channel_id=1, source_target_pairs={{0,21},{1,22},{2,23},{3,24},{4,25},{5,26},{6,27},{7,28},{8,29},{9,... | collective-permute-start | bytes 221192
  840.2 17.2 %collective-permute-start.21 = (f32[32,576]{1,0:T(8,128)S(1)}, f32[32,576]{1,0:T(8,128)S(1)}, u32[]{:S(2)}, u32[]{:S(2)}) collective-permute-start(f32[32,576]{1,0:T(8,128)S(1)} %fusion), channel_id=1, source_target_pairs={{0,22},{1,23},{2,24},{3,25},{4,26},{5,27},{6,28},{7,29},{8,30},{9,... | collective-permute-start | bytes 221192
  843.1 15.6 %collective-permute-start.22 = (f32[32,576]{1,0:T(8,128)S(1)}, f32[32,576]{1,0:T(8,128)S(1)}, u32[]{:S(2)}, u32[]{:S(2)}) collective-permute-start(f32[32,576]{1,0:T(8,128)S(1)} %fusion), channel_id=1, source_target_pairs={{0,23},{1,24},{2,25},{3,26},{4,27},{5,28},{6,29},{7,30},{8,31},{9,... | collective-permute-start | bytes 221192
  847.6 13.6 %collective-permute-start.23 = (f32[32,576]{1,0:T(8,128)S(1)}, f32[32,576]{1,0:T(8,128)S(1)}, u32[]{:S(2)}, u32[]{:S(2)}) collective-permute-start(f32[32,576]{1,0:T(8,128)S(1)} %fusion), channel_id=1, source_target_pairs={{0,24},{1,25},{2,26},{3,27},{4,28},{5,29},{6,30},{7,31},{8,32},{9,... | collective-permute-start | bytes 221192
  850.0 14.5 %collective-permute-start.24 = (f32[32,576]{1,0:T(8,128)S(1)}, f32[32,576]{1,0:T(8,128)S(1)}, u32[]{:S(2)}, u32[]{:S(2)}) collective-permute-start(f32[32,576]{1,0:T(8,128)S(1)} %fusion), channel_id=1, source_target_pairs={{0,25},{1,26},{2,27},{3,28},{4,29},{5,30},{6,31},{7,32},{8,33},{9,... | collective-permute-start | bytes 221192
  852.5 14.1 %collective-permute-start.25 = (f32[32,576]{1,0:T(8,128)S(1)}, f32[32,576]{1,0:T(8,128)S(1)}, u32[]{:S(2)}, u32[]{:S(2)}) collective-permute-start(f32[32,576]{1,0:T(8,128)S(1)} %fusion), channel_id=1, source_target_pairs={{0,26},{1,27},{2,28},{3,29},{4,30},{5,31},{6,32},{7,33},{8,34},{9,... | collective-permute-start | bytes 221192
  857.4 11.8 %collective-permute-start.26 = (f32[32,576]{1,0:T(8,128)S(1)}, f32[32,576]{1,0:T(8,128)S(1)}, u32[]{:S(2)}, u32[]{:S(2)}) collective-permute-start(f32[32,576]{1,0:T(8,128)S(1)} %fusion), channel_id=1, source_target_pairs={{0,27},{1,28},{2,29},{3,30},{4,31},{5,32},{6,33},{7,34},{8,35},{9,... | collective-permute-start | bytes 221192
  858.7 11.8 %collective-permute-start.27 = (f32[32,576]{1,0:T(8,128)S(1)}, f32[32,576]{1,0:T(8,128)S(1)}, u32[]{:S(2)}, u32[]{:S(2)}) collective-permute-start(f32[32,576]{1,0:T(8,128)S(1)} %fusion), channel_id=1, source_target_pairs={{0,28},{1,29},{2,30},{3,31},{4,32},{5,33},{6,34},{7,35},{8,36},{9,... | collective-permute-start | bytes 221192
  861.3 35.6 %copy-start.5 = (f32[32,576]{1,0:T(8,128)}, f32[32,576]{1,0:T(8,128)S(1)}, u32[]{:S(2)}) copy-start(f32[32,576]{1,0:T(8,128)S(1)} %collective-permute-done.23) | copy-start | bytes 221188
  861.3 10.6 %collective-permute-start.28 = (f32[32,576]{1,0:T(8,128)S(1)}, f32[32,576]{1,0:T(8,128)S(1)}, u32[]{:S(2)}, u32[]{:S(2)}) collective-permute-start(f32[32,576]{1,0:T(8,128)S(1)} %fusion), channel_id=1, source_target_pairs={{0,29},{1,30},{2,31},{3,32},{4,33},{5,34},{6,35},{7,36},{8,37},{9,... | collective-permute-start | bytes 221192
  864.4 32.5 %copy-start.6 = (f32[32,576]{1,0:T(8,128)}, f32[32,576]{1,0:T(8,128)S(1)}, u32[]{:S(2)}) copy-start(f32[32,576]{1,0:T(8,128)S(1)} %collective-permute-done.24) | copy-start | bytes 221188
  864.5 14.4 %collective-permute-start.29 = (f32[32,576]{1,0:T(8,128)S(1)}, f32[32,576]{1,0:T(8,128)S(1)}, u32[]{:S(2)}, u32[]{:S(2)}) collective-permute-start(f32[32,576]{1,0:T(8,128)S(1)} %fusion), channel_id=1, source_target_pairs={{0,30},{1,31},{2,32},{3,33},{4,34},{5,35},{6,36},{7,37},{8,38},{9,... | collective-permute-start | bytes 221192
  866.7 30.2 %copy-start.7 = (f32[32,576]{1,0:T(8,128)}, f32[32,576]{1,0:T(8,128)S(1)}, u32[]{:S(2)}) copy-start(f32[32,576]{1,0:T(8,128)S(1)} %collective-permute-done.25) | copy-start | bytes 221188
  866.7 15.3 %collective-permute-start.3 = (f32[32,576]{1,0:T(8,128)S(1)}, f32[32,576]{1,0:T(8,128)S(1)}, u32[]{:S(2)}, u32[]{:S(2)}) collective-permute-start(f32[32,576]{1,0:T(8,128)S(1)} %fusion), channel_id=1, source_target_pairs={{0,4},{1,5},{2,6},{3,7},{4,8},{5,9},{6,10},{7,11},{8,12},{9,13},{1... | collective-permute-start | bytes 221192
  869.2 21.5 %copy-start.8 = (f32[32,576]{1,0:T(8,128)}, f32[32,576]{1,0:T(8,128)S(1)}, u32[]{:S(2)}) copy-start(f32[32,576]{1,0:T(8,128)S(1)} %collective-permute-done.26) | copy-start | bytes 221188
  869.2 15.6 %collective-permute-start.30 = (f32[32,576]{1,0:T(8,128)S(1)}, f32[32,576]{1,0:T(8,128)S(1)}, u32[]{:S(2)}, u32[]{:S(2)}) collective-permute-start(f32[32,576]{1,0:T(8,128)S(1)} %fusion), channel_id=1, source_target_pairs={{0,31},{1,32},{2,33},{3,34},{4,35},{5,36},{6,37},{7,38},{8,39},{9,... | collective-permute-start | bytes 221192
  870.5 23.6 %copy-start.9 = (f32[32,576]{1,0:T(8,128)}, f32[32,576]{1,0:T(8,128)S(1)}, u32[]{:S(2)}) copy-start(f32[32,576]{1,0:T(8,128)S(1)} %collective-permute-done.27) | copy-start | bytes 221188
  870.5 20.2 %collective-permute-start.4 = (f32[32,576]{1,0:T(8,128)S(1)}, f32[32,576]{1,0:T(8,128)S(1)}, u32[]{:S(2)}, u32[]{:S(2)}) collective-permute-start(f32[32,576]{1,0:T(8,128)S(1)} %fusion), channel_id=1, source_target_pairs={{0,5},{1,6},{2,7},{3,8},{4,9},{5,10},{6,11},{7,12},{8,13},{9,14},{... | collective-permute-start | bytes 221192
  871.9 22.3 %copy-start.10 = (f32[32,576]{1,0:T(8,128)}, f32[32,576]{1,0:T(8,128)S(1)}, u32[]{:S(2)}) copy-start(f32[32,576]{1,0:T(8,128)S(1)} %collective-permute-done.28) | copy-start | bytes 221188
  871.9 30.6 %collective-permute-start.5 = (f32[32,576]{1,0:T(8,128)S(1)}, f32[32,576]{1,0:T(8,128)}, u32[]{:S(2)}, u32[]{:S(2)}) collective-permute-start(f32[32,576]{1,0:T(8,128)S(1)} %fusion), channel_id=1, source_target_pairs={{0,6},{1,7},{2,8},{3,9},{4,10},{5,11},{6,12},{7,13},{8,14},{9,15},... | collective-permute-start | bytes 221192
  878.9 15.2 %copy-start.11 = (f32[32,576]{1,0:T(8,128)}, f32[32,576]{1,0:T(8,128)S(1)}, u32[]{:S(2)}) copy-start(f32[32,576]{1,0:T(8,128)S(1)} %collective-permute-done.29) | copy-start | bytes 221188
  878.9 23.5 %collective-permute-start.6 = (f32[32,576]{1,0:T(8,128)S(1)}, f32[32,576]{1,0:T(8,128)}, u32[]{:S(2)}, u32[]{:S(2)}) collective-permute-start(f32[32,576]{1,0:T(8,128)S(1)} %fusion), channel_id=1, source_target_pairs={{0,7},{1,8},{2,9},{3,10},{4,11},{5,12},{6,13},{7,14},{8,15},{9,16}... | collective-permute-start | bytes 221192
  882.0 12.2 %copy-start.12 = (f32[32,576]{1,0:T(8,128)}, f32[32,576]{1,0:T(8,128)S(1)}, u32[]{:S(2)}) copy-start(f32[32,576]{1,0:T(8,128)S(1)} %collective-permute-done.3) | copy-start | bytes 221188
  882.0 20.5 %collective-permute-start.7 = (f32[32,576]{1,0:T(8,128)S(1)}, f32[32,576]{1,0:T(8,128)}, u32[]{:S(2)}, u32[]{:S(2)}) collective-permute-start(f32[32,576]{1,0:T(8,128)S(1)} %fusion), channel_id=1, source_target_pairs={{0,8},{1,9},{2,10},{3,11},{4,12},{5,13},{6,14},{7,15},{8,16},{9,17... | collective-permute-start | bytes 221192
  884.8 9.4 copy-start.13
  884.8 17.7 %collective-permute-start.8 = (f32[32,576]{1,0:T(8,128)S(1)}, f32[32,576]{1,0:T(8,128)}, u32[]{:S(2)}, u32[]{:S(2)}) collective-permute-start(f32[32,576]{1,0:T(8,128)S(1)} %fusion), channel_id=1, source_target_pairs={{0,9},{1,10},{2,11},{3,12},{4,13},{5,14},{6,15},{7,16},{8,17},{9,1... | collective-permute-start | bytes 221192
  890.7 3.5 copy-start.14
  890.7 11.8 %collective-permute-start.9 = (f32[32,576]{1,0:T(8,128)S(1)}, f32[32,576]{1,0:T(8,128)}, u32[]{:S(2)}, u32[]{:S(2)}) collective-permute-start(f32[32,576]{1,0:T(8,128)S(1)} %fusion), channel_id=1, source_target_pairs={{0,10},{1,11},{2,12},{3,13},{4,14},{5,15},{6,16},{7,17},{8,18},{9,... | collective-permute-start | bytes 221192
  902.4 47.8 %copy-start.2 = (f32[28,576]{1,0:T(8,128)S(1)}, f32[28,576]{1,0:T(8,128)}, u32[]{:S(2)}) copy-start(f32[28,576]{1,0:T(8,128)} %param.19) | copy-start | bytes 193540
  902.4 47.8 %copy-start.3 = (f32[28,576]{1,0:T(8,128)S(1)}, f32[28,576]{1,0:T(8,128)}, u32[]{:S(2)}) copy-start(f32[28,576]{1,0:T(8,128)} %param.21) | copy-start | bytes 193540
  902.4 47.8 %copy-start.4 = (f32[28,576]{1,0:T(8,128)S(1)}, f32[28,576]{1,0:T(8,128)}, u32[]{:S(2)}) copy-start(f32[28,576]{1,0:T(8,128)} %param.20) | copy-start | bytes 193540
Sparse Core Ops, SparseCore 0:
  24.5 89.8 reduce-scatter.5
where the time goes:
time: 975 us; the launch traced here: 968 us
  blocking collectives  751 us (77%)
  starting transfers between devices  110 us (11%)
  local copies, waits for them, and re-layouts  71.2 us (7%)
  between operations  15.4 us (2%)
  matrix products  14 us (1%)
    unnamed x1, blocking collectives  751 us
    unnamed x33, starting transfers between devices  110 us
    unnamed x38, local copies, waits for them, and re-layouts  71.2 us
  transfers between devices with their start and end apart: 33, of which 0 were waited for; matrix products, arithmetic and copies ran while one was open for 84% of the time, Pallas kernels for 0%

commit v1 on v0

v1 whole, which is shorter than its diff:
```python
import functools
import jax
import jax.numpy as jnp
import numpy as np
from jax import lax
from jax.experimental import pallas as pl
from jax.experimental.pallas import tpu as pltpu
from jax.sharding import Mesh, PartitionSpec as P

beta_first = 0.9
beta_second = 0.999
step_count = 1000.0
learn_rate = 0.05
weight_decay = 0.1
epsilon = 1e-08

SLOT = 128
HID = 1024
DW = 3584
HALF = 1792
D = 7168
KV = 576
PART = 896
ROWS = 28
PAD = 32
bf16, f32 = jnp.bfloat16, jnp.float32

PAIR_A = [(0, 1), (1, 0), (2, 3), (3, 2)]
PAIR_B = [(0, 3), (3, 0), (1, 2), (2, 1)]
VMEM = 48 * 1024 * 1024


def adam_step(master, moment, variance, gradient):
    moment_new = beta_first * moment + (1.0 - beta_first) * gradient
    variance_new = beta_second * variance + (1.0 - beta_second) * gradient * gradient
    first_fix = 1.0 - beta_first**step_count
    second_fix = 1.0 - beta_second**step_count
    update = moment_new / first_fix / (jnp.sqrt(variance_new / second_fix) + epsilon)
    return master - learn_rate * (update + weight_decay * master)


def dot0(left, right):
    return lax.dot_general(left, right, (((0,), (0,)), ((), ())), preferred_element_type=f32)


def pack_kernel(where, hid_ref, cot_ref, to_a_ref, to_b_ref, own_ref, masked):
    j, core, count = where[0], where[1], where[2]
    other = 1 - core
    near_a = j + 1 - 2 * lax.rem(j, 2)
    near_b = 3 - j
    across = lax.rem(j + 2, 4)
    live = lax.broadcasted_iota(jnp.int32, (SLOT, HID), 0) < count
    masked[...] = jnp.where(live, hid_ref[...], jnp.zeros_like(hid_ref))

    def block(chip, which):
        start = pl.multiple_of((chip * 2 + which) * 128, 128)
        return masked[:, pl.ds(start, 128)]

    to_a_ref[:, :HALF] = cot_ref[:, :HALF]
    to_b_ref[:, :HALF] = cot_ref[:, HALF:]
    for ref, near in ((to_a_ref, near_a), (to_b_ref, near_b)):
        for n, (chip, which) in enumerate(
            ((near, core), (across, core), (near, other), (across, other))
        ):
            ref[:, HALF + n * 128 : HALF + (n + 1) * 128] = block(chip, which)
    for n, chip in enumerate((j, near_b, j, near_a)):
        own_ref[:, n * 128 : (n + 1) * 128] = block(chip, core)


def sibling_kernel(where, hid_ref, cot_ref, out_ref, masked):
    j, core, count = where[0], where[1], where[2]
    other = 1 - core
    near_a = j + 1 - 2 * lax.rem(j, 2)
    near_b = 3 - j
    live = lax.broadcasted_iota(jnp.int32, (SLOT, HID), 0) < count
    masked[...] = jnp.where(live, hid_ref[...], jnp.zeros_like(hid_ref))
    out_ref[:, :DW] = cot_ref[...]
    for n, chip in enumerate((j, near_b, j, near_a)):
        start = pl.multiple_of((chip * 2 + other) * 128, 128)
        out_ref[:, DW + n * 128 : DW + (n + 1) * 128] = masked[:, pl.ds(start, 128)]


def dense_pack_kernel(where, lay_ref, cot_ref, out_ref):
    other = 1 - where[1]
    for n in range(4):
        start = pl.multiple_of((2 * n + other) * PART, 128)
        out_ref[:, n * PART : (n + 1) * PART] = lay_ref[:, pl.ds(start, PART)]
    out_ref[:, 4 * PART : 4 * PART + KV] = cot_ref[...]
    out_ref[:, 4 * PART + KV :] = jnp.zeros((SLOT, 64), bf16)


def whole(shape):
    return pl.BlockSpec(shape, lambda *_: (0,) * len(shape))


def packing(kernel, where, args, widths, scratch):
    outs = [jax.ShapeDtypeStruct((SLOT, w), bf16) for w in widths]
    return pl.pallas_call(
        kernel,
        out_shape=outs,
        grid_spec=pltpu.PrefetchScalarGridSpec(
            num_scalar_prefetch=1,
            grid=(1,),
            in_specs=[whole(a.shape) for a in args],
            out_specs=[whole(o.shape) for o in outs],
            scratch_shapes=scratch,
        ),
        compiler_params=pltpu.CompilerParams(vmem_limit_bytes=VMEM),
    )(where, *args)


def products_kernel(
    own_ca, own_cb, own_ha, own_hb, sib_ca, sib_cb, sib_ha, sib_hb,
    far_ca, far_ha, far_cb, far_hb, sf_ca, sf_ha, sf_cb, sf_hb,
    send_a, send_b, keep,
):
    for n, (h, c, send) in enumerate((
        ((own_ha, sib_ha, far_ha, sf_ha), (own_ca, sib_ca, far_ca, sf_ca), send_a),
        ((own_hb, sib_hb, far_hb, sf_hb), (own_cb, sib_cb, far_cb, sf_cb), send_b),
    )):
        left = jnp.concatenate([r[...] for r in h], axis=0)
        right = jnp.concatenate([r[...] for r in c], axis=0)
        result = dot0(left, right)
        keep[n] = result[:SLOT]
        send[...] = result[SLOT:].astype(bf16)


def expert_products(cot, own, sib, far_a, far_b, sib_far):
    def at(fixed):
        return pl.BlockSpec((SLOT, 256), lambda i: (0, fixed))

    def tile(first):
        return pl.BlockSpec((SLOT, 256), lambda i: (0, first + i))

    return pl.pallas_call(
        products_kernel,
        grid=(7,),
        out_shape=[
            jax.ShapeDtypeStruct((SLOT, HALF), bf16),
            jax.ShapeDtypeStruct((SLOT, HALF), bf16),
            jax.ShapeDtypeStruct((2, SLOT, HALF), f32),
        ],
        in_specs=[
            tile(0), tile(7), at(0), at(1),
            tile(0), tile(7), at(14), at(15),
            tile(0), at(7), tile(0), at(7),
            tile(0), at(7), tile(8), at(15),
        ],
        out_specs=[tile(0), tile(0), pl.BlockSpec((2, SLOT, 256), lambda i: (0, 0, i))],
        compiler_params=pltpu.CompilerParams(vmem_limit_bytes=VMEM),
    )(cot, cot, own, own, sib, sib, sib, sib, far_a, far_a, far_b, far_b,
      sib_far, sib_far, sib_far, sib_far)


def expert_adam_kernel(keep, got_a, got_b, master, moment, variance, out):
    half = pl.program_id(0)

    def go(got):
        gradient = keep[0] + got[...].astype(f32)
        out[...] = adam_step(master[...], moment[...], variance[...], gradient)

    @pl.when(half == 0)
    def _():
        go(got_a)

    @pl.when(half == 1)
    def _():
        go(got_b)


def expert_adam(keep, got_a, got_b, master, moment, variance):
    wide = pl.BlockSpec((SLOT, 256), lambda h, i: (0, h * 7 + i))
    return pl.pallas_call(
        expert_adam_kernel,
        grid=(2, 7),
        out_shape=jax.ShapeDtypeStruct((SLOT, DW), f32),
        in_specs=[
            pl.BlockSpec((1, SLOT, 256), lambda h, i: (h, 0, i)),
            pl.BlockSpec((SLOT, 256), lambda h, i: (0, jnp.where(h == 0, i, 6))),
            pl.BlockSpec((SLOT, 256), lambda h, i: (0, jnp.where(h == 0, 0, i))),
            wide, wide, wide,
        ],
        out_specs=wide,
        compiler_params=pltpu.CompilerParams(vmem_limit_bytes=VMEM),
    )(keep, got_a, got_b, master, moment, variance)


def row_sources():
    table = np.full((2, 1024), -1, np.int32)
    for first in range(4):
        for second in range(4):
            for low in range(2):
                for row in range(ROWS):
                    place = ((first * 4 + second) * 2 + low) * PAD + row
                    table[0, place] = low * 448 + first * 112 + second * 28 + row
                    table[1, place] = low * 448 + second * 112 + first * 28 + row
    return table[:, :, None]


def dense_kernel(where, lay_ref, cot_ref, got_ref, src_ref, out_ref, order):
    n = pl.program_id(0)

    @pl.when(n == 0)
    def _():
        columns = lax.broadcasted_iota(jnp.int32, (1024, PART), 1)
        order[...] = jnp.where(columns == src_ref[0], 1.0, 0.0).astype(bf16)

    start = pl.multiple_of(n * PART, 128)
    tokens = jnp.concatenate([lay_ref[...], got_ref[:, pl.ds(start, PART)]], axis=0)
    grads = jnp.concatenate([cot_ref[...], got_ref[:, 4 * PART : 4 * PART + KV]], axis=0)
    moved = lax.dot_general(
        order[...], tokens, (((1,), (1,)), ((), ())), preferred_element_type=f32
    ).astype(bf16)
    out_ref[0] = jnp.dot(moved, grads, preferred_element_type=f32).astype(bf16)


def dense_product(where, lay, cot, got):
    sources = jnp.asarray(row_sources())
    return pl.pallas_call(
        dense_kernel,
        out_shape=jax.ShapeDtypeStruct((4, 1024, KV), bf16),
        grid_spec=pltpu.PrefetchScalarGridSpec(
            num_scalar_prefetch=1,
            grid=(4,),
            in_specs=[
                pl.BlockSpec((SLOT, PART), lambda n, w: (0, 2 * n + w[1])),
                whole(cot.shape),
                whole(got.shape),
                pl.BlockSpec((1, 1024, 1), lambda n, w: (w[1], 0, 0)),
            ],
            out_specs=pl.BlockSpec((1, 1024, KV), lambda n, w: (n, 0, 0)),
            scratch_shapes=[pltpu.VMEM((1024, PART), bf16)],
        ),
        compiler_params=pltpu.CompilerParams(vmem_limit_bytes=VMEM),
    )(where, lay, cot, got, sources)


def plane_pairs(stage, step):
    pairs = []
    for core in range(2):
        for x in range(4):
            for y in range(4):
                along_x = (core + stage) % 2 == 0
                to = ((x + step) % 4, y) if along_x else (x, (y + step) % 4)
                pairs.append((core * 16 + x * 4 + y, core * 16 + to[0] * 4 + to[1]))
    return pairs


def ring_scatter(blocks, me, stage):
    axes = ("co", "x", "y")

    def take(place, first, last):
        return lax.dynamic_index_in_dim(blocks[first:last], place, axis=1, keepdims=False)

    up, down, across = (me + 1) % 4, (me + 3) % 4, (me + 2) % 4
    rise, fall = plane_pairs(stage, 1), plane_pairs(stage, -1)
    got_up = lax.ppermute(take(across, 0, 2).astype(bf16), axes, rise)
    got_down = lax.ppermute(take(across, 2, 4).astype(bf16), axes, fall)
    to_up = jnp.concatenate(
        [
            (take(up, 0, 2).astype(f32) + got_up.astype(f32)).astype(bf16),
            take(up, 2, 4).astype(bf16),
        ]
    )
    to_down = jnp.concatenate(
        [
            take(down, 0, 2).astype(bf16),
            (take(down, 2, 4).astype(f32) + got_down.astype(f32)).astype(bf16),
        ]
    )
    from_low = lax.ppermute(to_up, axes, rise)
    from_high = lax.ppermute(to_down, axes, fall)
    return take(me, 0, 4).astype(f32) + from_low.astype(f32) + from_high.astype(f32)


def on_device(
    expert_inputs,
    expert_cotangent,
    row_counts,
    expert_master,
    expert_moment,
    expert_variance,
    layer_inputs,
    layer_cotangent,
    dense_master,
    dense_moment,
    dense_variance,
):
    j, core = lax.axis_index("zh"), lax.axis_index("co")
    low, x, y = lax.axis_index("zl"), lax.axis_index("x"), lax.axis_index("y")
    where = jnp.stack([j, core, row_counts[0, 0]]).astype(jnp.int32)
    hid, cot = expert_inputs[0], expert_cotangent[0]
    swap = [(0, 1), (1, 0)]

    to_a, to_b, own = packing(
        pack_kernel, where, (hid, cot), (2304, 2304, 512), [pltpu.VMEM((SLOT, HID), bf16)]
    )
    far_a = lax.ppermute(to_a, "zh", PAIR_A)
    far_b = lax.ppermute(to_b, "zh", PAIR_B)

    (to_core,) = packing(dense_pack_kernel, where, (layer_inputs, layer_cotangent), (4224,), [])
    dense_got = lax.ppermute(to_core, "co", swap)
    (to_sib,) = packing(
        sibling_kernel, where, (hid, cot), (4096,), [pltpu.VMEM((SLOT, HID), bf16)]
    )
    sib = lax.ppermute(to_sib, "co", swap)
    product = dense_product(where, layer_inputs, layer_cotangent, dense_got)

    first = jnp.where(core == 0, x, y)
    second = jnp.where(core == 0, y, x)
    plane = ring_scatter(product.reshape(4, 4, 256, KV), first, 0)
    line = ring_scatter(plane.reshape(4, 4, 64, KV), second, 1)

    sib_far = lax.ppermute(
        jnp.concatenate(
            [far_a[:, :HALF], far_a[:, 2048:], far_b[:, :HALF], far_b[:, 2048:]], axis=1
        ),
        "co",
        swap,
    )
    send_a, send_b, keep = expert_products(cot, own, sib, far_a, far_b, sib_far)
    got_a = lax.ppermute(send_a, "zh", PAIR_B)
    got_b = lax.ppermute(send_b, "zh", PAIR_A)

    line = line.reshape(4, 2, PAD, KV)
    mine = lax.dynamic_index_in_dim(line, low, axis=1, keepdims=False)
    theirs = lax.dynamic_index_in_dim(line, 1 - low, axis=1, keepdims=False)
    mine = mine + lax.ppermute(theirs.astype(bf16), "zl", swap).astype(f32)
    dense_grad = lax.dynamic_index_in_dim(mine, j, keepdims=False)
    for step in (1, 2, 3):
        out = lax.dynamic_index_in_dim(mine, (j + step) % 4, keepdims=False).astype(bf16)
        got = lax.ppermute(out, "zh", [(i, (i + step) % 4) for i in range(4)])
        dense_grad = dense_grad + got.astype(f32)
    dense_updated = adam_step(dense_master, dense_moment, dense_variance, dense_grad[:ROWS])

    expert_updated = expert_adam(
        keep, got_a, got_b, expert_master[0], expert_moment[0], expert_variance[0]
    )
    return (expert_updated[None], dense_updated)


def solution(mesh):
    fine = Mesh(mesh.devices.reshape(4, 2, 2, 4, 4), ("zh", "co", "zl", "x", "y"))
    ep, rep = ("zl", "x", "y"), ("zh", "co")
    expert = P(ep, rep, None)
    dense = P(rep + ep, None)
    in_specs = (expert, expert, P(ep, rep)) + (expert,) * 3 + (dense,) * 5
    return jax.shard_map(
        on_device, mesh=fine, in_specs=in_specs, out_specs=(expert, dense), check_vma=False
    )
```

time: 975 us -> 160 us (0.16)
  blocking collectives: 751 us -> 0 us
  starting transfers between devices: 110 us -> 33.3 us
  waiting for transfers between devices: 0.1 us -> 52.6 us
  local copies, waits for them, and re-layouts: 71.2 us -> 27.4 us
  Pallas kernels: 0 us -> 30.7 us
  matrix products: 14 us -> 0 us
  between operations: 15.4 us -> 1.49 us
    unnamed x1 -> x0, blocking collectives: 751 us -> none
    unnamed x33 -> x0, starting transfers between devices: 110 us -> none
    unnamed x38 -> x39, local copies, waits for them, and re-layouts: 71.2 us -> 9 us
    ppermute x0 -> x19, waiting for transfers between devices: none -> 52.6 us  [the longest x1 17.7 us: on_device(): far_a = lax.ppermute(to_a, 'zh', PAIR_A)]
    ppermute x0 -> x19, starting transfers between devices: none -> 33.3 us  [the longest x3 7.36 us: on_device(): got = lax.ppermute(out, 'zh', [(i, (i + step) % 4) for i in range(4)])]
    pallas_call x0 -> x6, Pallas kernels: none -> 30.7 us  [the longest x1 9.95 us: dense_product(): pl.pallas_call(dense_kernel, out_shape=jax.ShapeDtypeStruct((4, 1024, KV)...]
    dot_general x2 -> x0, matrix products: 14 us -> none  [transpose_product(): lax.dot_general(left, right, (((0,), (0,)), ((), ())), preferred_element_...]
  transfers between devices with their start and end apart: 33 -> 19, of which waited for: 0 -> 9; matrix products, arithmetic and copies ran while one was open for 84% -> 15% of each run, Pallas kernels for 0% -> 12%
where the time goes in v1:
time: 160 us; the launch traced here: 158 us
  waiting for transfers between devices  52.6 us (33%)
  starting transfers between devices  33.3 us (21%)
  Pallas kernels  30.7 us (19%)
  local copies, waits for them, and re-layouts  27.4 us (17%)
  other arithmetic  12.3 us (8%)
    ppermute x1, waiting for transfers between devices, on_device(): far_a = lax.ppermute(to_a, 'zh', PAIR_A)  17.7 us
    ppermute x1, waiting for transfers between devices, on_device(): got_a = lax.ppermute(send_a, 'zh', PAIR_B)  16.7 us
    pallas_call x1, Pallas kernels, dense_product(): pl.pallas_call(dense_kernel, out_shape=jax.ShapeDtypeStruct((4, 1024, KV)...  9.95 us
    pallas_call x1, Pallas kernels, expert_adam(): pl.pallas_call(expert_adam_kernel, grid=(2, 7), out_shape=jax.ShapeDtypeS...  9.66 us
    unnamed x39, local copies, waits for them, and re-layouts  9 us
    ppermute x3, starting transfers between devices, on_device(): got = lax.ppermute(out, 'zh', [(i, (i + step) % 4) for i in range(4)])  7.36 us
    dynamic_slice x5, local copies, waits for them, and re-layouts, take(): lax.dynamic_index_in_dim(blocks[first:last], place, axis=1, keepdims=False)  7.12 us
    pallas_call x1, Pallas kernels, expert_products(): pl.pallas_call(products_kernel, grid=(7,), out_shape=[jax.ShapeDtypeStruc...  6.14 us
  transfers between devices with their start and end apart: 19, of which 9 were waited for; matrix products, arithmetic and copies ran while one was open for 15% of the time, Pallas kernels for 12%

profile of v1, /device:TPU:8, one launch (start us, length us, event | category | flops | bytes accessed | tf_op | source)
XLA Modules:
  0.0 157.8 jit_solution(17650967692139771298)
XLA Ops:
  1.3 1.1 copy.36.cot_ref
  2.4 1.5 copy-done.1
  3.9 1.6 %shard_map.135 = bf16[128,4224]{1,0:T(8,128)(2,1)} custom-call(s32[3]{0:T(128)S(1)} %pad_add_fusion.where, bf16[128,7168]{1,0:T(8,128)(2,1)S(1)} %copy-done.1, bf16[128,576]{1,0:T(8,128)(2,1)S(1)} %copy.36.cot_ref), custom_call_target="tpu_custom_call" | custom-call | tf_op jit(solution)/shard_map/pallas_call | solution.py:98
  5.5 2.9 %collective-permute-done.6.got_ref = bf16[128,4224]{1,0:T(8,128)(2,1)S(1)} collective-permute-done((bf16[128,4224]{1,0:T(8,128)(2,1)}, bf16[128,4224]{1,0:T(8,128)(2,1)S(1)}, u32[]{:S(2)}, u32[]{:S(2)}) %collective-permute-start.6) | collective-permute-done | bytes 1081376 | tf_op jit(solution)/shard_map/ppermute | solution.py:302
  8.5 1.2 copy-done.7
  9.7 9.9 %shard_map.136 = bf16[4,1024,576]{2,1,0:T(8,128)(2,1)} custom-call(s32[3]{0:T(128)S(1)} %pad_add_fusion.where, bf16[128,7168]{1,0:T(8,128)(2,1)S(1)} %copy-done.2, bf16[128,576]{1,0:T(8,128)(2,1)S(1)} %copy.36.cot_ref, bf16[128,4224]{1,0:T(8,128)(2,1)S(1)} %collective-permute-done.6.got_ref, s32[2,1024,1]{2,1,0:T(8,128)S(1)} %copy-done.7), custom_call_target="tpu_custom_call" | custom-call | tf_op jit(solution)/shard_map/pallas_call | solution.py:219
  19.6 3.0 %fusion.22 = (bf16[2,1024,576]{2,1,0:T(8,128)(2,1)S(1)}, bf16[2,1024,576]{2,1,0:T(8,128)(2,1)S(1)}) fusion(bf16[4,1024,576]{2,1,0:T(8,128)(2,1)} %shard_map.136), kind=kLoop, calls=%fused_computation.53 | loop fusion | bytes 9437184 | tf_op jit(solution)/shard_map/slice | solution.py:253
  22.6 1.5 constant_dynamic-slice_fusion.3
  24.1 2.2 %copy.39 = bf16[2,1,256,576]{2,3,0,1:T(8,128)(2,1)} copy(bf16[2,1,256,576]{3,2,1,0:T(8,128)(2,1)} %get-tuple-element.31) | data formatting | bytes 1179648 | tf_op jit(solution)/shard_map/jit(dynamic_index_in_dim)/dynamic_slice | solution.py:253
  26.3 1.5 collective-permute-start.7
  27.7 2.2 %copy.44 = bf16[2,1,256,576]{2,3,0,1:T(8,128)(2,1)} copy(bf16[2,1,256,576]{3,2,1,0:T(8,128)(2,1)} %get-tuple-element.22) | data formatting | bytes 1179648 | tf_op jit(solution)/shard_map/jit(dynamic_index_in_dim)/dynamic_slice | solution.py:253
  29.9 1.7 %collective-permute-start.9 = (bf16[2,256,576]{1,2,0:T(8,128)(2,1)}, bf16[2,256,576]{1,2,0:T(8,128)(2,1)}, u32[]{:S(2)}, u32[]{:S(2)}) collective-permute-start(bf16[2,256,576]{1,2,0:T(8,128)(2,1)} %bitcast.100), channel_id=1, source_target_pairs={{0,12},{1,13},{2,14},{3,15},{4,0},{5,1},{6,2},{7,3},{8,4},{9,5},{1... | collective-permute-start | bytes 1769480 | tf_op jit(solution)/shard_map/ppermute | solution.py:258
  31.7 1.1 copy.51
  32.7 1.1 copy.40
  34.3 3.4 %collective-permute-done.7 = bf16[2,256,576]{1,2,0:T(8,128)(2,1)} collective-permute-done((bf16[2,256,576]{1,2,0:T(8,128)(2,1)}, bf16[2,256,576]{1,2,0:T(8,128)(2,1)}, u32[]{:S(2)}, u32[]{:S(2)}) %collective-permute-start.7) | collective-permute-done | bytes 589856 | tf_op jit(solution)/shard_map/ppermute | solution.py:257
  37.7 1.2 fusion.2
  38.9 1.1 pad_maximum_fusion
  40.3 1.2 fusion.1
  41.5 1.1 pad_maximum_fusion.1
  42.7 3.0 %collective-permute-start.10 = (bf16[4,256,576]{1,2,0:T(8,128)(2,1)}, bf16[4,256,576]{1,2,0:T(8,128)(2,1)}, u32[]{:S(2)}, u32[]{:S(2)}) collective-permute-start(bf16[4,256,576]{1,2,0:T(8,128)(2,1)} %pad_maximum_fusion.1), channel_id=1, source_target_pairs={{0,12},{1,13},{2,14},{3,15},{4,0},{5,1},{6,2},{7,3},{8,4},{9,5},{1... | collective-permute-start | bytes 3538952 | tf_op jit(solution)/shard_map/ppermute | solution.py:272
  45.6 1.7 %shard_map.131 = (bf16[128,2304]{1,0:T(8,128)(2,1)}, bf16[128,2304]{1,0:T(8,128)(2,1)}, bf16[128,512]{1,0:T(8,128)(2,1)S(1)}) custom-call(s32[3]{0:T(128)S(1)} %pad_add_fusion.where, bf16[128,1024]{1,0:T(8,128)(2,1)S(1)} %bitcast.83, bf16[128,3584]{1,0:T(8,128)(2,1)S(1)} %bitcast.78), custom_call_target="tpu_custom_call" | custom-call | tf_op jit(solution)/shard_map/pallas_call | solution.py:98
  47.3 3.3 %collective-permute-start.1 = (bf16[128,2304]{1,0:T(8,128)(2,1)}, bf16[128,2304]{1,0:T(8,128)(2,1)S(1)}, u32[]{:S(2)}, u32[]{:S(2)}) collective-permute-start(bf16[128,2304]{1,0:T(8,128)(2,1)} %get-tuple-element.9), channel_id=1, source_target_pairs={{0,64},{64,0},{128,192},{192,128},{1,65},{65,1},{129,193},{193,129... | collective-permute-start | bytes 1769480 | tf_op jit(solution)/shard_map/ppermute | solution.py:298
  50.6 4.5 %collective-permute-start.2 = (bf16[128,2304]{1,0:T(8,128)(2,1)}, bf16[128,2304]{1,0:T(8,128)(2,1)}, u32[]{:S(2)}, u32[]{:S(2)}) collective-permute-start(bf16[128,2304]{1,0:T(8,128)(2,1)} %get-tuple-element.10), channel_id=1, source_target_pairs={{0,192},{192,0},{64,128},{128,64},{1,193},{193,1},{65,129},{129,65... | collective-permute-start | bytes 1769480 | tf_op jit(solution)/shard_map/ppermute | solution.py:299
  55.1 1.6 %shard_map.132 = bf16[128,4096]{1,0:T(8,128)(2,1)} custom-call(s32[3]{0:T(128)S(1)} %pad_add_fusion.where, bf16[128,1024]{1,0:T(8,128)(2,1)S(1)} %bitcast.84, bf16[128,3584]{1,0:T(8,128)(2,1)S(1)} %bitcast.79), custom_call_target="tpu_custom_call" | custom-call | tf_op jit(solution)/shard_map/pallas_call | solution.py:98
  56.7 17.7 %collective-permute-done.1.far_ca.far_ha = bf16[128,2304]{1,0:T(8,128)(2,1)S(1)} collective-permute-done((bf16[128,2304]{1,0:T(8,128)(2,1)}, bf16[128,2304]{1,0:T(8,128)(2,1)S(1)}, u32[]{:S(2)}, u32[]{:S(2)}) %collective-permute-start.1) | collective-permute-done | bytes 589856 | tf_op jit(solution)/shard_map/ppermute | solution.py:298
  74.3 2.8 %collective-permute-done.2.far_cb.far_hb = bf16[128,2304]{1,0:T(8,128)(2,1)} collective-permute-done((bf16[128,2304]{1,0:T(8,128)(2,1)}, bf16[128,2304]{1,0:T(8,128)(2,1)}, u32[]{:S(2)}, u32[]{:S(2)}) %collective-permute-start.2) | collective-permute-done | bytes 589856 | tf_op jit(solution)/shard_map/ppermute | solution.py:299
  78.2 1.5 slice.63
  79.7 2.4 %copy.41 = bf16[4,256,576]{2,1,0:T(8,128)(2,1)} copy(bf16[4,256,576]{1,2,0:T(8,128)(2,1)} %collective-permute-done.8) | data formatting | bytes 2359296 | tf_op jit(solution)/shard_map/ppermute | solution.py:271
  82.1 2.4 %copy.45 = bf16[4,256,576]{2,1,0:T(8,128)(2,1)} copy(bf16[4,256,576]{1,2,0:T(8,128)(2,1)} %collective-permute-done.10) | data formatting | bytes 2359296 | tf_op jit(solution)/shard_map/ppermute | solution.py:272
  84.5 2.5 %fusion = f32[4,256,576]{2,1,0:T(8,128)S(1)} fusion(bf16[4,256,576]{2,1,0:T(8,128)(2,1)} %copy.45, bf16[4,256,576]{2,1,0:T(8,128)(2,1)} %copy.41, bf16[4,4,256,576]{3,2,1,0:T(8,128)(2,1)} %bitcast.85, s32[]{:T(128)S(6)} %select_n.100), kind=kLoop, calls=%fused_computation.1 | loop fusion | flops 2949120 | bytes 5898244 | tf_op jit(solution)/shard_map/add | solution.py:273
  87.3 1.3 copy-done.11
  88.6 1.5 collective-permute-start.11
  90.1 1.1 pad_maximum_fusion.2
  92.1 2.1 %collective-permute-done.11 = bf16[2,64,576]{2,1,0:T(8,128)(2,1)S(1)} collective-permute-done((bf16[2,64,576]{2,1,0:T(8,128)(2,1)S(1)}, bf16[2,64,576]{2,1,0:T(8,128)(2,1)S(1)}, u32[]{:S(2)}, u32[]{:S(2)}) %collective-permute-start.11) | collective-permute-done | bytes 147488 | tf_op jit(solution)/shard_map/ppermute | solution.py:257
  94.3 1.4 collective-permute-start.12
  98.3 1.1 copy-done.4
  99.3 6.1 %shard_map.133 = (bf16[128,1792]{1,0:T(8,128)(2,1)}, bf16[128,1792]{1,0:T(8,128)(2,1)}, f32[2,128,1792]{2,1,0:T(8,128)}) custom-call(bf16[128,3584]{1,0:T(8,128)(2,1)S(1)} %bitcast.80, bf16[128,3584]{1,0:T(8,128)(2,1)S(1)} %bitcast.81, bf16[128,512]{1,0:T(8,128)(2,1)S(1)} %copy-done.10, bf16[128,512]{1,0:T(8,128)(2,1)S(1)} %copy-done.10, ...), custom_call_target="tpu_custom_call" | custom-call | tf_op jit(solution)/shard_map/pallas_call | solution.py:135
  105.4 5.8 %collective-permute-start.4 = (bf16[128,1792]{1,0:T(8,128)(2,1)}, bf16[128,1792]{1,0:T(8,128)(2,1)S(1)}, u32[]{:S(2)}, u32[]{:S(2)}) collective-permute-start(bf16[128,1792]{1,0:T(8,128)(2,1)} %get-tuple-element.12), channel_id=1, source_target_pairs={{0,192},{192,0},{64,128},{128,64},{1,193},{193,1},{65,129},{129,65... | collective-permute-start | bytes 1376264 | tf_op jit(solution)/shard_map/ppermute | solution.py:322
  111.3 1.4 collective-permute-start.5
  112.7 1.4 fusion.3
  114.8 16.7 %collective-permute-done.4.got_a = bf16[128,1792]{1,0:T(8,128)(2,1)S(1)} collective-permute-done((bf16[128,1792]{1,0:T(8,128)(2,1)}, bf16[128,1792]{1,0:T(8,128)(2,1)S(1)}, u32[]{:S(2)}, u32[]{:S(2)}) %collective-permute-start.4) | collective-permute-done | bytes 458784 | tf_op jit(solution)/shard_map/ppermute | solution.py:322
  131.5 2.2 %collective-permute-done.5.got_b = bf16[128,1792]{1,0:T(8,128)(2,1)S(1)} collective-permute-done((bf16[128,1792]{1,0:T(8,128)(2,1)}, bf16[128,1792]{1,0:T(8,128)(2,1)S(1)}, u32[]{:S(2)}, u32[]{:S(2)}) %collective-permute-start.5) | collective-permute-done | bytes 458784 | tf_op jit(solution)/shard_map/ppermute | solution.py:323
  133.7 1.5 copy-done.6
  135.2 9.7 %shard_map.134 = f32[128,3584]{1,0:T(8,128)} custom-call(f32[2,128,1792]{2,1,0:T(8,128)S(1)} %copy-done.6, bf16[128,1792]{1,0:T(8,128)(2,1)S(1)} %collective-permute-done.4.got_a, bf16[128,1792]{1,0:T(8,128)(2,1)S(1)} %collective-permute-done.5.got_b, f32[128,3584]{1,0:T(8,128)S(1)} %bitcast.82, f32[128,3584]{1,0:T(8,128)} %bitcast.97, f32[128,3584]{1,0:T(8,128)} %bitcast.98), custom_call_target="tpu_custom_call" | custom-call | tf_op jit(solution)/shard_map/pallas_call | solution.py:173
  145.9 3.3 %collective-permute-start.16 = (bf16[32,576]{1,0:T(8,128)(2,1)S(1)}, bf16[32,576]{1,0:T(8,128)(2,1)S(1)}, u32[]{:S(2)}, u32[]{:S(2)}) collective-permute-start(bf16[32,576]{1,0:T(8,128)(2,1)S(1)} %get-tuple-element.28), channel_id=1, source_target_pairs={{0,64},{64,128},{128,192},{192,0},{1,65},{65,129},{129,193},{193,1... | collective-permute-start | bytes 110600 | tf_op jit(solution)/shard_map/ppermute | solution.py:332
  149.2 1.5 collective-permute-start.17
  150.6 2.6 %collective-permute-start.18 = (bf16[32,576]{1,0:T(8,128)(2,1)S(1)}, bf16[32,576]{1,0:T(8,128)(2,1)S(1)}, u32[]{:S(2)}, u32[]{:S(2)}) collective-permute-start(bf16[32,576]{1,0:T(8,128)(2,1)S(1)} %get-tuple-element.29), channel_id=1, source_target_pairs={{0,192},{64,0},{128,64},{192,128},{1,193},{65,1},{129,65},{193,129... | collective-permute-start | bytes 110600 | tf_op jit(solution)/shard_map/ppermute | solution.py:332
  153.3 3.8 %collective-permute-done.17 = bf16[32,576]{1,0:T(8,128)(2,1)S(1)} collective-permute-done((bf16[32,576]{1,0:T(8,128)(2,1)S(1)}, bf16[32,576]{1,0:T(8,128)(2,1)S(1)}, u32[]{:S(2)}, u32[]{:S(2)}) %collective-permute-start.17) | collective-permute-done | bytes 36896 | tf_op jit(solution)/shard_map/ppermute | solution.py:332
  (69 shorter events, 8.2 us)
Async XLA Ops:
  2.4 1.5 copy-start.1
  3.9 4.5 %copy-start.2 = (bf16[128,7168]{1,0:T(8,128)(2,1)S(1)}, bf16[128,7168]{1,0:T(8,128)(2,1)}, u32[]{:S(2)}) copy-start(bf16[128,7168]{1,0:T(8,128)(2,1)} %lay_ref.3) | copy-start | bytes 5505028
  5.5 2.9 %collective-permute-start.6 = (bf16[128,4224]{1,0:T(8,128)(2,1)}, bf16[128,4224]{1,0:T(8,128)(2,1)S(1)}, u32[]{:S(2)}, u32[]{:S(2)}) collective-permute-start(bf16[128,4224]{1,0:T(8,128)(2,1)} %shard_map.135), channel_id=1, source_target_pairs={{0,32},{32,0},{1,33},{33,1},{2,34},{34,2},{3,35},{35,3},{4,36},{36... | collective-permute-start | bytes 3244040 | tf_op jit(solution)/shard_map/ppermute | solution.py:302
  8.5 1.2 copy-start.7
  26.3 11.4 %collective-permute-start.7 = (bf16[2,256,576]{1,2,0:T(8,128)(2,1)}, bf16[2,256,576]{1,2,0:T(8,128)(2,1)}, u32[]{:S(2)}, u32[]{:S(2)}) collective-permute-start(bf16[2,256,576]{1,2,0:T(8,128)(2,1)} %bitcast.101), channel_id=1, source_target_pairs={{0,4},{1,5},{2,6},{3,7},{4,8},{5,9},{6,10},{7,11},{8,12},{9,13},{1... | collective-permute-start | bytes 1769480 | tf_op jit(solution)/shard_map/ppermute | solution.py:257
  29.9 10.4 %collective-permute-start.9 = (bf16[2,256,576]{1,2,0:T(8,128)(2,1)}, bf16[2,256,576]{1,2,0:T(8,128)(2,1)}, u32[]{:S(2)}, u32[]{:S(2)}) collective-permute-start(bf16[2,256,576]{1,2,0:T(8,128)(2,1)} %bitcast.100), channel_id=1, source_target_pairs={{0,12},{1,13},{2,14},{3,15},{4,0},{5,1},{6,2},{7,3},{8,4},{9,5},{1... | collective-permute-start | bytes 1769480 | tf_op jit(solution)/shard_map/ppermute | solution.py:258
  33.8 3.9 %copy-start.12 = (bf16[2,1,256,576]{2,3,0,1:T(8,128)(2,1)S(1)}, bf16[2,1,256,576]{2,3,0,1:T(8,128)(2,1)}, u32[]{:S(2)}) copy-start(bf16[2,1,256,576]{2,3,0,1:T(8,128)(2,1)} %copy.51) | copy-start | bytes 1769476
  34.3 4.6 %copy-start.13 = (bf16[2,1,256,576]{2,3,0,1:T(8,128)(2,1)S(1)}, bf16[2,1,256,576]{2,3,0,1:T(8,128)(2,1)}, u32[]{:S(2)}) copy-start(bf16[2,1,256,576]{2,3,0,1:T(8,128)(2,1)} %copy.40) | copy-start | bytes 1769476
  40.0 39.7 %collective-permute-start.8 = (bf16[4,256,576]{1,2,0:T(8,128)(2,1)}, bf16[4,256,576]{1,2,0:T(8,128)(2,1)}, u32[]{:S(2)}, u32[]{:S(2)}) collective-permute-start(bf16[4,256,576]{1,2,0:T(8,128)(2,1)} %pad_maximum_fusion), channel_id=1, source_target_pairs={{0,4},{1,5},{2,6},{3,7},{4,8},{5,9},{6,10},{7,11},{8,12},{9,13},{1... | collective-permute-start | bytes 3538952 | tf_op jit(solution)/shard_map/ppermute | solution.py:271
  41.5 4.1 %copy-start = (bf16[1,128,3584]{2,1,0:T(8,128)(2,1)S(1)}, bf16[1,128,3584]{2,1,0:T(8,128)(2,1)}, u32[]{:S(2)}) copy-start(bf16[1,128,3584]{2,1,0:T(8,128)(2,1)} %param.13) | copy-start | bytes 2752516
  41.5 4.1 %copy-start.8 = (bf16[1,128,1024]{2,1,0:T(8,128)(2,1)S(1)}, bf16[1,128,1024]{2,1,0:T(8,128)(2,1)}, u32[]{:S(2)}) copy-start(bf16[1,128,1024]{2,1,0:T(8,128)(2,1)} %param.12) | copy-start | bytes 786436
  42.7 39.5 %collective-permute-start.10 = (bf16[4,256,576]{1,2,0:T(8,128)(2,1)}, bf16[4,256,576]{1,2,0:T(8,128)(2,1)}, u32[]{:S(2)}, u32[]{:S(2)}) collective-permute-start(bf16[4,256,576]{1,2,0:T(8,128)(2,1)} %pad_maximum_fusion.1), channel_id=1, source_target_pairs={{0,12},{1,13},{2,14},{3,15},{4,0},{5,1},{6,2},{7,3},{8,4},{9,5},{1... | collective-permute-start | bytes 3538952 | tf_op jit(solution)/shard_map/ppermute | solution.py:272
  47.3 27.0 %copy-start.9 = (bf16[128,512]{1,0:T(8,128)(2,1)}, bf16[128,512]{1,0:T(8,128)(2,1)S(1)}, u32[]{:S(2)}) copy-start(bf16[128,512]{1,0:T(8,128)(2,1)S(1)} %get-tuple-element.8.own_ha.own_hb) | copy-start | bytes 393220
  47.3 27.0 %collective-permute-start.1 = (bf16[128,2304]{1,0:T(8,128)(2,1)}, bf16[128,2304]{1,0:T(8,128)(2,1)S(1)}, u32[]{:S(2)}, u32[]{:S(2)}) collective-permute-start(bf16[128,2304]{1,0:T(8,128)(2,1)} %get-tuple-element.9), channel_id=1, source_target_pairs={{0,64},{64,0},{128,192},{192,128},{1,65},{65,1},{129,193},{193,129... | collective-permute-start | bytes 1769480 | tf_op jit(solution)/shard_map/ppermute | solution.py:298
  50.6 26.6 %collective-permute-start.2 = (bf16[128,2304]{1,0:T(8,128)(2,1)}, bf16[128,2304]{1,0:T(8,128)(2,1)}, u32[]{:S(2)}, u32[]{:S(2)}) collective-permute-start(bf16[128,2304]{1,0:T(8,128)(2,1)} %get-tuple-element.10), channel_id=1, source_target_pairs={{0,192},{192,0},{64,128},{128,64},{1,193},{193,1},{65,129},{129,65... | collective-permute-start | bytes 1769480 | tf_op jit(solution)/shard_map/ppermute | solution.py:299
  56.7 41.5 %collective-permute-start = (bf16[128,4096]{1,0:T(8,128)(2,1)}, bf16[128,4096]{1,0:T(8,128)(2,1)S(1)}, u32[]{:S(2)}, u32[]{:S(2)}) collective-permute-start(bf16[128,4096]{1,0:T(8,128)(2,1)} %shard_map.132), channel_id=1, source_target_pairs={{0,32},{32,0},{1,33},{33,1},{2,34},{34,2},{3,35},{35,3},{4,36},{36... | collective-permute-start | bytes 3145736 | tf_op jit(solution)/shard_map/ppermute | solution.py:306
  74.3 7.8 %copy-start.3 = (bf16[128,2304]{1,0:T(8,128)(2,1)}, bf16[128,2304]{1,0:T(8,128)(2,1)S(1)}, u32[]{:S(2)}) copy-start(bf16[128,2304]{1,0:T(8,128)(2,1)S(1)} %collective-permute-done.1.far_ca.far_ha) | copy-start | bytes 1769476
  87.0 1.5 copy-start.11
  87.0 3.1 %slice-start = ((bf16[128,2304]{1,0:T(8,128)(2,1)}), bf16[128,1792]{1,0:T(8,128)(2,1)S(1)}, s32[]{:S(2)}) async-start(bf16[128,2304]{1,0:T(8,128)(2,1)} %copy-done.3), calls=%async_computation | async-start | bytes 917504 | tf_op jit(solution)/shard_map/slice | solution.py:316
  87.1 3.1 %slice-start.1 = ((bf16[128,2304]{1,0:T(8,128)(2,1)}), bf16[128,256]{1,0:T(8,128)(2,1)S(1)}, s32[]{:S(2)}) async-start(bf16[128,2304]{1,0:T(8,128)(2,1)} %copy-done.3), calls=%async_computation.1 | async-start | bytes 131072 | tf_op jit(solution)/shard_map/slice | solution.py:316
  87.1 3.1 %copy-start.14 = (bf16[128,256]{1,0:T(8,128)(2,1)S(1)}, bf16[128,256]{1,0:T(8,128)(2,1)}, u32[]{:S(2)}) copy-start(bf16[128,256]{1,0:T(8,128)(2,1)} %slice.63) | copy-start | bytes 196612
  88.6 5.6 %collective-permute-start.11 = (bf16[2,64,576]{2,1,0:T(8,128)(2,1)S(1)}, bf16[2,64,576]{2,1,0:T(8,128)(2,1)S(1)}, u32[]{:S(2)}, u32[]{:S(2)}) collective-permute-start(bf16[2,64,576]{2,1,0:T(8,128)(2,1)S(1)} %get-tuple-element.24), channel_id=1, source_target_pairs={{0,1},{1,2},{2,3},{3,0},{4,5},{5,6},{6,7},{7,4},{8,9},{9,10},{10,1... | collective-permute-start | bytes 442376 | tf_op jit(solution)/shard_map/ppermute | solution.py:257
  91.2 7.0 %collective-permute-start.3 = (bf16[128,4096]{1,0:T(8,128)(2,1)}, bf16[128,4096]{1,0:T(8,128)(2,1)S(1)}, u32[]{:S(2)}, u32[]{:S(2)}) collective-permute-start(bf16[128,4096]{1,0:T(8,128)(2,1)} %pad_maximum_fusion.2), channel_id=1, source_target_pairs={{0,32},{32,0},{1,33},{33,1},{2,34},{34,2},{3,35},{35,3},{4,36},{36... | collective-permute-start | bytes 3145736 | tf_op jit(solution)/shard_map/ppermute | solution.py:314
  91.2 7.0 %copy-start.10 = (bf16[128,512]{1,0:T(8,128)(2,1)S(1)}, bf16[128,512]{1,0:T(8,128)(2,1)}, u32[]{:S(2)}) copy-start(bf16[128,512]{1,0:T(8,128)(2,1)} %copy-done.9) | copy-start | bytes 393220
  91.3 5.4 %collective-permute-start.13 = (bf16[2,64,576]{2,1,0:T(8,128)(2,1)S(1)}, bf16[2,64,576]{2,1,0:T(8,128)(2,1)S(1)}, u32[]{:S(2)}, u32[]{:S(2)}) collective-permute-start(bf16[2,64,576]{2,1,0:T(8,128)(2,1)S(1)} %get-tuple-element.27), channel_id=1, source_target_pairs={{0,3},{1,0},{2,1},{3,2},{4,7},{5,4},{6,5},{7,6},{8,11},{9,8},{10,9... | collective-permute-start | bytes 442376 | tf_op jit(solution)/shard_map/ppermute | solution.py:258
  94.3 18.5 %collective-permute-start.12 = (bf16[4,64,576]{2,1,0:T(8,128)(2,1)S(1)}, bf16[4,64,576]{2,1,0:T(8,128)(2,1)}, u32[]{:S(2)}, u32[]{:S(2)}) collective-permute-start(bf16[4,64,576]{2,1,0:T(8,128)(2,1)S(1)} %pad_maximum_fusion.3), channel_id=1, source_target_pairs={{0,1},{1,2},{2,3},{3,0},{4,5},{5,6},{6,7},{7,4},{8,9},{9,10},{10,1... | collective-permute-start | bytes 884744 | tf_op jit(solution)/shard_map/ppermute | solution.py:271
  97.5 15.2 %collective-permute-start.14 = (bf16[4,64,576]{2,1,0:T(8,128)(2,1)}, bf16[4,64,576]{2,1,0:T(8,128)(2,1)}, u32[]{:S(2)}, u32[]{:S(2)}) collective-permute-start(bf16[4,64,576]{2,1,0:T(8,128)(2,1)} %pad_maximum_fusion.4), channel_id=1, source_target_pairs={{0,3},{1,0},{2,1},{3,2},{4,7},{5,4},{6,5},{7,6},{8,11},{9,8},{10,9... | collective-permute-start | bytes 884744 | tf_op jit(solution)/shard_map/ppermute | solution.py:272
  98.2 1.1 copy-start.4
  105.4 28.3 %copy-start.5 = (f32[1,128,3584]{2,1,0:T(8,128)S(1)}, f32[1,128,3584]{2,1,0:T(8,128)}, u32[]{:S(2)}) copy-start(f32[1,128,3584]{2,1,0:T(8,128)} %param.15) | copy-start | bytes 5505028
  105.4 26.0 %collective-permute-start.4 = (bf16[128,1792]{1,0:T(8,128)(2,1)}, bf16[128,1792]{1,0:T(8,128)(2,1)S(1)}, u32[]{:S(2)}, u32[]{:S(2)}) collective-permute-start(bf16[128,1792]{1,0:T(8,128)(2,1)} %get-tuple-element.12), channel_id=1, source_target_pairs={{0,192},{192,0},{64,128},{128,64},{1,193},{193,1},{65,129},{129,65... | collective-permute-start | bytes 1376264 | tf_op jit(solution)/shard_map/ppermute | solution.py:322
  111.3 22.5 %collective-permute-start.5 = (bf16[128,1792]{1,0:T(8,128)(2,1)}, bf16[128,1792]{1,0:T(8,128)(2,1)S(1)}, u32[]{:S(2)}, u32[]{:S(2)}) collective-permute-start(bf16[128,1792]{1,0:T(8,128)(2,1)} %get-tuple-element.13), channel_id=1, source_target_pairs={{0,64},{64,0},{128,192},{192,128},{1,65},{65,1},{129,193},{193,129... | collective-permute-start | bytes 1376264 | tf_op jit(solution)/shard_map/ppermute | solution.py:323
  114.8 30.1 %collective-permute-start.15 = (bf16[4,32,576]{2,1,0:T(8,128)(2,1)}, bf16[4,32,576]{2,1,0:T(8,128)(2,1)}, u32[]{:S(2)}, u32[]{:S(2)}) collective-permute-start(bf16[4,32,576]{2,1,0:T(8,128)(2,1)} %fusion.7), channel_id=1, source_target_pairs={{0,16},{16,0},{1,17},{17,1},{2,18},{18,2},{3,19},{19,3},{4,20},{20... | collective-permute-start | bytes 442376 | tf_op jit(solution)/shard_map/ppermute | solution.py:328
  133.7 1.5 copy-start.6
  135.2 21.9 %copy-start.15 = (f32[28,576]{1,0:T(8,128)S(1)}, f32[28,576]{1,0:T(8,128)}, u32[]{:S(2)}) copy-start(f32[28,576]{1,0:T(8,128)} %param.20) | copy-start | bytes 193540
  135.2 21.9 %copy-start.16 = (f32[28,576]{1,0:T(8,128)S(1)}, f32[28,576]{1,0:T(8,128)}, u32[]{:S(2)}) copy-start(f32[28,576]{1,0:T(8,128)} %param.22) | copy-start | bytes 193540
  135.2 21.9 %copy-start.17 = (f32[28,576]{1,0:T(8,128)S(1)}, f32[28,576]{1,0:T(8,128)}, u32[]{:S(2)}) copy-start(f32[28,576]{1,0:T(8,128)} %param.21) | copy-start | bytes 193540
  145.9 7.4 %collective-permute-start.16 = (bf16[32,576]{1,0:T(8,128)(2,1)S(1)}, bf16[32,576]{1,0:T(8,128)(2,1)S(1)}, u32[]{:S(2)}, u32[]{:S(2)}) collective-permute-start(bf16[32,576]{1,0:T(8,128)(2,1)S(1)} %get-tuple-element.28), channel_id=1, source_target_pairs={{0,64},{64,128},{128,192},{192,0},{1,65},{65,129},{129,193},{193,1... | collective-permute-start | bytes 110600 | tf_op jit(solution)/shard_map/ppermute | solution.py:332
  149.2 7.9 %collective-permute-start.17 = (bf16[32,576]{1,0:T(8,128)(2,1)S(1)}, bf16[32,576]{1,0:T(8,128)(2,1)S(1)}, u32[]{:S(2)}, u32[]{:S(2)}) collective-permute-start(bf16[32,576]{1,0:T(8,128)(2,1)S(1)} %get-tuple-element.30), channel_id=1, source_target_pairs={{0,128},{64,192},{128,0},{192,64},{1,129},{65,193},{129,1},{193,65... | collective-permute-start | bytes 110600 | tf_op jit(solution)/shard_map/ppermute | solution.py:332
  150.6 6.5 %collective-permute-start.18 = (bf16[32,576]{1,0:T(8,128)(2,1)S(1)}, bf16[32,576]{1,0:T(8,128)(2,1)S(1)}, u32[]{:S(2)}, u32[]{:S(2)}) collective-permute-start(bf16[32,576]{1,0:T(8,128)(2,1)S(1)} %get-tuple-element.29), channel_id=1, source_target_pairs={{0,192},{64,0},{128,64},{192,128},{1,193},{65,1},{129,65},{193,129... | collective-permute-start | bytes 110600 | tf_op jit(solution)/shard_map/ppermute | solution.py:332

commit v2 on v0

v2 whole, which is shorter than its diff:
```python
import functools
import jax
import jax.numpy as jnp
from jax import lax
from jax.experimental import pallas as pl
from jax.experimental.pallas import tpu as pltpu
from jax.sharding import Mesh, PartitionSpec as P

beta_first = 0.9
beta_second = 0.999
step_count = 1000.0
learn_rate = 0.05
weight_decay = 0.1
epsilon = 1e-08

SLOT = 128
HID = 1024
DW = 3584
HALF = 1792
TILE = 896
D = 7168
KV = 576
PART = 896
ROWS = 28
PAD = 32
bf16, f32 = jnp.bfloat16, jnp.float32

PAIR_A = [(0, 1), (1, 0), (2, 3), (3, 2)]
PAIR_B = [(0, 3), (3, 0), (1, 2), (2, 1)]
VMEM = 24 * 1024 * 1024
ADAM_COST = pl.CostEstimate(flops=20_000_000, bytes_accessed=10_000_000, transcendentals=0)
FAR_COST = pl.CostEstimate(flops=6_000_000_000, bytes_accessed=4_000_000, transcendentals=0)


def adam_step(master, moment, variance, gradient):
    moment_new = beta_first * moment + (1.0 - beta_first) * gradient
    variance_new = beta_second * variance + (1.0 - beta_second) * gradient * gradient
    first_fix = 1.0 - beta_first**step_count
    second_fix = 1.0 - beta_second**step_count
    update = moment_new / first_fix / (jnp.sqrt(variance_new / second_fix) + epsilon)
    return master - learn_rate * (update + weight_decay * master)


def dot0(left, right):
    return lax.dot_general(left, right, (((0,), (0,)), ((), ())), preferred_element_type=f32)


def spot_of(*axes):
    return tuple(lax.axis_index(a) for a in axes)


def masked_blocks(counts, hid_ref, masked):
    live = lax.broadcasted_iota(jnp.int32, (SLOT, HID), 0) < counts[0, 0]
    masked[...] = jnp.where(live, hid_ref[...], jnp.zeros_like(hid_ref))

    def block(chip, which):
        start = pl.multiple_of((chip * 2 + which) * 128, 128)
        return masked[:, pl.ds(start, 128)]

    return block


def nearest(j):
    return j + 1 - 2 * lax.rem(j, 2), 3 - j, lax.rem(j + 2, 4)


def pack_kernel(counts, hid_ref, cot_ref, to_a, to_b, own_ref, masked, sems):
    j, core = spot_of("zh", "co")
    other = 1 - core
    near_a, near_b, across = nearest(j)
    copies = [
        pltpu.make_async_copy(
            cot_ref.at[:, n * HALF : (n + 1) * HALF], to.at[:, :HALF], sems.at[n]
        )
        for n, to in enumerate((to_a, to_b))
    ]
    for copy in copies:
        copy.start()
    block = masked_blocks(counts, hid_ref, masked)
    for to, near in ((to_a, near_a), (to_b, near_b)):
        for n, (chip, which) in enumerate(
            ((near, core), (across, core), (near, other), (across, other))
        ):
            to[:, HALF + n * 128 : HALF + (n + 1) * 128] = block(chip, which)
    for n, chip in enumerate((j, near_b, j, near_a)):
        own_ref[:, n * 128 : (n + 1) * 128] = block(chip, core)
    for copy in copies:
        copy.wait()


def sibling_kernel(counts, hid_ref, cot_ref, out_ref, masked, sems):
    j, core = spot_of("zh", "co")
    near_a, near_b, _ = nearest(j)
    copy = pltpu.make_async_copy(cot_ref, out_ref.at[:, :DW], sems.at[0])
    copy.start()
    block = masked_blocks(counts, hid_ref, masked)
    for n, chip in enumerate((j, near_b, j, near_a)):
        out_ref[:, DW + n * 128 : DW + (n + 1) * 128] = block(chip, 1 - core)
    copy.wait()


def dense_pack_kernel(lay_ref, cot_ref, out_ref, own_ref, cot, sems):
    j, core = spot_of("zh", "co")
    last = pltpu.make_async_copy(cot_ref, cot, sems.at[8])
    last.start()
    copies = []
    for n in range(4):
        for m, (ref, side) in enumerate(((out_ref, 1 - core), (own_ref, core))):
            start = pl.multiple_of((2 * lax.rem(j + n, 4) + side) * PART, 128)
            copies.append(
                pltpu.make_async_copy(
                    lay_ref.at[:, pl.ds(start, PART)],
                    ref.at[:, n * PART : (n + 1) * PART],
                    sems.at[2 * n + m],
                )
            )
    for copy in copies[::2] + copies[1::2]:
        copy.start()
    last.wait()
    out_ref[:, 4 * PART : 4 * PART + KV] = cot[...].T
    out_ref[:, 4 * PART + KV :] = jnp.zeros((SLOT, 64), bf16)
    for copy in copies:
        copy.wait()


def whole(shape):
    return pl.BlockSpec(shape, lambda *_: (0,) * len(shape))


def in_vmem(kernel, outs, *args, scratch=(), far=(), vmem=VMEM, cost=None):
    specs = [
        pl.BlockSpec(
            memory_space=pltpu.SMEM if a.dtype == jnp.int32 else pltpu.HBM if n in far else pltpu.VMEM
        )
        for n, a in enumerate(args)
    ]
    return pl.pallas_call(
        kernel,
        out_shape=[jax.ShapeDtypeStruct(shape, dtype) for shape, dtype in outs],
        in_specs=specs,
        out_specs=[pl.BlockSpec(memory_space=pltpu.VMEM)] * len(outs),
        scratch_shapes=scratch,
        cost_estimate=cost,
        compiler_params=pltpu.CompilerParams(vmem_limit_bytes=vmem),
    )(*args)


def far_kernel(near_a, near_b, out):
    for n, near in enumerate((near_a, near_b)):
        at = n * (HALF + 256)
        out[:, at : at + HALF] = near[:, :HALF]
        out[:, at + HALF : at + HALF + 256] = near[:, HALF + 256 :]


def products_kernel(cot, own, sib, near_a, near_b, far, a0, a1, b0, b1, keep):
    for n, (near, sends) in enumerate(((near_a, (a0, a1)), (near_b, (b0, b1)))):
        at = n * HALF
        there = n * (HALF + 256)
        h = jnp.concatenate(
            [
                own[:, n * 256 : n * 256 + 256],
                sib[:, DW + n * 256 : DW + n * 256 + 256],
                near[:, HALF : HALF + 256],
                far[:, there + HALF : there + HALF + 256],
            ]
        )
        c = jnp.concatenate(
            [cot[:, at : at + HALF], sib[:, at : at + HALF], near[:, :HALF],
             far[:, there : there + HALF]]
        )
        result = dot0(h, c)
        keep[n] = result[:SLOT]
        for i, send in enumerate(sends):
            send[...] = result[SLOT:, i * TILE : (i + 1) * TILE].astype(bf16)


def expert_products(*args):
    outs = [((SLOT, TILE), bf16)] * 4 + [((2, SLOT, HALF), f32)]
    return in_vmem(products_kernel, outs, *args)


def expert_adam_kernel(keep, a0, a1, b0, b1, master, moment, variance, out):
    for n, got in enumerate((a0, a1, b0, b1)):

        @pl.when(pl.program_id(0) == n)
        def _(got=got):
            gradient = keep[0] + got[...].astype(f32)
            out[...] = adam_step(master[...], moment[...], variance[...], gradient)


def expert_adam(keep, got, master, moment, variance):
    wide = pl.BlockSpec((SLOT, TILE), lambda n: (0, n))
    return pl.pallas_call(
        expert_adam_kernel,
        grid=(4,),
        out_shape=jax.ShapeDtypeStruct((SLOT, DW), f32),
        in_specs=[
            pl.BlockSpec((1, SLOT, TILE), lambda n: (n // 2, 0, n % 2)),
            *[pl.BlockSpec((SLOT, TILE), lambda n: (0, 0))] * 4,
            wide, wide, wide,
        ],
        out_specs=wide,
        cost_estimate=ADAM_COST,
        compiler_params=pltpu.CompilerParams(vmem_limit_bytes=VMEM),
    )(keep, *got, master, moment, variance)


def order_kernel(order):
    core, low, x, y = spot_of("co", "zl", "x", "y")
    place = lax.broadcasted_iota(jnp.int32, (1, 1024), 1)
    first = (place // 256 + x + core * (y - x)) % 4
    second = (place // 64 % 4 + y + core * (x - y)) % 4
    half = (place // 32 % 2 + low) % 2
    row = place % PAD
    spot = half * 448 + first * (112 - 84 * core) + second * (28 + 84 * core) + row
    spot = jnp.where(row < ROWS, spot, -1)
    rows = lax.broadcasted_iota(jnp.int32, (PART, 1024), 0)
    order[...] = jnp.where(rows == spot, 1.0, 0.0).astype(bf16)


def permute_kernel(order, own, to_core, got, *outs):
    for n in range(4):
        part = slice(n * PART, (n + 1) * PART)
        tokens = jnp.concatenate([own[:, part], got[:, part]])
        moved = jnp.dot(tokens, order[...], preferred_element_type=f32).astype(bf16)
        for k, out in enumerate(outs):
            out[:, n * 256 : n * 256 + 256] = moved[:, k * 256 : k * 256 + 256]
    for out in outs:
        out[:SLOT, 1024:] = to_core[:, 4 * PART :]
        out[SLOT:, 1024:] = got[:, 4 * PART :]


def dense_product_kernel(b0, b1, b2, b3, keep, up, across, down):
    blocks = (b0, b1, b2, b3)
    grads = jnp.concatenate([b[:, 1024 : 1024 + KV] for b in blocks])
    for n in range(4):
        tokens = jnp.concatenate([b[:, n * 256 : n * 256 + 256] for b in blocks])
        result = dot0(tokens, grads)
        keep[n] = result[:64]
        for k, out in enumerate((up, across, down)):
            out[n] = result[64 * k + 64 : 64 * k + 128].astype(bf16)


def plane_pairs(stage, step):
    pairs = []
    for core in range(2):
        for x in range(4):
            for y in range(4):
                along_x = (core + stage) % 2 == 0
                to = ((x + step) % 4, y) if along_x else (x, (y + step) % 4)
                pairs.append((core * 16 + x * 4 + y, core * 16 + to[0] * 4 + to[1]))
    return pairs


def add(*terms):
    return functools.reduce(lambda a, b: a + b, [t.astype(f32) for t in terms])


def tie(values, *others):
    return lax.optimization_barrier((values, others))[0]


def on_device(
    expert_inputs,
    expert_cotangent,
    row_counts,
    expert_master,
    expert_moment,
    expert_variance,
    layer_inputs,
    layer_cotangent,
    dense_master,
    dense_moment,
    dense_variance,
):
    hid, cot = expert_inputs[0], expert_cotangent[0]
    swap = [(0, 1), (1, 0)]

    (order,) = in_vmem(order_kernel, [((PART, 1024), bf16)])
    to_core, own_part = in_vmem(
        dense_pack_kernel,
        [((SLOT, 4224), bf16), ((SLOT, 4 * PART), bf16)],
        layer_inputs,
        layer_cotangent.T,
        scratch=[pltpu.VMEM((KV, SLOT), bf16), pltpu.SemaphoreType.DMA((9,))],
        far=(0, 1),
        vmem=56 * 1024 * 1024,
    )
    dense_got = lax.ppermute(to_core, "co", swap)

    to_a, to_b, own = in_vmem(
        pack_kernel,
        [((SLOT, w), bf16) for w in (2304, 2304, 512)],
        row_counts,
        hid,
        cot,
        scratch=[pltpu.VMEM((SLOT, HID), bf16), pltpu.SemaphoreType.DMA((2,))],
        far=(2,),
    )
    near_a = lax.ppermute(to_a, "zh", PAIR_A)
    near_b = lax.ppermute(to_b, "zh", PAIR_B)
    (to_sib,) = in_vmem(
        sibling_kernel,
        [((SLOT, DW + 512), bf16)],
        row_counts,
        hid,
        cot,
        scratch=[pltpu.VMEM((SLOT, HID), bf16), pltpu.SemaphoreType.DMA((1,))],
        far=(2,),
    )
    sib = lax.ppermute(to_sib, "co", swap)

    axes = ("co", "x", "y")
    blocks = list(
        in_vmem(permute_kernel, [((256, 1664), bf16)] * 4, order, own_part, to_core, dense_got)
    )
    blocks = [blocks[0]] + [
        lax.ppermute(blocks[step], axes, plane_pairs(0, step)) for step in (2, 1, 3)
    ]
    keep, up, across, down = in_vmem(
        dense_product_kernel, [((4, 64, KV), f32)] + [((4, 64, KV), bf16)] * 3, *blocks
    )

    (to_far,) = in_vmem(
        far_kernel, [((SLOT, DW + 512), bf16)], near_a, near_b, cost=FAR_COST
    )
    far = lax.ppermute(tie(to_far, *blocks[1:]), "co", swap)
    a0, a1, b0, b1, mine_too = expert_products(cot, own, sib, near_a, near_b, far)
    sums = [
        lax.ppermute(send, "zh", pairs)
        for send, pairs in ((a0, PAIR_B), (a1, PAIR_B), (b0, PAIR_A), (b1, PAIR_A))
    ]

    up, across, down = tie((up, across, down), a0)
    terms = [
        lax.ppermute(block, axes, plane_pairs(1, step))
        for step, block in ((2, across), (1, up), (3, down))
    ]

    line = add(tie(keep, sums[0], sums[2]), *terms).reshape(4, 2, PAD, KV)
    mine = line[:, 0] + lax.ppermute(line[:, 1].astype(bf16), "zl", swap).astype(f32)
    dense_grad = mine[0]
    for step in (2, 1, 3):
        got = lax.ppermute(mine[step].astype(bf16), "zh", [(i, (i + step) % 4) for i in range(4)])
        dense_grad = dense_grad + got.astype(f32)
    dense_updated = adam_step(dense_master, dense_moment, dense_variance, dense_grad[:ROWS])

    expert_updated = expert_adam(
        mine_too, sums, expert_master[0], expert_moment[0], expert_variance[0]
    )
    return (expert_updated[None], dense_updated)


def solution(mesh):
    fine = Mesh(mesh.devices.reshape(4, 2, 2, 4, 4), ("zh", "co", "zl", "x", "y"))
    ep, rep = ("zl", "x", "y"), ("zh", "co")
    expert = P(ep, rep, None)
    dense = P(rep + ep, None)
    in_specs = (expert, expert, P(ep, rep)) + (expert,) * 3 + (dense,) * 5
    return jax.shard_map(
        on_device, mesh=fine, in_specs=in_specs, out_specs=(expert, dense), check_vma=False
    )
```

time: 975 us -> 92.9 us (0.10)
  blocking collectives: 751 us -> 0 us
  local copies, waits for them, and re-layouts: 71.2 us -> 0.09 us
  starting transfers between devices: 110 us -> 39.5 us
  waiting for transfers between devices: 0.1 us -> 38.4 us
  matrix products: 14 us -> 0 us
  between operations: 15.4 us -> 1.64 us
  Pallas kernels: 0 us -> 12.3 us
    unnamed x1 -> x0, blocking collectives: 751 us -> none
    unnamed x33 -> x0, starting transfers between devices: 110 us -> none
    unnamed x38 -> x20, local copies, waits for them, and re-layouts: 71.2 us -> 0.05 us
    ppermute x0 -> x19, starting transfers between devices: none -> 39.5 us  [the longest x4 10.6 us: on_device(): lax.ppermute(send, 'zh', pairs)]
    ppermute x0 -> x19, waiting for transfers between devices: none -> 38.4 us  [the longest x4 18.4 us: on_device(): lax.ppermute(send, 'zh', pairs)]
    dot_general x2 -> x0, matrix products: 14 us -> none  [transpose_product(): lax.dot_general(left, right, (((0,), (0,)), ((), ())), preferred_element_...]
    pallas_call x0 -> x9, Pallas kernels: none -> 12.3 us  [the longest x8 9.12 us: in_vmem(): pl.pallas_call(kernel, out_shape=[jax.ShapeDtypeStruct(shape, dtype) for...]
  transfers between devices with their start and end apart: 33 -> 19, of which waited for: 0 -> 11; matrix products, arithmetic and copies ran while one was open for 84% -> 0% of each run, Pallas kernels for 0% -> 9%
where the time goes in v2:
time: 92.9 us; the launch traced here: 92.8 us
  starting transfers between devices  39.5 us (43%)
  waiting for transfers between devices  38.4 us (41%)
  Pallas kernels  12.3 us (13%)
  between operations  1.64 us (2%)
    ppermute x4, waiting for transfers between devices, on_device(): lax.ppermute(send, 'zh', pairs)  18.4 us
    ppermute x1, waiting for transfers between devices, on_device(): near_a = lax.ppermute(to_a, 'zh', PAIR_A)  12.9 us
    ppermute x4, starting transfers between devices, on_device(): lax.ppermute(send, 'zh', pairs)  10.6 us
    ppermute x3, starting transfers between devices, on_device(): lax.ppermute(mine[step].astype(bf16), 'zh', [(i, (i + step) % 4) for i in...  10.1 us
    pallas_call x8, Pallas kernels, in_vmem(): pl.pallas_call(kernel, out_shape=[jax.ShapeDtypeStruct(shape, dtype) for...  9.12 us
    ppermute x3, starting transfers between devices, on_device(): lax.ppermute(blocks[step], axes, plane_pairs(0, step))  6.35 us
    ppermute x1, starting transfers between devices, on_device(): near_b = lax.ppermute(to_b, 'zh', PAIR_B)  4.48 us
    ppermute x3, starting transfers between devices, on_device(): lax.ppermute(block, axes, plane_pairs(1, step))  4.41 us
  transfers between devices with their start and end apart: 19, of which 11 were waited for; matrix products, arithmetic and copies ran while one was open for 0% of the time, Pallas kernels for 9%

profile of v2, /device:TPU:8, one launch (start us, length us, event | category | flops | bytes accessed | tf_op | source)
XLA Modules:
  0.0 92.8 jit_solution(7484813443497342854)
XLA Ops:
  0.7 3.0 %shard_map.126 = (bf16[128,4224]{1,0:T(8,128)(2,1)}, bf16[128,3584]{1,0:T(8,128)(2,1)}) custom-call(bf16[128,7168]{1,0:T(8,128)(2,1)} %lay_ref.1, bf16[576,128]{1,0:T(8,128)(2,1)} %bitcast.34), custom_call_target="tpu_custom_call" | custom-call | tf_op jit(solution)/shard_map/pallas_call | solution.py:137
  3.7 0.0 copy-start.4
  3.7 0.1 collective-permute-start.3
  4.6 0.2 shard_map.122
  4.8 3.4 %collective-permute-start.1 = (bf16[128,2304]{1,0:T(8,128)(2,1)S(1)}, bf16[128,2304]{1,0:T(8,128)(2,1)S(1)}, u32[]{:S(2)}, u32[]{:S(2)}) collective-permute-start(bf16[128,2304]{1,0:T(8,128)(2,1)S(1)} %get-tuple-element.26), channel_id=1, source_target_pairs={{0,64},{64,0},{128,192},{192,128},{1,65},{65,1},{129,193},{193,129... | collective-permute-start | bytes 1769480 | tf_op jit(solution)/shard_map/ppermute | solution.py:300
  8.2 4.5 %collective-permute-start.2 = (bf16[128,2304]{1,0:T(8,128)(2,1)S(1)}, bf16[128,2304]{1,0:T(8,128)(2,1)S(1)}, u32[]{:S(2)}, u32[]{:S(2)}) collective-permute-start(bf16[128,2304]{1,0:T(8,128)(2,1)S(1)} %get-tuple-element.27), channel_id=1, source_target_pairs={{0,192},{192,0},{64,128},{128,64},{1,193},{193,1},{65,129},{129,65... | collective-permute-start | bytes 1769480 | tf_op jit(solution)/shard_map/ppermute | solution.py:301
  12.7 0.4 shard_map.125.order
  13.1 2.3 %shard_map.127 = (bf16[256,1664]{1,0:T(8,128)(2,1)S(1)}, bf16[256,1664]{1,0:T(8,128)(2,1)S(1)}, bf16[256,1664]{1,0:T(8,128)(2,1)S(1)}, bf16[256,1664]{1,0:T(8,128)(2,1)S(1)}) custom-call(bf16[896,1024]{1,0:T(8,128)(2,1)S(1)} %shard_map.125.order, bf16[128,3584]{1,0:T(8,128)(2,1)S(1)} %copy-done.6, bf16[128,4224]{1,0:T(8,128)(2,1)S(1)} %copy-done.4, ...), custom_call_target="tpu_custom_call" | custom-call | tf_op jit(solution)/shard_map/pallas_call | solution.py:137
  15.4 3.1 %collective-permute-start.4 = (bf16[256,1664]{1,0:T(8,128)(2,1)S(1)}, bf16[256,1664]{1,0:T(8,128)(2,1)S(1)}, u32[]{:S(2)}, u32[]{:S(2)}) collective-permute-start(bf16[256,1664]{1,0:T(8,128)(2,1)S(1)} %get-tuple-element.30), channel_id=1, source_target_pairs={{0,8},{1,9},{2,10},{3,11},{4,12},{5,13},{6,14},{7,15},{8,0},{9,1},... | collective-permute-start | bytes 2555912 | tf_op jit(solution)/shard_map/ppermute | solution.py:318
  18.5 0.6 collective-permute-start.5
  19.1 2.6 %collective-permute-start.6 = (bf16[256,1664]{1,0:T(8,128)(2,1)S(1)}, bf16[256,1664]{1,0:T(8,128)(2,1)S(1)}, u32[]{:S(2)}, u32[]{:S(2)}) collective-permute-start(bf16[256,1664]{1,0:T(8,128)(2,1)S(1)} %get-tuple-element.32), channel_id=1, source_target_pairs={{0,12},{1,13},{2,14},{3,15},{4,0},{5,1},{6,2},{7,3},{8,4},{9,5},{1... | collective-permute-start | bytes 2555912 | tf_op jit(solution)/shard_map/ppermute | solution.py:318
  21.8 0.1 shard_map.123
  21.9 12.9 %collective-permute-done.1.near_a = bf16[128,2304]{1,0:T(8,128)(2,1)S(1)} collective-permute-done((bf16[128,2304]{1,0:T(8,128)(2,1)S(1)}, bf16[128,2304]{1,0:T(8,128)(2,1)S(1)}, u32[]{:S(2)}, u32[]{:S(2)}) %collective-permute-start.1) | collective-permute-done | bytes 589856 | tf_op jit(solution)/shard_map/ppermute | solution.py:300
  34.8 0.0 collective-permute-start
  34.8 3.4 %collective-permute-done.2.near_b = bf16[128,2304]{1,0:T(8,128)(2,1)S(1)} collective-permute-done((bf16[128,2304]{1,0:T(8,128)(2,1)S(1)}, bf16[128,2304]{1,0:T(8,128)(2,1)S(1)}, u32[]{:S(2)}, u32[]{:S(2)}) %collective-permute-start.2) | collective-permute-done | bytes 589856 | tf_op jit(solution)/shard_map/ppermute | solution.py:301
  38.2 0.1 shard_map.124
  38.3 0.0 collective-permute-done.4.b1
  38.3 0.6 collective-permute-done.5.b2
  38.8 0.1 collective-permute-done.6.b3
  39.0 0.0 collective-permute-start.7
  39.0 1.8 %shard_map.130 = (f32[4,64,576]{2,1,0:T(8,128)S(1)}, bf16[4,64,576]{2,1,0:T(8,128)(2,1)S(1)}, bf16[4,64,576]{2,1,0:T(8,128)(2,1)S(1)}, bf16[4,64,576]{2,1,0:T(8,128)(2,1)S(1)}) custom-call(bf16[256,1664]{1,0:T(8,128)(2,1)S(1)} %get-tuple-element.39.b0, bf16[256,1664]{1,0:T(8,128)(2,1)S(1)} %collective-permute-done.4.b1, ...), custom_call_target="tpu_custom_call" | custom-call | tf_op jit(solution)/shard_map/pallas_call | solution.py:137
  40.8 0.0 collective-permute-done.sib
  40.8 0.8 collective-permute-done.7.far
  41.6 1.1 %shard_map.128 = (bf16[128,896]{1,0:T(8,128)(2,1)S(1)}, bf16[128,896]{1,0:T(8,128)(2,1)S(1)}, bf16[128,896]{1,0:T(8,128)(2,1)S(1)}, bf16[128,896]{1,0:T(8,128)(2,1)S(1)}, f32[2,128,1792]{2,1,0:T(8,128)S(1)}) custom-call(bf16[128,3584]{1,0:T(8,128)(2,1)S(1)} %bitcast.25, bf16[128,512]{1,0:T(8,128)(2,1)S(1)} %get-tuple-element.25.own, ...), custom_call_target="tpu_custom_call" | custom-call | tf_op jit(solution)/shard_map/pallas_call | solution.py:137
  42.8 0.0 copy-start.1
  42.8 2.4 %collective-permute-start.12 = (bf16[4,64,576]{2,1,0:T(8,128)(2,1)S(1)}, bf16[4,64,576]{2,1,0:T(8,128)(2,1)S(1)}, u32[]{:S(2)}, u32[]{:S(2)}) collective-permute-start(bf16[4,64,576]{2,1,0:T(8,128)(2,1)S(1)} %get-tuple-element.45), channel_id=1, source_target_pairs={{0,2},{1,3},{2,0},{3,1},{4,6},{5,7},{6,4},{7,5},{8,10},{9,11},{10,... | collective-permute-start | bytes 884744 | tf_op jit(solution)/shard_map/ppermute | solution.py:336
  45.2 2.0 %collective-permute-start.14 = (bf16[4,64,576]{2,1,0:T(8,128)(2,1)S(1)}, bf16[4,64,576]{2,1,0:T(8,128)(2,1)S(1)}, u32[]{:S(2)}, u32[]{:S(2)}) collective-permute-start(bf16[4,64,576]{2,1,0:T(8,128)(2,1)S(1)} %get-tuple-element.47), channel_id=1, source_target_pairs={{0,3},{1,0},{2,1},{3,2},{4,7},{5,4},{6,5},{7,6},{8,11},{9,8},{10,9... | collective-permute-start | bytes 884744 | tf_op jit(solution)/shard_map/ppermute | solution.py:336
  47.2 4.0 %collective-permute-start.8 = (bf16[128,896]{1,0:T(8,128)(2,1)S(1)}, bf16[128,896]{1,0:T(8,128)(2,1)S(1)}, u32[]{:S(2)}, u32[]{:S(2)}) collective-permute-start(bf16[128,896]{1,0:T(8,128)(2,1)S(1)} %get-tuple-element.35), channel_id=1, source_target_pairs={{0,192},{192,0},{64,128},{128,64},{1,193},{193,1},{65,129},{129,65... | collective-permute-start | bytes 688136 | tf_op jit(solution)/shard_map/ppermute | solution.py:330
  51.2 1.4 %collective-permute-start.10 = (bf16[128,896]{1,0:T(8,128)(2,1)S(1)}, bf16[128,896]{1,0:T(8,128)(2,1)S(1)}, u32[]{:S(2)}, u32[]{:S(2)}) collective-permute-start(bf16[128,896]{1,0:T(8,128)(2,1)S(1)} %get-tuple-element.37), channel_id=1, source_target_pairs={{0,64},{64,0},{128,192},{192,128},{1,65},{65,1},{129,193},{193,129... | collective-permute-start | bytes 688136 | tf_op jit(solution)/shard_map/ppermute | solution.py:330
  52.5 9.6 %collective-permute-done.8.a0 = bf16[128,896]{1,0:T(8,128)(2,1)S(1)} collective-permute-done((bf16[128,896]{1,0:T(8,128)(2,1)S(1)}, bf16[128,896]{1,0:T(8,128)(2,1)S(1)}, u32[]{:S(2)}, u32[]{:S(2)}) %collective-permute-start.8) | collective-permute-done | bytes 229408 | tf_op jit(solution)/shard_map/ppermute | solution.py:330
  62.1 1.9 %collective-permute-start.11 = (bf16[128,896]{1,0:T(8,128)(2,1)S(1)}, bf16[128,896]{1,0:T(8,128)(2,1)S(1)}, u32[]{:S(2)}, u32[]{:S(2)}) collective-permute-start(bf16[128,896]{1,0:T(8,128)(2,1)S(1)} %get-tuple-element.38), channel_id=1, source_target_pairs={{0,64},{64,0},{128,192},{192,128},{1,65},{65,1},{129,193},{193,129... | collective-permute-start | bytes 688136 | tf_op jit(solution)/shard_map/ppermute | solution.py:330
  64.0 0.5 collective-permute-done.10.b0
  64.5 3.4 %collective-permute-start.9 = (bf16[128,896]{1,0:T(8,128)(2,1)S(1)}, bf16[128,896]{1,0:T(8,128)(2,1)S(1)}, u32[]{:S(2)}, u32[]{:S(2)}) collective-permute-start(bf16[128,896]{1,0:T(8,128)(2,1)S(1)} %get-tuple-element.36), channel_id=1, source_target_pairs={{0,192},{192,0},{64,128},{128,64},{1,193},{193,1},{65,129},{129,65... | collective-permute-start | bytes 688136 | tf_op jit(solution)/shard_map/ppermute | solution.py:330
  67.9 0.0 collective-permute-done.12
  67.9 0.0 collective-permute-done.13
  67.9 0.1 convert_add_fusion
  68.1 0.1 collective-permute-start.15
  68.2 7.0 %collective-permute-done.11.b1 = bf16[128,896]{1,0:T(8,128)(2,1)S(1)} collective-permute-done((bf16[128,896]{1,0:T(8,128)(2,1)S(1)}, bf16[128,896]{1,0:T(8,128)(2,1)S(1)}, u32[]{:S(2)}, u32[]{:S(2)}) %collective-permute-start.11) | collective-permute-done | bytes 229408 | tf_op jit(solution)/shard_map/ppermute | solution.py:330
  75.2 1.4 %collective-permute-done.9.a1 = bf16[128,896]{1,0:T(8,128)(2,1)S(1)} collective-permute-done((bf16[128,896]{1,0:T(8,128)(2,1)S(1)}, bf16[128,896]{1,0:T(8,128)(2,1)S(1)}, u32[]{:S(2)}, u32[]{:S(2)}) %collective-permute-start.9) | collective-permute-done | bytes 229408 | tf_op jit(solution)/shard_map/ppermute | solution.py:330
  76.5 0.0 copy-start.8
  76.6 0.0 copy-start.9
  76.6 3.2 %shard_map.129 = f32[128,3584]{1,0:T(8,128)} custom-call(f32[2,128,1792]{2,1,0:T(8,128)S(1)} %get-tuple-element.34.keep, bf16[128,896]{1,0:T(8,128)(2,1)S(1)} %collective-permute-done.8.a0, bf16[128,896]{1,0:T(8,128)(2,1)S(1)} %collective-permute-done.9.a1, bf16[128,896]{1,0:T(8,128)(2,1)S(1)} %collective-permute-done.10.b0, ...), custom_call_target="tpu_custom_call" | custom-call | flops 20000000 | bytes 10000000 | tf_op jit(solution)/shard_map/pallas_call | solution.py:193
  79.8 5.9 %collective-permute-start.16 = (bf16[32,576]{1,0:T(8,128)(2,1)S(1)}, bf16[32,576]{1,0:T(8,128)(2,1)S(1)}, u32[]{:S(2)}, u32[]{:S(2)}) collective-permute-start(bf16[32,576]{1,0:T(8,128)(2,1)S(1)} %get-tuple-element.50), channel_id=1, source_target_pairs={{0,128},{64,192},{128,0},{192,64},{1,129},{65,193},{129,1},{193,65... | collective-permute-start | bytes 110600 | tf_op jit(solution)/shard_map/ppermute | solution.py:344
  85.8 1.1 %collective-permute-start.17 = (bf16[32,576]{1,0:T(8,128)(2,1)S(1)}, bf16[32,576]{1,0:T(8,128)(2,1)S(1)}, u32[]{:S(2)}, u32[]{:S(2)}) collective-permute-start(bf16[32,576]{1,0:T(8,128)(2,1)S(1)} %get-tuple-element.52), channel_id=1, source_target_pairs={{0,64},{64,128},{128,192},{192,0},{1,65},{65,129},{129,193},{193,1... | collective-permute-start | bytes 110600 | tf_op jit(solution)/shard_map/ppermute | solution.py:344
  86.8 3.1 %collective-permute-start.18 = (bf16[32,576]{1,0:T(8,128)(2,1)S(1)}, bf16[32,576]{1,0:T(8,128)(2,1)S(1)}, u32[]{:S(2)}, u32[]{:S(2)}) collective-permute-start(bf16[32,576]{1,0:T(8,128)(2,1)S(1)} %get-tuple-element.51), channel_id=1, source_target_pairs={{0,192},{64,0},{128,64},{192,128},{1,193},{65,1},{129,65},{193,129... | collective-permute-start | bytes 110600 | tf_op jit(solution)/shard_map/ppermute | solution.py:344
  89.9 2.0 %collective-permute-done.17 = bf16[32,576]{1,0:T(8,128)(2,1)S(1)} collective-permute-done((bf16[32,576]{1,0:T(8,128)(2,1)S(1)}, bf16[32,576]{1,0:T(8,128)(2,1)S(1)}, u32[]{:S(2)}, u32[]{:S(2)}) %collective-permute-start.17) | collective-permute-done | bytes 36896 | tf_op jit(solution)/shard_map/ppermute | solution.py:344
  91.9 0.2 collective-permute-done.18
  92.0 0.7 multiply_subtract_fusion
  (25 shorter events, 0.1 us)
Async XLA Ops:
  0.6 4.0 %copy-start = (bf16[1,128,3584]{2,1,0:T(8,128)(2,1)S(1)}, bf16[1,128,3584]{2,1,0:T(8,128)(2,1)}, u32[]{:S(2)}) copy-start(bf16[1,128,3584]{2,1,0:T(8,128)(2,1)} %param.12) | copy-start | bytes 2752516
  0.6 4.0 %copy-start.5 = (bf16[1,128,1024]{2,1,0:T(8,128)(2,1)S(1)}, bf16[1,128,1024]{2,1,0:T(8,128)(2,1)}, u32[]{:S(2)}) copy-start(bf16[1,128,1024]{2,1,0:T(8,128)(2,1)} %param.11) | copy-start | bytes 786436
  3.7 9.4 %copy-start.4 = (bf16[128,4224]{1,0:T(8,128)(2,1)S(1)}, bf16[128,4224]{1,0:T(8,128)(2,1)}, u32[]{:S(2)}) copy-start(bf16[128,4224]{1,0:T(8,128)(2,1)} %get-tuple-element.29.to_core) | copy-start | bytes 3244036
  3.7 9.4 %copy-start.6 = (bf16[128,3584]{1,0:T(8,128)(2,1)S(1)}, bf16[128,3584]{1,0:T(8,128)(2,1)}, u32[]{:S(2)}) copy-start(bf16[128,3584]{1,0:T(8,128)(2,1)} %get-tuple-element.28.own) | copy-start | bytes 2752516
  3.7 9.3 %collective-permute-start.3 = (bf16[128,4224]{1,0:T(8,128)(2,1)}, bf16[128,4224]{1,0:T(8,128)(2,1)S(1)}, u32[]{:S(2)}, u32[]{:S(2)}) collective-permute-start(bf16[128,4224]{1,0:T(8,128)(2,1)} %get-tuple-element.29.to_core), channel_id=1, source_target_pairs={{0,32},{32,0},{1,33},{33,1},{2,34},{34,2},{3,35},{35,3},{4,36},{36... | collective-permute-start | bytes 3244040 | tf_op jit(solution)/shard_map/ppermute | solution.py:289
  4.8 30.0 %collective-permute-start.1 = (bf16[128,2304]{1,0:T(8,128)(2,1)S(1)}, bf16[128,2304]{1,0:T(8,128)(2,1)S(1)}, u32[]{:S(2)}, u32[]{:S(2)}) collective-permute-start(bf16[128,2304]{1,0:T(8,128)(2,1)S(1)} %get-tuple-element.26), channel_id=1, source_target_pairs={{0,64},{64,0},{128,192},{192,128},{1,65},{65,1},{129,193},{193,129... | collective-permute-start | bytes 1769480 | tf_op jit(solution)/shard_map/ppermute | solution.py:300
  8.2 30.0 %collective-permute-start.2 = (bf16[128,2304]{1,0:T(8,128)(2,1)S(1)}, bf16[128,2304]{1,0:T(8,128)(2,1)S(1)}, u32[]{:S(2)}, u32[]{:S(2)}) collective-permute-start(bf16[128,2304]{1,0:T(8,128)(2,1)S(1)} %get-tuple-element.27), channel_id=1, source_target_pairs={{0,192},{192,0},{64,128},{128,64},{1,193},{193,1},{65,129},{129,65... | collective-permute-start | bytes 1769480 | tf_op jit(solution)/shard_map/ppermute | solution.py:301
  15.4 22.8 %collective-permute-start.4 = (bf16[256,1664]{1,0:T(8,128)(2,1)S(1)}, bf16[256,1664]{1,0:T(8,128)(2,1)S(1)}, u32[]{:S(2)}, u32[]{:S(2)}) collective-permute-start(bf16[256,1664]{1,0:T(8,128)(2,1)S(1)} %get-tuple-element.30), channel_id=1, source_target_pairs={{0,8},{1,9},{2,10},{3,11},{4,12},{5,13},{6,14},{7,15},{8,0},{9,1},... | collective-permute-start | bytes 2555912 | tf_op jit(solution)/shard_map/ppermute | solution.py:318
  18.5 20.3 %collective-permute-start.5 = (bf16[256,1664]{1,0:T(8,128)(2,1)S(1)}, bf16[256,1664]{1,0:T(8,128)(2,1)S(1)}, u32[]{:S(2)}, u32[]{:S(2)}) collective-permute-start(bf16[256,1664]{1,0:T(8,128)(2,1)S(1)} %get-tuple-element.31), channel_id=1, source_target_pairs={{0,4},{1,5},{2,6},{3,7},{4,8},{5,9},{6,10},{7,11},{8,12},{9,13},{1... | collective-permute-start | bytes 2555912 | tf_op jit(solution)/shard_map/ppermute | solution.py:318
  19.1 19.8 %collective-permute-start.6 = (bf16[256,1664]{1,0:T(8,128)(2,1)S(1)}, bf16[256,1664]{1,0:T(8,128)(2,1)S(1)}, u32[]{:S(2)}, u32[]{:S(2)}) collective-permute-start(bf16[256,1664]{1,0:T(8,128)(2,1)S(1)} %get-tuple-element.32), channel_id=1, source_target_pairs={{0,12},{1,13},{2,14},{3,15},{4,0},{5,1},{6,2},{7,3},{8,4},{9,5},{1... | collective-permute-start | bytes 2555912 | tf_op jit(solution)/shard_map/ppermute | solution.py:318
  34.8 6.0 %collective-permute-start = (bf16[128,4096]{1,0:T(8,128)(2,1)S(1)}, bf16[128,4096]{1,0:T(8,128)(2,1)S(1)}, u32[]{:S(2)}, u32[]{:S(2)}) collective-permute-start(bf16[128,4096]{1,0:T(8,128)(2,1)S(1)} %shard_map.123), channel_id=1, source_target_pairs={{0,32},{32,0},{1,33},{33,1},{2,34},{34,2},{3,35},{35,3},{4,36},{36... | collective-permute-start | bytes 3145736 | tf_op jit(solution)/shard_map/ppermute | solution.py:311
  39.0 2.7 %collective-permute-start.7 = (bf16[128,4096]{1,0:T(8,128)(2,1)S(1)}, bf16[128,4096]{1,0:T(8,128)(2,1)S(1)}, u32[]{:S(2)}, u32[]{:S(2)}) collective-permute-start(bf16[128,4096]{1,0:T(8,128)(2,1)S(1)} %shard_map.124), channel_id=1, source_target_pairs={{0,32},{32,0},{1,33},{33,1},{2,34},{34,2},{3,35},{35,3},{4,36},{36... | collective-permute-start | bytes 3145736 | tf_op jit(solution)/shard_map/ppermute | solution.py:327
  41.6 34.9 %copy-start.2 = (f32[1,128,3584]{2,1,0:T(8,128)S(1)}, f32[1,128,3584]{2,1,0:T(8,128)}, u32[]{:S(2)}) copy-start(f32[1,128,3584]{2,1,0:T(8,128)} %param.15) | copy-start | bytes 5505028
  41.6 34.9 %copy-start.3 = (f32[1,128,3584]{2,1,0:T(8,128)S(1)}, f32[1,128,3584]{2,1,0:T(8,128)}, u32[]{:S(2)}) copy-start(f32[1,128,3584]{2,1,0:T(8,128)} %param.16) | copy-start | bytes 5505028
  42.8 33.8 %copy-start.1 = (f32[1,128,3584]{2,1,0:T(8,128)S(1)}, f32[1,128,3584]{2,1,0:T(8,128)}, u32[]{:S(2)}) copy-start(f32[1,128,3584]{2,1,0:T(8,128)} %param.14) | copy-start | bytes 5505028
  42.8 25.1 %collective-permute-start.12 = (bf16[4,64,576]{2,1,0:T(8,128)(2,1)S(1)}, bf16[4,64,576]{2,1,0:T(8,128)(2,1)S(1)}, u32[]{:S(2)}, u32[]{:S(2)}) collective-permute-start(bf16[4,64,576]{2,1,0:T(8,128)(2,1)S(1)} %get-tuple-element.45), channel_id=1, source_target_pairs={{0,2},{1,3},{2,0},{3,1},{4,6},{5,7},{6,4},{7,5},{8,10},{9,11},{10,... | collective-permute-start | bytes 884744 | tf_op jit(solution)/shard_map/ppermute | solution.py:336
  45.2 22.7 %collective-permute-start.13 = (bf16[4,64,576]{2,1,0:T(8,128)(2,1)S(1)}, bf16[4,64,576]{2,1,0:T(8,128)(2,1)S(1)}, u32[]{:S(2)}, u32[]{:S(2)}) collective-permute-start(bf16[4,64,576]{2,1,0:T(8,128)(2,1)S(1)} %get-tuple-element.46), channel_id=1, source_target_pairs={{0,1},{1,2},{2,3},{3,0},{4,5},{5,6},{6,7},{7,4},{8,9},{9,10},{10,1... | collective-permute-start | bytes 884744 | tf_op jit(solution)/shard_map/ppermute | solution.py:336
  45.2 22.7 %collective-permute-start.14 = (bf16[4,64,576]{2,1,0:T(8,128)(2,1)S(1)}, bf16[4,64,576]{2,1,0:T(8,128)(2,1)S(1)}, u32[]{:S(2)}, u32[]{:S(2)}) collective-permute-start(bf16[4,64,576]{2,1,0:T(8,128)(2,1)S(1)} %get-tuple-element.47), channel_id=1, source_target_pairs={{0,3},{1,0},{2,1},{3,2},{4,7},{5,4},{6,5},{7,6},{8,11},{9,8},{10,9... | collective-permute-start | bytes 884744 | tf_op jit(solution)/shard_map/ppermute | solution.py:336
  47.2 14.9 %collective-permute-start.8 = (bf16[128,896]{1,0:T(8,128)(2,1)S(1)}, bf16[128,896]{1,0:T(8,128)(2,1)S(1)}, u32[]{:S(2)}, u32[]{:S(2)}) collective-permute-start(bf16[128,896]{1,0:T(8,128)(2,1)S(1)} %get-tuple-element.35), channel_id=1, source_target_pairs={{0,192},{192,0},{64,128},{128,64},{1,193},{193,1},{65,129},{129,65... | collective-permute-start | bytes 688136 | tf_op jit(solution)/shard_map/ppermute | solution.py:330
  51.2 13.4 %collective-permute-start.10 = (bf16[128,896]{1,0:T(8,128)(2,1)S(1)}, bf16[128,896]{1,0:T(8,128)(2,1)S(1)}, u32[]{:S(2)}, u32[]{:S(2)}) collective-permute-start(bf16[128,896]{1,0:T(8,128)(2,1)S(1)} %get-tuple-element.37), channel_id=1, source_target_pairs={{0,64},{64,0},{128,192},{192,128},{1,65},{65,1},{129,193},{193,129... | collective-permute-start | bytes 688136 | tf_op jit(solution)/shard_map/ppermute | solution.py:330
  62.1 13.1 %collective-permute-start.11 = (bf16[128,896]{1,0:T(8,128)(2,1)S(1)}, bf16[128,896]{1,0:T(8,128)(2,1)S(1)}, u32[]{:S(2)}, u32[]{:S(2)}) collective-permute-start(bf16[128,896]{1,0:T(8,128)(2,1)S(1)} %get-tuple-element.38), channel_id=1, source_target_pairs={{0,64},{64,0},{128,192},{192,128},{1,65},{65,1},{129,193},{193,129... | collective-permute-start | bytes 688136 | tf_op jit(solution)/shard_map/ppermute | solution.py:330
  64.5 12.0 %collective-permute-start.9 = (bf16[128,896]{1,0:T(8,128)(2,1)S(1)}, bf16[128,896]{1,0:T(8,128)(2,1)S(1)}, u32[]{:S(2)}, u32[]{:S(2)}) collective-permute-start(bf16[128,896]{1,0:T(8,128)(2,1)S(1)} %get-tuple-element.36), channel_id=1, source_target_pairs={{0,192},{192,0},{64,128},{128,64},{1,193},{193,1},{65,129},{129,65... | collective-permute-start | bytes 688136 | tf_op jit(solution)/shard_map/ppermute | solution.py:330
  68.1 11.7 %collective-permute-start.15 = (bf16[4,32,576]{2,1,0:T(8,128)(2,1)S(1)}, bf16[4,32,576]{2,1,0:T(8,128)(2,1)S(1)}, u32[]{:S(2)}, u32[]{:S(2)}) collective-permute-start(bf16[4,32,576]{2,1,0:T(8,128)(2,1)S(1)} %fusion.1), channel_id=1, source_target_pairs={{0,16},{16,0},{1,17},{17,1},{2,18},{18,2},{3,19},{19,3},{4,20},{20... | collective-permute-start | bytes 442376 | tf_op jit(solution)/shard_map/ppermute | solution.py:341
  76.5 15.5 %copy-start.7 = (f32[28,576]{1,0:T(8,128)S(1)}, f32[28,576]{1,0:T(8,128)}, u32[]{:S(2)}) copy-start(f32[28,576]{1,0:T(8,128)} %param.19) | copy-start | bytes 193540
  76.5 15.5 %copy-start.8 = (f32[28,576]{1,0:T(8,128)S(1)}, f32[28,576]{1,0:T(8,128)}, u32[]{:S(2)}) copy-start(f32[28,576]{1,0:T(8,128)} %param.21) | copy-start | bytes 193540
  76.6 15.5 %copy-start.9 = (f32[28,576]{1,0:T(8,128)S(1)}, f32[28,576]{1,0:T(8,128)}, u32[]{:S(2)}) copy-start(f32[28,576]{1,0:T(8,128)} %param.20) | copy-start | bytes 193540
  79.8 10.1 %collective-permute-start.16 = (bf16[32,576]{1,0:T(8,128)(2,1)S(1)}, bf16[32,576]{1,0:T(8,128)(2,1)S(1)}, u32[]{:S(2)}, u32[]{:S(2)}) collective-permute-start(bf16[32,576]{1,0:T(8,128)(2,1)S(1)} %get-tuple-element.50), channel_id=1, source_target_pairs={{0,128},{64,192},{128,0},{192,64},{1,129},{65,193},{129,1},{193,65... | collective-permute-start | bytes 110600 | tf_op jit(solution)/shard_map/ppermute | solution.py:344
  85.8 6.1 %collective-permute-start.17 = (bf16[32,576]{1,0:T(8,128)(2,1)S(1)}, bf16[32,576]{1,0:T(8,128)(2,1)S(1)}, u32[]{:S(2)}, u32[]{:S(2)}) collective-permute-start(bf16[32,576]{1,0:T(8,128)(2,1)S(1)} %get-tuple-element.52), channel_id=1, source_target_pairs={{0,64},{64,128},{128,192},{192,0},{1,65},{65,129},{129,193},{193,1... | collective-permute-start | bytes 110600 | tf_op jit(solution)/shard_map/ppermute | solution.py:344
  86.8 5.2 %collective-permute-start.18 = (bf16[32,576]{1,0:T(8,128)(2,1)S(1)}, bf16[32,576]{1,0:T(8,128)(2,1)S(1)}, u32[]{:S(2)}, u32[]{:S(2)}) collective-permute-start(bf16[32,576]{1,0:T(8,128)(2,1)S(1)} %get-tuple-element.51), channel_id=1, source_target_pairs={{0,192},{64,0},{128,64},{192,128},{1,193},{65,1},{129,65},{193,129... | collective-permute-start | bytes 110600 | tf_op jit(solution)/shard_map/ppermute | solution.py:344

commit v3 on v2

--- a/solution.py
+++ b/solution.py
@@ -17,7 +17,8 @@
 HID = 1024
 DW = 3584
 HALF = 1792
-TILE = 896
+LEAD = 896
+REST = HALF - LEAD
 D = 7168
 KV = 576
 PART = 896
@@ -28,7 +29,7 @@
 PAIR_A = [(0, 1), (1, 0), (2, 3), (3, 2)]
 PAIR_B = [(0, 3), (3, 0), (1, 2), (2, 1)]
 VMEM = 24 * 1024 * 1024
-ADAM_COST = pl.CostEstimate(flops=20_000_000, bytes_accessed=10_000_000, transcendentals=0)
+LONG = pl.CostEstimate(flops=10_000_000_000, bytes_accessed=4_000_000, transcendentals=0)
 FAR_COST = pl.CostEstimate(flops=6_000_000_000, bytes_accessed=4_000_000, transcendentals=0)
 
 
@@ -99,22 +100,26 @@
     copy.wait()
 
 
-def dense_pack_kernel(lay_ref, cot_ref, out_ref, own_ref, cot, sems):
-    j, core = spot_of("zh", "co")
-    last = pltpu.make_async_copy(cot_ref, cot, sems.at[8])
-    last.start()
+def part_copies(lay_ref, ref, side, sems):
+    j = lax.axis_index("zh")
     copies = []
     for n in range(4):
-        for m, (ref, side) in enumerate(((out_ref, 1 - core), (own_ref, core))):
-            start = pl.multiple_of((2 * lax.rem(j + n, 4) + side) * PART, 128)
-            copies.append(
-                pltpu.make_async_copy(
-                    lay_ref.at[:, pl.ds(start, PART)],
-                    ref.at[:, n * PART : (n + 1) * PART],
-                    sems.at[2 * n + m],
-                )
+        start = pl.multiple_of((2 * lax.rem(j + n, 4) + side) * PART, 128)
+        copies.append(
+            pltpu.make_async_copy(
+                lay_ref.at[:, pl.ds(start, PART)],
+                ref.at[:, n * PART : (n + 1) * PART],
+                sems.at[n],
             )
-    for copy in copies[::2] + copies[1::2]:
+        )
+    return copies
+
+
+def dense_pack_kernel(lay_ref, cot_ref, out_ref, cot, sems):
+    last = pltpu.make_async_copy(cot_ref, cot, sems.at[4])
+    last.start()
+    copies = part_copies(lay_ref, out_ref, 1 - lax.axis_index("co"), sems)
+    for copy in copies:
         copy.start()
     last.wait()
     out_ref[:, 4 * PART : 4 * PART + KV] = cot[...].T
@@ -145,68 +150,75 @@
     )(*args)
 
 
-def far_kernel(near_a, near_b, out):
+def far_kernel(near_a, near_b, first, rest):
     for n, near in enumerate((near_a, near_b)):
-        at = n * (HALF + 256)
-        out[:, at : at + HALF] = near[:, :HALF]
-        out[:, at + HALF : at + HALF + 256] = near[:, HALF + 256 :]
-
-
-def products_kernel(cot, own, sib, near_a, near_b, far, a0, a1, b0, b1, keep):
-    for n, (near, sends) in enumerate(((near_a, (a0, a1)), (near_b, (b0, b1)))):
-        at = n * HALF
-        there = n * (HALF + 256)
+        at = n * (LEAD + 256)
+        first[:, at : at + LEAD] = near[:, :LEAD]
+        first[:, at + LEAD : at + LEAD + 256] = near[:, HALF + 256 :]
+        rest[:, n * REST : n * REST + REST] = near[:, LEAD:HALF]
+
+
+def products_kernel(first, cot, own, sib, near_a, near_b, far, columns, to_a, to_b, keep):
+    width = to_a.shape[1]
+    for n, (near, send) in enumerate(((near_a, to_a), (near_b, to_b))):
+        at = n * HALF + first
+        there = n * (columns.shape[1] // 2)
+        factors = n * (LEAD + 256) + LEAD
         h = jnp.concatenate(
             [
                 own[:, n * 256 : n * 256 + 256],
                 sib[:, DW + n * 256 : DW + n * 256 + 256],
                 near[:, HALF : HALF + 256],
-                far[:, there + HALF : there + HALF + 256],
+                far[:, factors : factors + 256],
             ]
         )
         c = jnp.concatenate(
-            [cot[:, at : at + HALF], sib[:, at : at + HALF], near[:, :HALF],
-             far[:, there : there + HALF]]
+            [cot[:, at : at + width], sib[:, at : at + width], near[:, first : first + width],
+             columns[:, there : there + width]]
         )
         result = dot0(h, c)
         keep[n] = result[:SLOT]
-        for i, send in enumerate(sends):
-            send[...] = result[SLOT:, i * TILE : (i + 1) * TILE].astype(bf16)
-
-
-def expert_products(*args):
-    outs = [((SLOT, TILE), bf16)] * 4 + [((2, SLOT, HALF), f32)]
-    return in_vmem(products_kernel, outs, *args)
-
-
-def expert_adam_kernel(keep, a0, a1, b0, b1, master, moment, variance, out):
-    for n, got in enumerate((a0, a1, b0, b1)):
-
-        @pl.when(pl.program_id(0) == n)
-        def _(got=got):
-            gradient = keep[0] + got[...].astype(f32)
-            out[...] = adam_step(master[...], moment[...], variance[...], gradient)
-
-
-def expert_adam(keep, got, master, moment, variance):
-    wide = pl.BlockSpec((SLOT, TILE), lambda n: (0, n))
+        send[...] = result[SLOT:].astype(bf16)
+
+
+def expert_products(first, width, *args):
+    outs = [((SLOT, width), bf16)] * 2 + [((2, SLOT, width), f32)]
+    return in_vmem(functools.partial(products_kernel, first), outs, *args)
+
+
+def expert_adam_kernel(keep0, keep1, a0, a1, b0, b1, master, moment, variance, out):
+    for half, parts in enumerate(((a0, a1), (b0, b1))):
+
+        @pl.when(pl.program_id(0) == half)
+        def _(parts=parts):
+            for at, keep, got in zip(
+                (slice(0, LEAD), slice(LEAD, HALF)), (keep0, keep1), parts
+            ):
+                gradient = keep[0] + got[...].astype(f32)
+                out[:, at] = adam_step(master[:, at], moment[:, at], variance[:, at], gradient)
+
+
+def expert_adam(keeps, got, master, moment, variance):
+    wide = pl.BlockSpec((SLOT, HALF), lambda n: (0, n))
     return pl.pallas_call(
         expert_adam_kernel,
-        grid=(4,),
+        grid=(2,),
         out_shape=jax.ShapeDtypeStruct((SLOT, DW), f32),
         in_specs=[
-            pl.BlockSpec((1, SLOT, TILE), lambda n: (n // 2, 0, n % 2)),
-            *[pl.BlockSpec((SLOT, TILE), lambda n: (0, 0))] * 4,
+            *[pl.BlockSpec((1, SLOT, k.shape[2]), lambda n: (n, 0, 0)) for k in keeps],
+            *[pl.BlockSpec(g.shape, lambda n: (0, 0)) for g in got],
             wide, wide, wide,
         ],
         out_specs=wide,
-        cost_estimate=ADAM_COST,
         compiler_params=pltpu.CompilerParams(vmem_limit_bytes=VMEM),
-    )(keep, *got, master, moment, variance)
-
-
-def order_kernel(order):
+    )(*keeps, *got, master, moment, variance)
+
+
+def order_kernel(lay_ref, order, own_ref, sems):
     core, low, x, y = spot_of("co", "zl", "x", "y")
+    copies = part_copies(lay_ref, own_ref, core, sems)
+    for copy in copies:
+        copy.start()
     place = lax.broadcasted_iota(jnp.int32, (1, 1024), 1)
     first = (place // 256 + x + core * (y - x)) % 4
     second = (place // 64 % 4 + y + core * (x - y)) % 4
@@ -216,6 +228,8 @@
     spot = jnp.where(row < ROWS, spot, -1)
     rows = lax.broadcasted_iota(jnp.int32, (PART, 1024), 0)
     order[...] = jnp.where(rows == spot, 1.0, 0.0).astype(bf16)
+    for copy in copies:
+        copy.wait()
 
 
 def permute_kernel(order, own, to_core, got, *outs):
@@ -239,6 +253,22 @@
         keep[n] = result[:64]
         for k, out in enumerate((up, across, down)):
             out[n] = result[64 * k + 64 : 64 * k + 128].astype(bf16)
+
+
+def after_kernel(*refs):
+    pass
+
+
+def after(values, *others):
+    return pl.pallas_call(
+        after_kernel,
+        out_shape=jax.ShapeDtypeStruct(values.shape, values.dtype),
+        in_specs=[pl.BlockSpec(memory_space=pltpu.VMEM)] * (1 + len(others)),
+        out_specs=pl.BlockSpec(memory_space=pltpu.VMEM),
+        input_output_aliases={0: 0},
+        cost_estimate=LONG,
+        compiler_params=pltpu.CompilerParams(vmem_limit_bytes=VMEM),
+    )(values, *others)
 
 
 def plane_pairs(stage, step):
@@ -276,17 +306,23 @@
     hid, cot = expert_inputs[0], expert_cotangent[0]
     swap = [(0, 1), (1, 0)]
 
-    (order,) = in_vmem(order_kernel, [((PART, 1024), bf16)])
-    to_core, own_part = in_vmem(
+    (to_core,) = in_vmem(
         dense_pack_kernel,
-        [((SLOT, 4224), bf16), ((SLOT, 4 * PART), bf16)],
+        [((SLOT, 4224), bf16)],
         layer_inputs,
         layer_cotangent.T,
-        scratch=[pltpu.VMEM((KV, SLOT), bf16), pltpu.SemaphoreType.DMA((9,))],
+        scratch=[pltpu.VMEM((KV, SLOT), bf16), pltpu.SemaphoreType.DMA((5,))],
         far=(0, 1),
         vmem=56 * 1024 * 1024,
     )
     dense_got = lax.ppermute(to_core, "co", swap)
+    order, own_part = in_vmem(
+        order_kernel,
+        [((PART, 1024), bf16), ((SLOT, 4 * PART), bf16)],
+        layer_inputs,
+        scratch=[pltpu.SemaphoreType.DMA((4,))],
+        far=(0,),
+    )
 
     to_a, to_b, own = in_vmem(
         pack_kernel,
@@ -321,32 +357,39 @@
         dense_product_kernel, [((4, 64, KV), f32)] + [((4, 64, KV), bf16)] * 3, *blocks
     )
 
-    (to_far,) = in_vmem(
-        far_kernel, [((SLOT, DW + 512), bf16)], near_a, near_b, cost=FAR_COST
+    to_far, to_far_rest = in_vmem(
+        far_kernel,
+        [((SLOT, 2 * LEAD + 512), bf16), ((SLOT, 2 * REST), bf16)],
+        near_a,
+        near_b,
+        cost=FAR_COST,
     )
     far = lax.ppermute(tie(to_far, *blocks[1:]), "co", swap)
-    a0, a1, b0, b1, mine_too = expert_products(cot, own, sib, near_a, near_b, far)
-    sums = [
-        lax.ppermute(send, "zh", pairs)
-        for send, pairs in ((a0, PAIR_B), (a1, PAIR_B), (b0, PAIR_A), (b1, PAIR_A))
-    ]
-
-    up, across, down = tie((up, across, down), a0)
+    mine_too = cot, own, sib, near_a, near_b
+    p_a, p_b, keep_p = expert_products(0, LEAD, *mine_too, far, far)
+    p_a, p_b = tie((p_a, p_b), keep)
+    p_a, p_b = lax.ppermute(p_a, "zh", PAIR_B), lax.ppermute(p_b, "zh", PAIR_A)
+    rest = lax.ppermute(to_far_rest, "co", swap)
+    q_a, q_b, keep_q = expert_products(LEAD, REST, *mine_too, far, rest)
+    keep = tie(keep, q_a)
+    q_a, q_b = lax.ppermute(q_a, "zh", PAIR_B), lax.ppermute(q_b, "zh", PAIR_A)
+
+    up, across, down = tie((up, across, down), rest)
     terms = [
         lax.ppermute(block, axes, plane_pairs(1, step))
         for step, block in ((2, across), (1, up), (3, down))
     ]
-
-    line = add(tie(keep, sums[0], sums[2]), *terms).reshape(4, 2, PAD, KV)
+    line = add(after(keep, p_a, p_b), *terms).reshape(4, 2, PAD, KV)
+
     mine = line[:, 0] + lax.ppermute(line[:, 1].astype(bf16), "zl", swap).astype(f32)
     dense_grad = mine[0]
     for step in (2, 1, 3):
-        got = lax.ppermute(mine[step].astype(bf16), "zh", [(i, (i + step) % 4) for i in range(4)])
-        dense_grad = dense_grad + got.astype(f32)
+        term = lax.ppermute(mine[step].astype(bf16), "zh", [(i, (i + step) % 4) for i in range(4)])
+        dense_grad = dense_grad + term.astype(f32)
     dense_updated = adam_step(dense_master, dense_moment, dense_variance, dense_grad[:ROWS])
 
     expert_updated = expert_adam(
-        mine_too, sums, expert_master[0], expert_moment[0], expert_variance[0]
+        (keep_p, tie(keep_q, dense_updated)), (p_a, q_a, p_b, q_b), expert_master[0], expert_moment[0], expert_variance[0]
     )
     return (expert_updated[None], dense_updated)
 

time: 92.9 us -> 84.8 us (0.913)
  starting transfers between devices: 39.5 us -> 34.7 us
  waiting for transfers between devices: 38.4 us -> 34.8 us
    ppermute x4 -> x5, waiting for transfers between devices: 18.4 us -> 4.67 us  [the longest x1 3.03 us: on_device(): lax.ppermute(p_b, 'zh', PAIR_A)]
    ppermute x1, waiting for transfers between devices: 0.01 us -> 8.73 us  [on_device(): lax.ppermute(line[:, 1].astype(bf16), 'zl', swap).astype(f32)]
    ppermute x3, starting transfers between devices: 10.1 us -> 6.84 us  [on_device(): lax.ppermute(mine[step].astype(bf16), 'zh', [(i, (i + step) % 4) for i in...]
    ppermute x3, waiting for transfers between devices: 0.01 us -> 2.48 us  [on_device(): lax.ppermute(block, axes, plane_pairs(1, step))]
    ppermute x4 -> x5, starting transfers between devices: 10.6 us -> 9.16 us  [the longest x1 3.79 us: on_device(): lax.ppermute(p_a, 'zh', PAIR_B)]
    pallas_call x1 -> x2, Pallas kernels: 3.18 us -> 2.81 us  [the longest x1 2.81 us: expert_adam(): pl.pallas_call(expert_adam_kernel, grid=(2,), out_shape=jax.ShapeDtypeStr...]
    pallas_call x8 -> x9, Pallas kernels: 9.12 us -> 9.05 us  [in_vmem(): pl.pallas_call(kernel, out_shape=[jax.ShapeDtypeStruct(shape, dtype) for...]
  transfers between devices with their start and end apart: 19 -> 20, of which waited for: 11 -> 10; matrix products, arithmetic and copies ran while one was open for 0% -> 1% of each run, Pallas kernels for 9% -> 8%
where the time goes in v3:
time: 84.8 us; the launch traced here: 84 us
  waiting for transfers between devices  34.8 us (41%)
  starting transfers between devices  34.7 us (41%)
  Pallas kernels  11.9 us (14%)
  between operations  1.62 us (2%)
  other arithmetic  0.9 us (1%)
    ppermute x1, waiting for transfers between devices, on_device(): near_a = lax.ppermute(to_a, 'zh', PAIR_A)  12.8 us
    pallas_call x9, Pallas kernels, in_vmem(): pl.pallas_call(kernel, out_shape=[jax.ShapeDtypeStruct(shape, dtype) for...  9.05 us
    ppermute x1, waiting for transfers between devices, on_device(): lax.ppermute(line[:, 1].astype(bf16), 'zl', swap).astype(f32)  8.73 us
    ppermute x3, starting transfers between devices, on_device(): lax.ppermute(mine[step].astype(bf16), 'zh', [(i, (i + step) % 4) for i in...  6.84 us
    ppermute x3, starting transfers between devices, on_device(): lax.ppermute(blocks[step], axes, plane_pairs(0, step))  6.35 us
    ppermute x1, starting transfers between devices, on_device(): near_b = lax.ppermute(to_b, 'zh', PAIR_B)  4.48 us
    ppermute x3, starting transfers between devices, on_device(): lax.ppermute(block, axes, plane_pairs(1, step))  4.33 us
    ppermute x1, starting transfers between devices, on_device(): lax.ppermute(p_a, 'zh', PAIR_B)  3.79 us
  transfers between devices with their start and end apart: 20, of which 10 were waited for; matrix products, arithmetic and copies ran while one was open for 1% of the time, Pallas kernels for 8%

profile of v3, /device:TPU:8, one launch (start us, length us, event | category | flops | bytes accessed | tf_op | source)
XLA Modules:
  0.0 84.0 jit_solution(2970404473719064849)
XLA Ops:
  0.7 2.5 %shard_map.126.to_core = bf16[128,4224]{1,0:T(8,128)(2,1)} custom-call(bf16[128,7168]{1,0:T(8,128)(2,1)} %lay_ref.3, bf16[576,128]{1,0:T(8,128)(2,1)} %bitcast.35), custom_call_target="tpu_custom_call" | custom-call | tf_op jit(solution)/shard_map/pallas_call | solution.py:142
  3.1 0.0 copy-start.2
  3.2 0.1 collective-permute-start.3
  4.0 0.2 shard_map.122
  4.2 3.4 %collective-permute-start.1 = (bf16[128,2304]{1,0:T(8,128)(2,1)S(1)}, bf16[128,2304]{1,0:T(8,128)(2,1)S(1)}, u32[]{:S(2)}, u32[]{:S(2)}) collective-permute-start(bf16[128,2304]{1,0:T(8,128)(2,1)S(1)} %get-tuple-element.32), channel_id=1, source_target_pairs={{0,64},{64,0},{128,192},{192,128},{1,65},{65,1},{129,193},{193,129... | collective-permute-start | bytes 1769480 | tf_op jit(solution)/shard_map/ppermute | solution.py:336
  7.6 4.5 %collective-permute-start.2 = (bf16[128,2304]{1,0:T(8,128)(2,1)S(1)}, bf16[128,2304]{1,0:T(8,128)(2,1)S(1)}, u32[]{:S(2)}, u32[]{:S(2)}) collective-permute-start(bf16[128,2304]{1,0:T(8,128)(2,1)S(1)} %get-tuple-element.33), channel_id=1, source_target_pairs={{0,192},{192,0},{64,128},{128,64},{1,193},{193,1},{65,129},{129,65... | collective-permute-start | bytes 1769480 | tf_op jit(solution)/shard_map/ppermute | solution.py:337
  12.0 0.5 shard_map.125
  12.6 0.0 collective-permute-done.3.got
  12.6 2.3 %shard_map.127 = (bf16[256,1664]{1,0:T(8,128)(2,1)S(1)}, bf16[256,1664]{1,0:T(8,128)(2,1)S(1)}, bf16[256,1664]{1,0:T(8,128)(2,1)S(1)}, bf16[256,1664]{1,0:T(8,128)(2,1)S(1)}) custom-call(bf16[896,1024]{1,0:T(8,128)(2,1)S(1)} %get-tuple-element.35.order, bf16[128,3584]{1,0:T(8,128)(2,1)S(1)} %get-tuple-element.36.own, bf16[128,4224]{1,0:T(8,128)(2,1)S(1)} %copy-done.2, ...), custom_call_target="tpu_custom_call" | custom-call | tf_op jit(solution)/shard_map/pallas_call | solution.py:142
  15.0 3.1 %collective-permute-start.4 = (bf16[256,1664]{1,0:T(8,128)(2,1)S(1)}, bf16[256,1664]{1,0:T(8,128)(2,1)S(1)}, u32[]{:S(2)}, u32[]{:S(2)}) collective-permute-start(bf16[256,1664]{1,0:T(8,128)(2,1)S(1)} %get-tuple-element.37), channel_id=1, source_target_pairs={{0,8},{1,9},{2,10},{3,11},{4,12},{5,13},{6,14},{7,15},{8,0},{9,1},... | collective-permute-start | bytes 2555912 | tf_op jit(solution)/shard_map/ppermute | solution.py:354
  18.1 0.6 collective-permute-start.5
  18.7 2.6 %collective-permute-start.6 = (bf16[256,1664]{1,0:T(8,128)(2,1)S(1)}, bf16[256,1664]{1,0:T(8,128)(2,1)S(1)}, u32[]{:S(2)}, u32[]{:S(2)}) collective-permute-start(bf16[256,1664]{1,0:T(8,128)(2,1)S(1)} %get-tuple-element.39), channel_id=1, source_target_pairs={{0,12},{1,13},{2,14},{3,15},{4,0},{5,1},{6,2},{7,3},{8,4},{9,5},{1... | collective-permute-start | bytes 2555912 | tf_op jit(solution)/shard_map/ppermute | solution.py:354
  21.3 0.1 shard_map.123
  21.4 12.8 %collective-permute-done.1.near_a = bf16[128,2304]{1,0:T(8,128)(2,1)S(1)} collective-permute-done((bf16[128,2304]{1,0:T(8,128)(2,1)S(1)}, bf16[128,2304]{1,0:T(8,128)(2,1)S(1)}, u32[]{:S(2)}, u32[]{:S(2)}) %collective-permute-start.1) | collective-permute-done | bytes 589856 | tf_op jit(solution)/shard_map/ppermute | solution.py:336
  34.2 0.0 collective-permute-start
  34.2 3.4 %collective-permute-done.2.near_b = bf16[128,2304]{1,0:T(8,128)(2,1)S(1)} collective-permute-done((bf16[128,2304]{1,0:T(8,128)(2,1)S(1)}, bf16[128,2304]{1,0:T(8,128)(2,1)S(1)}, u32[]{:S(2)}, u32[]{:S(2)}) %collective-permute-start.2) | collective-permute-done | bytes 589856 | tf_op jit(solution)/shard_map/ppermute | solution.py:337
  37.6 0.1 shard_map.124
  37.7 0.0 collective-permute-done.4.b1
  37.7 0.7 collective-permute-done.5.b2
  38.4 0.1 collective-permute-done.6.b3
  38.5 0.5 collective-permute-start.8
  39.0 1.8 %shard_map.130 = (f32[4,64,576]{2,1,0:T(8,128)S(1)}, bf16[4,64,576]{2,1,0:T(8,128)(2,1)S(1)}, bf16[4,64,576]{2,1,0:T(8,128)(2,1)S(1)}, bf16[4,64,576]{2,1,0:T(8,128)(2,1)S(1)}) custom-call(bf16[256,1664]{1,0:T(8,128)(2,1)S(1)} %get-tuple-element.44.b0, bf16[256,1664]{1,0:T(8,128)(2,1)S(1)} %collective-permute-done.4.b1, ...), custom_call_target="tpu_custom_call" | custom-call | tf_op jit(solution)/shard_map/pallas_call | solution.py:142
  40.8 0.0 collective-permute-done.7.far.columns
  40.9 0.7 shard_map.128
  41.6 1.5 %collective-permute-start.10 = (bf16[128,896]{1,0:T(8,128)(2,1)S(1)}, bf16[128,896]{1,0:T(8,128)(2,1)S(1)}, u32[]{:S(2)}, u32[]{:S(2)}) collective-permute-start(bf16[128,896]{1,0:T(8,128)(2,1)S(1)} %get-tuple-element.51), channel_id=1, source_target_pairs={{0,64},{64,0},{128,192},{192,128},{1,65},{65,1},{129,193},{193,129... | collective-permute-start | bytes 688136 | tf_op jit(solution)/shard_map/ppermute | solution.py:371
  43.2 3.8 %collective-permute-start.9 = (bf16[128,896]{1,0:T(8,128)(2,1)S(1)}, bf16[128,896]{1,0:T(8,128)(2,1)S(1)}, u32[]{:S(2)}, u32[]{:S(2)}) collective-permute-start(bf16[128,896]{1,0:T(8,128)(2,1)S(1)} %get-tuple-element.50), channel_id=1, source_target_pairs={{0,192},{192,0},{64,128},{128,64},{1,193},{193,1},{65,129},{129,65... | collective-permute-start | bytes 688136 | tf_op jit(solution)/shard_map/ppermute | solution.py:371
  46.9 0.0 collective-permute-done.8.columns
  46.9 2.3 %collective-permute-start.11 = (bf16[4,64,576]{2,1,0:T(8,128)(2,1)S(1)}, bf16[4,64,576]{2,1,0:T(8,128)(2,1)S(1)}, u32[]{:S(2)}, u32[]{:S(2)}) collective-permute-start(bf16[4,64,576]{2,1,0:T(8,128)(2,1)S(1)} %get-tuple-element.55), channel_id=1, source_target_pairs={{0,2},{1,3},{2,0},{3,1},{4,6},{5,7},{6,4},{7,5},{8,10},{9,11},{10,... | collective-permute-start | bytes 884744 | tf_op jit(solution)/shard_map/ppermute | solution.py:379
  49.3 0.0 collective-permute-start.12
  49.3 2.0 %collective-permute-start.13 = (bf16[4,64,576]{2,1,0:T(8,128)(2,1)S(1)}, bf16[4,64,576]{2,1,0:T(8,128)(2,1)S(1)}, u32[]{:S(2)}, u32[]{:S(2)}) collective-permute-start(bf16[4,64,576]{2,1,0:T(8,128)(2,1)S(1)} %get-tuple-element.57), channel_id=1, source_target_pairs={{0,3},{1,0},{2,1},{3,2},{4,7},{5,4},{6,5},{7,6},{8,11},{9,8},{10,9... | collective-permute-start | bytes 884744 | tf_op jit(solution)/shard_map/ppermute | solution.py:379
  51.3 0.7 shard_map.129
  52.0 3.0 %collective-permute-done.10.refs_2_.b0 = bf16[128,896]{1,0:T(8,128)(2,1)S(1)} collective-permute-done((bf16[128,896]{1,0:T(8,128)(2,1)S(1)}, bf16[128,896]{1,0:T(8,128)(2,1)S(1)}, u32[]{:S(2)}, u32[]{:S(2)}) %collective-permute-start.10) | collective-permute-done | bytes 229408 | tf_op jit(solution)/shard_map/ppermute | solution.py:371
  55.0 1.6 %collective-permute-done.9.refs_1_.a0 = bf16[128,896]{1,0:T(8,128)(2,1)S(1)} collective-permute-done((bf16[128,896]{1,0:T(8,128)(2,1)S(1)}, bf16[128,896]{1,0:T(8,128)(2,1)S(1)}, u32[]{:S(2)}, u32[]{:S(2)}) %collective-permute-start.9) | collective-permute-done | bytes 229408 | tf_op jit(solution)/shard_map/ppermute | solution.py:371
  56.7 0.0 copy-start.3
  56.7 0.0 copy-start.4
  56.7 2.5 %collective-permute-done.12 = bf16[4,64,576]{2,1,0:T(8,128)(2,1)S(1)} collective-permute-done((bf16[4,64,576]{2,1,0:T(8,128)(2,1)S(1)}, bf16[4,64,576]{2,1,0:T(8,128)(2,1)S(1)}, u32[]{:S(2)}, u32[]{:S(2)}) %collective-permute-start.12) | collective-permute-done | bytes 294944 | tf_op jit(solution)/shard_map/ppermute | solution.py:379
  59.2 0.1 convert_add_fusion
  59.4 0.1 collective-permute-start.14
  59.5 1.3 %collective-permute-start.18 = (bf16[128,896]{1,0:T(8,128)(2,1)S(1)}, bf16[128,896]{1,0:T(8,128)(2,1)S(1)}, u32[]{:S(2)}, u32[]{:S(2)}) collective-permute-start(bf16[128,896]{1,0:T(8,128)(2,1)S(1)} %get-tuple-element.46), channel_id=1, source_target_pairs={{0,192},{192,0},{64,128},{128,64},{1,193},{193,1},{65,129},{129,65... | collective-permute-start | bytes 688136 | tf_op jit(solution)/shard_map/ppermute | solution.py:375
  60.8 2.0 %collective-permute-start.19 = (bf16[128,896]{1,0:T(8,128)(2,1)S(1)}, bf16[128,896]{1,0:T(8,128)(2,1)S(1)}, u32[]{:S(2)}, u32[]{:S(2)}) collective-permute-start(bf16[128,896]{1,0:T(8,128)(2,1)S(1)} %get-tuple-element.59), channel_id=1, source_target_pairs={{0,64},{64,0},{128,192},{192,128},{1,65},{65,1},{129,193},{193,129... | collective-permute-start | bytes 688136 | tf_op jit(solution)/shard_map/ppermute | solution.py:375
  62.8 8.7 %collective-permute-done.14 = bf16[4,32,576]{2,1,0:T(8,128)(2,1)S(1)} collective-permute-done((bf16[4,32,576]{2,1,0:T(8,128)(2,1)S(1)}, bf16[4,32,576]{2,1,0:T(8,128)(2,1)S(1)}, u32[]{:S(2)}, u32[]{:S(2)}) %collective-permute-start.14) | collective-permute-done | bytes 147488 | tf_op jit(solution)/shard_map/ppermute | solution.py:384
  71.6 2.7 %collective-permute-start.15 = (bf16[32,576]{1,0:T(8,128)(2,1)S(1)}, bf16[32,576]{1,0:T(8,128)(2,1)S(1)}, u32[]{:S(2)}, u32[]{:S(2)}) collective-permute-start(bf16[32,576]{1,0:T(8,128)(2,1)S(1)} %get-tuple-element.62), channel_id=1, source_target_pairs={{0,128},{64,192},{128,0},{192,64},{1,129},{65,193},{129,1},{193,65... | collective-permute-start | bytes 110600 | tf_op jit(solution)/shard_map/ppermute | solution.py:387
  74.3 0.1 collective-permute-start.16
  74.4 4.0 %collective-permute-start.17 = (bf16[32,576]{1,0:T(8,128)(2,1)S(1)}, bf16[32,576]{1,0:T(8,128)(2,1)S(1)}, u32[]{:S(2)}, u32[]{:S(2)}) collective-permute-start(bf16[32,576]{1,0:T(8,128)(2,1)S(1)} %get-tuple-element.63), channel_id=1, source_target_pairs={{0,192},{64,0},{128,64},{192,128},{1,193},{65,1},{129,65},{193,129... | collective-permute-start | bytes 110600 | tf_op jit(solution)/shard_map/ppermute | solution.py:387
  78.4 1.5 %collective-permute-done.15 = bf16[32,576]{1,0:T(8,128)(2,1)S(1)} collective-permute-done((bf16[32,576]{1,0:T(8,128)(2,1)S(1)}, bf16[32,576]{1,0:T(8,128)(2,1)S(1)}, u32[]{:S(2)}, u32[]{:S(2)}) %collective-permute-start.15) | collective-permute-done | bytes 36896 | tf_op jit(solution)/shard_map/ppermute | solution.py:387
  79.9 0.5 collective-permute-done.16
  80.4 0.7 multiply_subtract_fusion
  81.2 2.8 %shard_map.132 = f32[128,3584]{1,0:T(8,128)} custom-call(f32[2,128,896]{2,1,0:T(8,128)S(1)} %get-tuple-element.41.keep0, f32[2,128,896]{2,1,0:T(8,128)S(1)} %get-tuple-element.58.keep1, bf16[128,896]{1,0:T(8,128)(2,1)S(1)} %collective-permute-done.9.refs_1_.a0, bf16[128,896]{1,0:T(8,128)(2,1)S(1)} %collective-permute-done.18.a1, ...), custom_call_target="tpu_custom_call" | custom-call | tf_op jit(solution)/shard_map/pallas_call | solution.py:203
  (29 shorter events, 0.1 us)
Async XLA Ops:
  0.6 3.3 %copy-start = (bf16[1,128,3584]{2,1,0:T(8,128)(2,1)S(1)}, bf16[1,128,3584]{2,1,0:T(8,128)(2,1)}, u32[]{:S(2)}) copy-start(bf16[1,128,3584]{2,1,0:T(8,128)(2,1)} %param.12) | copy-start | bytes 2752516
  0.6 3.3 %copy-start.6 = (bf16[1,128,1024]{2,1,0:T(8,128)(2,1)S(1)}, bf16[1,128,1024]{2,1,0:T(8,128)(2,1)}, u32[]{:S(2)}) copy-start(bf16[1,128,1024]{2,1,0:T(8,128)(2,1)} %param.11) | copy-start | bytes 786436
  0.7 11.4 %copy-start.1 = (bf16[128,7168]{1,0:T(8,128)(2,1)S(1)}, bf16[128,7168]{1,0:T(8,128)(2,1)}, u32[]{:S(2)}) copy-start(bf16[128,7168]{1,0:T(8,128)(2,1)} %lay_ref.3) | copy-start | bytes 5505028
  3.1 9.5 %copy-start.2 = (bf16[128,4224]{1,0:T(8,128)(2,1)S(1)}, bf16[128,4224]{1,0:T(8,128)(2,1)}, u32[]{:S(2)}) copy-start(bf16[128,4224]{1,0:T(8,128)(2,1)} %shard_map.126.to_core) | copy-start | bytes 3244036
  3.2 9.4 %collective-permute-start.3 = (bf16[128,4224]{1,0:T(8,128)(2,1)}, bf16[128,4224]{1,0:T(8,128)(2,1)S(1)}, u32[]{:S(2)}, u32[]{:S(2)}) collective-permute-start(bf16[128,4224]{1,0:T(8,128)(2,1)} %shard_map.126.to_core), channel_id=1, source_target_pairs={{0,32},{32,0},{1,33},{33,1},{2,34},{34,2},{3,35},{35,3},{4,36},{36... | collective-permute-start | bytes 3244040 | tf_op jit(solution)/shard_map/ppermute | solution.py:318
  4.2 30.0 %collective-permute-start.1 = (bf16[128,2304]{1,0:T(8,128)(2,1)S(1)}, bf16[128,2304]{1,0:T(8,128)(2,1)S(1)}, u32[]{:S(2)}, u32[]{:S(2)}) collective-permute-start(bf16[128,2304]{1,0:T(8,128)(2,1)S(1)} %get-tuple-element.32), channel_id=1, source_target_pairs={{0,64},{64,0},{128,192},{192,128},{1,65},{65,1},{129,193},{193,129... | collective-permute-start | bytes 1769480 | tf_op jit(solution)/shard_map/ppermute | solution.py:336
  7.6 30.1 %collective-permute-start.2 = (bf16[128,2304]{1,0:T(8,128)(2,1)S(1)}, bf16[128,2304]{1,0:T(8,128)(2,1)S(1)}, u32[]{:S(2)}, u32[]{:S(2)}) collective-permute-start(bf16[128,2304]{1,0:T(8,128)(2,1)S(1)} %get-tuple-element.33), channel_id=1, source_target_pairs={{0,192},{192,0},{64,128},{128,64},{1,193},{193,1},{65,129},{129,65... | collective-permute-start | bytes 1769480 | tf_op jit(solution)/shard_map/ppermute | solution.py:337
  15.0 22.8 %collective-permute-start.4 = (bf16[256,1664]{1,0:T(8,128)(2,1)S(1)}, bf16[256,1664]{1,0:T(8,128)(2,1)S(1)}, u32[]{:S(2)}, u32[]{:S(2)}) collective-permute-start(bf16[256,1664]{1,0:T(8,128)(2,1)S(1)} %get-tuple-element.37), channel_id=1, source_target_pairs={{0,8},{1,9},{2,10},{3,11},{4,12},{5,13},{6,14},{7,15},{8,0},{9,1},... | collective-permute-start | bytes 2555912 | tf_op jit(solution)/shard_map/ppermute | solution.py:354
  18.1 20.3 %collective-permute-start.5 = (bf16[256,1664]{1,0:T(8,128)(2,1)S(1)}, bf16[256,1664]{1,0:T(8,128)(2,1)S(1)}, u32[]{:S(2)}, u32[]{:S(2)}) collective-permute-start(bf16[256,1664]{1,0:T(8,128)(2,1)S(1)} %get-tuple-element.38), channel_id=1, source_target_pairs={{0,4},{1,5},{2,6},{3,7},{4,8},{5,9},{6,10},{7,11},{8,12},{9,13},{1... | collective-permute-start | bytes 2555912 | tf_op jit(solution)/shard_map/ppermute | solution.py:354
  18.7 19.8 %collective-permute-start.6 = (bf16[256,1664]{1,0:T(8,128)(2,1)S(1)}, bf16[256,1664]{1,0:T(8,128)(2,1)S(1)}, u32[]{:S(2)}, u32[]{:S(2)}) collective-permute-start(bf16[256,1664]{1,0:T(8,128)(2,1)S(1)} %get-tuple-element.39), channel_id=1, source_target_pairs={{0,12},{1,13},{2,14},{3,15},{4,0},{5,1},{6,2},{7,3},{8,4},{9,5},{1... | collective-permute-start | bytes 2555912 | tf_op jit(solution)/shard_map/ppermute | solution.py:354
  34.2 6.6 %collective-permute-start = (bf16[128,4096]{1,0:T(8,128)(2,1)S(1)}, bf16[128,4096]{1,0:T(8,128)(2,1)S(1)}, u32[]{:S(2)}, u32[]{:S(2)}) collective-permute-start(bf16[128,4096]{1,0:T(8,128)(2,1)S(1)} %shard_map.123), channel_id=1, source_target_pairs={{0,32},{32,0},{1,33},{33,1},{2,34},{34,2},{3,35},{35,3},{4,36},{36... | collective-permute-start | bytes 3145736 | tf_op jit(solution)/shard_map/ppermute | solution.py:347
  38.5 2.4 %collective-permute-start.7 = (bf16[128,2304]{1,0:T(8,128)(2,1)S(1)}, bf16[128,2304]{1,0:T(8,128)(2,1)S(1)}, u32[]{:S(2)}, u32[]{:S(2)}) collective-permute-start(bf16[128,2304]{1,0:T(8,128)(2,1)S(1)} %get-tuple-element.40), channel_id=1, source_target_pairs={{0,32},{32,0},{1,33},{33,1},{2,34},{34,2},{3,35},{35,3},{4,36},{36... | collective-permute-start | bytes 1769480 | tf_op jit(solution)/shard_map/ppermute | solution.py:367
  38.5 8.4 %collective-permute-start.8 = (bf16[128,1792]{1,0:T(8,128)(2,1)S(1)}, bf16[128,1792]{1,0:T(8,128)(2,1)S(1)}, u32[]{:S(2)}, u32[]{:S(2)}) collective-permute-start(bf16[128,1792]{1,0:T(8,128)(2,1)S(1)} %get-tuple-element.42), channel_id=1, source_target_pairs={{0,32},{32,0},{1,33},{33,1},{2,34},{34,2},{3,35},{35,3},{4,36},{36... | collective-permute-start | bytes 1376264 | tf_op jit(solution)/shard_map/ppermute | solution.py:372
  41.6 13.4 %collective-permute-start.10 = (bf16[128,896]{1,0:T(8,128)(2,1)S(1)}, bf16[128,896]{1,0:T(8,128)(2,1)S(1)}, u32[]{:S(2)}, u32[]{:S(2)}) collective-permute-start(bf16[128,896]{1,0:T(8,128)(2,1)S(1)} %get-tuple-element.51), channel_id=1, source_target_pairs={{0,64},{64,0},{128,192},{192,128},{1,65},{65,1},{129,193},{193,129... | collective-permute-start | bytes 688136 | tf_op jit(solution)/shard_map/ppermute | solution.py:371
  43.2 13.5 %collective-permute-start.9 = (bf16[128,896]{1,0:T(8,128)(2,1)S(1)}, bf16[128,896]{1,0:T(8,128)(2,1)S(1)}, u32[]{:S(2)}, u32[]{:S(2)}) collective-permute-start(bf16[128,896]{1,0:T(8,128)(2,1)S(1)} %get-tuple-element.50), channel_id=1, source_target_pairs={{0,192},{192,0},{64,128},{128,64},{1,193},{193,1},{65,129},{129,65... | collective-permute-start | bytes 688136 | tf_op jit(solution)/shard_map/ppermute | solution.py:371
  46.9 9.8 %collective-permute-start.11 = (bf16[4,64,576]{2,1,0:T(8,128)(2,1)S(1)}, bf16[4,64,576]{2,1,0:T(8,128)(2,1)S(1)}, u32[]{:S(2)}, u32[]{:S(2)}) collective-permute-start(bf16[4,64,576]{2,1,0:T(8,128)(2,1)S(1)} %get-tuple-element.55), channel_id=1, source_target_pairs={{0,2},{1,3},{2,0},{3,1},{4,6},{5,7},{6,4},{7,5},{8,10},{9,11},{10,... | collective-permute-start | bytes 884744 | tf_op jit(solution)/shard_map/ppermute | solution.py:379
  49.3 10.0 %collective-permute-start.12 = (bf16[4,64,576]{2,1,0:T(8,128)(2,1)S(1)}, bf16[4,64,576]{2,1,0:T(8,128)(2,1)S(1)}, u32[]{:S(2)}, u32[]{:S(2)}) collective-permute-start(bf16[4,64,576]{2,1,0:T(8,128)(2,1)S(1)} %get-tuple-element.56), channel_id=1, source_target_pairs={{0,1},{1,2},{2,3},{3,0},{4,5},{5,6},{6,7},{7,4},{8,9},{9,10},{10,1... | collective-permute-start | bytes 884744 | tf_op jit(solution)/shard_map/ppermute | solution.py:379
  49.3 10.0 %collective-permute-start.13 = (bf16[4,64,576]{2,1,0:T(8,128)(2,1)S(1)}, bf16[4,64,576]{2,1,0:T(8,128)(2,1)S(1)}, u32[]{:S(2)}, u32[]{:S(2)}) collective-permute-start(bf16[4,64,576]{2,1,0:T(8,128)(2,1)S(1)} %get-tuple-element.57), channel_id=1, source_target_pairs={{0,3},{1,0},{2,1},{3,2},{4,7},{5,4},{6,5},{7,6},{8,11},{9,8},{10,9... | collective-permute-start | bytes 884744 | tf_op jit(solution)/shard_map/ppermute | solution.py:379
  56.7 24.5 %copy-start.5 = (f32[1,128,3584]{2,1,0:T(8,128)S(1)}, f32[1,128,3584]{2,1,0:T(8,128)}, u32[]{:S(2)}) copy-start(f32[1,128,3584]{2,1,0:T(8,128)} %param.16) | copy-start | bytes 5505028
  56.7 23.7 %copy-start.7 = (f32[28,576]{1,0:T(8,128)S(1)}, f32[28,576]{1,0:T(8,128)}, u32[]{:S(2)}) copy-start(f32[28,576]{1,0:T(8,128)} %param.19) | copy-start | bytes 193540
  56.7 23.7 %copy-start.8 = (f32[28,576]{1,0:T(8,128)S(1)}, f32[28,576]{1,0:T(8,128)}, u32[]{:S(2)}) copy-start(f32[28,576]{1,0:T(8,128)} %param.21) | copy-start | bytes 193540
  56.7 23.7 %copy-start.9 = (f32[28,576]{1,0:T(8,128)S(1)}, f32[28,576]{1,0:T(8,128)}, u32[]{:S(2)}) copy-start(f32[28,576]{1,0:T(8,128)} %param.20) | copy-start | bytes 193540
  56.7 24.5 %copy-start.3 = (f32[1,128,3584]{2,1,0:T(8,128)S(1)}, f32[1,128,3584]{2,1,0:T(8,128)}, u32[]{:S(2)}) copy-start(f32[1,128,3584]{2,1,0:T(8,128)} %param.14) | copy-start | bytes 5505028
  56.7 24.5 %copy-start.4 = (f32[1,128,3584]{2,1,0:T(8,128)S(1)}, f32[1,128,3584]{2,1,0:T(8,128)}, u32[]{:S(2)}) copy-start(f32[1,128,3584]{2,1,0:T(8,128)} %param.15) | copy-start | bytes 5505028
  59.4 12.1 %collective-permute-start.14 = (bf16[4,32,576]{2,1,0:T(8,128)(2,1)S(1)}, bf16[4,32,576]{2,1,0:T(8,128)(2,1)S(1)}, u32[]{:S(2)}, u32[]{:S(2)}) collective-permute-start(bf16[4,32,576]{2,1,0:T(8,128)(2,1)S(1)} %fusion.1), channel_id=1, source_target_pairs={{0,16},{16,0},{1,17},{17,1},{2,18},{18,2},{3,19},{19,3},{4,20},{20... | collective-permute-start | bytes 442376 | tf_op jit(solution)/shard_map/ppermute | solution.py:384
  59.5 21.7 %collective-permute-start.18 = (bf16[128,896]{1,0:T(8,128)(2,1)S(1)}, bf16[128,896]{1,0:T(8,128)(2,1)S(1)}, u32[]{:S(2)}, u32[]{:S(2)}) collective-permute-start(bf16[128,896]{1,0:T(8,128)(2,1)S(1)} %get-tuple-element.46), channel_id=1, source_target_pairs={{0,192},{192,0},{64,128},{128,64},{1,193},{193,1},{65,129},{129,65... | collective-permute-start | bytes 688136 | tf_op jit(solution)/shard_map/ppermute | solution.py:375
  60.8 20.3 %collective-permute-start.19 = (bf16[128,896]{1,0:T(8,128)(2,1)S(1)}, bf16[128,896]{1,0:T(8,128)(2,1)S(1)}, u32[]{:S(2)}, u32[]{:S(2)}) collective-permute-start(bf16[128,896]{1,0:T(8,128)(2,1)S(1)} %get-tuple-element.59), channel_id=1, source_target_pairs={{0,64},{64,0},{128,192},{192,128},{1,65},{65,1},{129,193},{193,129... | collective-permute-start | bytes 688136 | tf_op jit(solution)/shard_map/ppermute | solution.py:375
  71.6 8.3 %collective-permute-start.15 = (bf16[32,576]{1,0:T(8,128)(2,1)S(1)}, bf16[32,576]{1,0:T(8,128)(2,1)S(1)}, u32[]{:S(2)}, u32[]{:S(2)}) collective-permute-start(bf16[32,576]{1,0:T(8,128)(2,1)S(1)} %get-tuple-element.62), channel_id=1, source_target_pairs={{0,128},{64,192},{128,0},{192,64},{1,129},{65,193},{129,1},{193,65... | collective-permute-start | bytes 110600 | tf_op jit(solution)/shard_map/ppermute | solution.py:387
  74.3 6.1 %collective-permute-start.16 = (bf16[32,576]{1,0:T(8,128)(2,1)S(1)}, bf16[32,576]{1,0:T(8,128)(2,1)S(1)}, u32[]{:S(2)}, u32[]{:S(2)}) collective-permute-start(bf16[32,576]{1,0:T(8,128)(2,1)S(1)} %get-tuple-element.64), channel_id=1, source_target_pairs={{0,64},{64,128},{128,192},{192,0},{1,65},{65,129},{129,193},{193,1... | collective-permute-start | bytes 110600 | tf_op jit(solution)/shard_map/ppermute | solution.py:387
  74.4 6.0 %collective-permute-start.17 = (bf16[32,576]{1,0:T(8,128)(2,1)S(1)}, bf16[32,576]{1,0:T(8,128)(2,1)S(1)}, u32[]{:S(2)}, u32[]{:S(2)}) collective-permute-start(bf16[32,576]{1,0:T(8,128)(2,1)S(1)} %get-tuple-element.63), channel_id=1, source_target_pairs={{0,192},{64,0},{128,64},{192,128},{1,193},{65,1},{129,65},{193,129... | collective-permute-start | bytes 110600 | tf_op jit(solution)/shard_map/ppermute | solution.py:387

commit v4 on v3

--- a/solution.py
+++ b/solution.py
@@ -17,7 +17,7 @@
 HID = 1024
 DW = 3584
 HALF = 1792
-LEAD = 896
+LEAD = 1152
 REST = HALF - LEAD
 D = 7168
 KV = 576
@@ -186,7 +186,7 @@
     return in_vmem(functools.partial(products_kernel, first), outs, *args)
 
 
-def expert_adam_kernel(keep0, keep1, a0, a1, b0, b1, master, moment, variance, out):
+def expert_adam_kernel(keep0, keep1, a0, a1, b0, b1, master, moment, variance, _, out):
     for half, parts in enumerate(((a0, a1), (b0, b1))):
 
         @pl.when(pl.program_id(0) == half)
@@ -198,7 +198,7 @@
                 out[:, at] = adam_step(master[:, at], moment[:, at], variance[:, at], gradient)
 
 
-def expert_adam(keeps, got, master, moment, variance):
+def expert_adam(keeps, got, master, moment, variance, last):
     wide = pl.BlockSpec((SLOT, HALF), lambda n: (0, n))
     return pl.pallas_call(
         expert_adam_kernel,
@@ -207,11 +207,12 @@
         in_specs=[
             *[pl.BlockSpec((1, SLOT, k.shape[2]), lambda n: (n, 0, 0)) for k in keeps],
             *[pl.BlockSpec(g.shape, lambda n: (0, 0)) for g in got],
-            wide, wide, wide,
+            wide, wide, wide, pl.BlockSpec(last.shape, lambda n: (0, 0)),
         ],
         out_specs=wide,
+        cost_estimate=LONG,
         compiler_params=pltpu.CompilerParams(vmem_limit_bytes=VMEM),
-    )(*keeps, *got, master, moment, variance)
+    )(*keeps, *got, master, moment, variance, last)
 
 
 def order_kernel(lay_ref, order, own_ref, sems):
@@ -381,16 +382,18 @@
     ]
     line = add(after(keep, p_a, p_b), *terms).reshape(4, 2, PAD, KV)
 
-    mine = line[:, 0] + lax.ppermute(line[:, 1].astype(bf16), "zl", swap).astype(f32)
-    dense_grad = mine[0]
+    mine = line[0]
     for step in (2, 1, 3):
-        term = lax.ppermute(mine[step].astype(bf16), "zh", [(i, (i + step) % 4) for i in range(4)])
-        dense_grad = dense_grad + term.astype(f32)
+        term = lax.ppermute(line[step].astype(bf16), "zh", [(i, (i + step) % 4) for i in range(4)])
+        mine = mine + term.astype(f32)
+    theirs = mine[1].astype(bf16)
+    dense_grad = mine[0] + lax.ppermute(theirs, "zl", swap).astype(f32)
     dense_updated = adam_step(dense_master, dense_moment, dense_variance, dense_grad[:ROWS])
 
-    expert_updated = expert_adam(
-        (keep_p, tie(keep_q, dense_updated)), (p_a, q_a, p_b, q_b), expert_master[0], expert_moment[0], expert_variance[0]
-    )
+    last = lax.ppermute(q_a[:16, :128] + q_b[:16, :128], "co", swap)
+    state = expert_master[0], expert_moment[0], expert_variance[0]
+    keeps = keep_p, tie(keep_q, theirs)
+    expert_updated = expert_adam(keeps, (p_a, q_a, p_b, q_b), *state, last)
     return (expert_updated[None], dense_updated)
 
 

time: 84.8 us -> 84.3 us (level)
  waiting for transfers between devices: 34.8 us -> 29.8 us
  starting transfers between devices: 34.7 us -> 39.5 us
    ppermute x4 -> x5, waiting for transfers between devices: 10.7 us -> 4.03 us  [the longest x3 2.93 us: on_device(): lax.ppermute(line[step].astype(bf16), 'zh', [(i, (i + step) % 4) for i in...]
    ppermute x4 -> x5, starting transfers between devices: 6.93 us -> 11.1 us  [the longest x3 11 us: on_device(): lax.ppermute(line[step].astype(bf16), 'zh', [(i, (i + step) % 4) for i in...]
    ppermute x1, waiting for transfers between devices: 3.03 us -> 6.05 us  [on_device(): lax.ppermute(p_b, 'zh', PAIR_A)]
    ppermute x1, waiting for transfers between devices: 0.01 us -> 2.74 us  [on_device(): lax.ppermute(q_b, 'zh', PAIR_A)]
    ppermute x1, starting transfers between devices: 1.34 us -> 3.93 us  [on_device(): lax.ppermute(q_a, 'zh', PAIR_B)]
    ppermute x3, waiting for transfers between devices: 2.48 us -> 0.01 us  [on_device(): lax.ppermute(block, axes, plane_pairs(1, step))]
    ppermute x1, starting transfers between devices: 1.98 us -> 0.01 us  [on_device(): lax.ppermute(q_b, 'zh', PAIR_A)]
    ppermute x1, waiting for transfers between devices: 1.64 us -> 0.01 us  [on_device(): lax.ppermute(p_a, 'zh', PAIR_B)]
  transfers between devices with their start and end apart: 20 -> 21, of which waited for: 10 -> 8; matrix products, arithmetic and copies ran while one was open for 1% -> 0% of each run, Pallas kernels for 8% -> 11%
where the time goes in v4:
time: 84.3 us; the launch traced here: 83.9 us
  starting transfers between devices  39.5 us (47%)
  waiting for transfers between devices  29.8 us (35%)
  Pallas kernels  11.9 us (14%)
  between operations  1.67 us (2%)
  other arithmetic  0.9 us (1%)
    ppermute x1, waiting for transfers between devices, on_device(): near_a = lax.ppermute(to_a, 'zh', PAIR_A)  12.8 us
    ppermute x3, starting transfers between devices, on_device(): lax.ppermute(line[step].astype(bf16), 'zh', [(i, (i + step) % 4) for i in...  11 us
    pallas_call x9, Pallas kernels, in_vmem(): pl.pallas_call(kernel, out_shape=[jax.ShapeDtypeStruct(shape, dtype) for...  9.05 us
    ppermute x3, starting transfers between devices, on_device(): lax.ppermute(blocks[step], axes, plane_pairs(0, step))  6.35 us
    ppermute x1, waiting for transfers between devices, on_device(): lax.ppermute(p_b, 'zh', PAIR_A)  6.05 us
    ppermute x1, starting transfers between devices, on_device(): near_b = lax.ppermute(to_b, 'zh', PAIR_B)  4.48 us
    ppermute x3, starting transfers between devices, on_device(): lax.ppermute(block, axes, plane_pairs(1, step))  4.33 us
    ppermute x1, starting transfers between devices, on_device(): lax.ppermute(q_a, 'zh', PAIR_B)  3.93 us
  transfers between devices with their start and end apart: 21, of which 8 were waited for; matrix products, arithmetic and copies ran while one was open for 0% of the time, Pallas kernels for 11%

profile of v4, /device:TPU:8, one launch (start us, length us, event | category | flops | bytes accessed | tf_op | source)
XLA Modules:
  0.0 83.9 jit_solution(18242959833914580530)
XLA Ops:
  0.7 2.5 %shard_map.126.to_core = bf16[128,4224]{1,0:T(8,128)(2,1)} custom-call(bf16[128,7168]{1,0:T(8,128)(2,1)} %lay_ref.3, bf16[576,128]{1,0:T(8,128)(2,1)} %bitcast.25), custom_call_target="tpu_custom_call" | custom-call | tf_op jit(solution)/shard_map/pallas_call | solution.py:142
  3.1 0.0 copy-start.2
  3.2 0.1 collective-permute-start.3
  4.0 0.2 shard_map.122
  4.2 3.4 %collective-permute-start.1 = (bf16[128,2304]{1,0:T(8,128)(2,1)S(1)}, bf16[128,2304]{1,0:T(8,128)(2,1)S(1)}, u32[]{:S(2)}, u32[]{:S(2)}) collective-permute-start(bf16[128,2304]{1,0:T(8,128)(2,1)S(1)} %get-tuple-element.32), channel_id=1, source_target_pairs={{0,64},{64,0},{128,192},{192,128},{1,65},{65,1},{129,193},{193,129... | collective-permute-start | bytes 1769480 | tf_op jit(solution)/shard_map/ppermute | solution.py:337
  7.6 4.5 %collective-permute-start.2 = (bf16[128,2304]{1,0:T(8,128)(2,1)S(1)}, bf16[128,2304]{1,0:T(8,128)(2,1)S(1)}, u32[]{:S(2)}, u32[]{:S(2)}) collective-permute-start(bf16[128,2304]{1,0:T(8,128)(2,1)S(1)} %get-tuple-element.33), channel_id=1, source_target_pairs={{0,192},{192,0},{64,128},{128,64},{1,193},{193,1},{65,129},{129,65... | collective-permute-start | bytes 1769480 | tf_op jit(solution)/shard_map/ppermute | solution.py:338
  12.0 0.5 shard_map.125
  12.6 0.0 collective-permute-done.3.got
  12.6 2.3 %shard_map.127 = (bf16[256,1664]{1,0:T(8,128)(2,1)S(1)}, bf16[256,1664]{1,0:T(8,128)(2,1)S(1)}, bf16[256,1664]{1,0:T(8,128)(2,1)S(1)}, bf16[256,1664]{1,0:T(8,128)(2,1)S(1)}) custom-call(bf16[896,1024]{1,0:T(8,128)(2,1)S(1)} %get-tuple-element.35.order, bf16[128,3584]{1,0:T(8,128)(2,1)S(1)} %get-tuple-element.36.own, bf16[128,4224]{1,0:T(8,128)(2,1)S(1)} %copy-done.2, ...), custom_call_target="tpu_custom_call" | custom-call | tf_op jit(solution)/shard_map/pallas_call | solution.py:142
  15.0 3.1 %collective-permute-start.4 = (bf16[256,1664]{1,0:T(8,128)(2,1)S(1)}, bf16[256,1664]{1,0:T(8,128)(2,1)S(1)}, u32[]{:S(2)}, u32[]{:S(2)}) collective-permute-start(bf16[256,1664]{1,0:T(8,128)(2,1)S(1)} %get-tuple-element.37), channel_id=1, source_target_pairs={{0,8},{1,9},{2,10},{3,11},{4,12},{5,13},{6,14},{7,15},{8,0},{9,1},... | collective-permute-start | bytes 2555912 | tf_op jit(solution)/shard_map/ppermute | solution.py:355
  18.1 0.6 collective-permute-start.5
  18.7 2.6 %collective-permute-start.6 = (bf16[256,1664]{1,0:T(8,128)(2,1)S(1)}, bf16[256,1664]{1,0:T(8,128)(2,1)S(1)}, u32[]{:S(2)}, u32[]{:S(2)}) collective-permute-start(bf16[256,1664]{1,0:T(8,128)(2,1)S(1)} %get-tuple-element.39), channel_id=1, source_target_pairs={{0,12},{1,13},{2,14},{3,15},{4,0},{5,1},{6,2},{7,3},{8,4},{9,5},{1... | collective-permute-start | bytes 2555912 | tf_op jit(solution)/shard_map/ppermute | solution.py:355
  21.3 0.1 shard_map.123
  21.4 12.8 %collective-permute-done.1.near_a = bf16[128,2304]{1,0:T(8,128)(2,1)S(1)} collective-permute-done((bf16[128,2304]{1,0:T(8,128)(2,1)S(1)}, bf16[128,2304]{1,0:T(8,128)(2,1)S(1)}, u32[]{:S(2)}, u32[]{:S(2)}) %collective-permute-start.1) | collective-permute-done | bytes 589856 | tf_op jit(solution)/shard_map/ppermute | solution.py:337
  34.2 3.4 %collective-permute-done.2.near_b = bf16[128,2304]{1,0:T(8,128)(2,1)S(1)} collective-permute-done((bf16[128,2304]{1,0:T(8,128)(2,1)S(1)}, bf16[128,2304]{1,0:T(8,128)(2,1)S(1)}, u32[]{:S(2)}, u32[]{:S(2)}) %collective-permute-start.2) | collective-permute-done | bytes 589856 | tf_op jit(solution)/shard_map/ppermute | solution.py:338
  37.6 0.1 shard_map.124
  37.7 0.7 collective-permute-done.5.b2
  38.4 0.1 collective-permute-done.6.b3
  38.5 0.5 collective-permute-start.8
  39.0 1.8 %shard_map.130 = (f32[4,64,576]{2,1,0:T(8,128)S(1)}, bf16[4,64,576]{2,1,0:T(8,128)(2,1)S(1)}, bf16[4,64,576]{2,1,0:T(8,128)(2,1)S(1)}, bf16[4,64,576]{2,1,0:T(8,128)(2,1)S(1)}) custom-call(bf16[256,1664]{1,0:T(8,128)(2,1)S(1)} %get-tuple-element.44.b0, bf16[256,1664]{1,0:T(8,128)(2,1)S(1)} %collective-permute-done.4.b1, ...), custom_call_target="tpu_custom_call" | custom-call | tf_op jit(solution)/shard_map/pallas_call | solution.py:142
  40.8 0.0 collective-permute-done.sib
  40.8 0.0 collective-permute-done.7.far.columns
  40.9 0.9 %shard_map.128 = (bf16[128,1152]{1,0:T(8,128)(2,1)S(1)}, bf16[128,1152]{1,0:T(8,128)(2,1)S(1)}, f32[2,128,1152]{2,1,0:T(8,128)S(1)}) custom-call(bf16[128,3584]{1,0:T(8,128)(2,1)S(1)} %bitcast.17, bf16[128,512]{1,0:T(8,128)(2,1)S(1)} %get-tuple-element.31.own, bf16[128,4096]{1,0:T(8,128)(2,1)S(1)} %collective-permute-done.sib, ...), custom_call_target="tpu_custom_call" | custom-call | tf_op jit(solution)/shard_map/pallas_call | solution.py:142
  41.7 1.5 %collective-permute-start.10 = (bf16[128,1152]{1,0:T(8,128)(2,1)S(1)}, bf16[128,1152]{1,0:T(8,128)(2,1)S(1)}, u32[]{:S(2)}, u32[]{:S(2)}) collective-permute-start(bf16[128,1152]{1,0:T(8,128)(2,1)S(1)} %get-tuple-element.51), channel_id=1, source_target_pairs={{0,64},{64,0},{128,192},{192,128},{1,65},{65,1},{129,193},{193,129... | collective-permute-start | bytes 884744 | tf_op jit(solution)/shard_map/ppermute | solution.py:372
  43.3 3.8 %collective-permute-start.9 = (bf16[128,1152]{1,0:T(8,128)(2,1)S(1)}, bf16[128,1152]{1,0:T(8,128)(2,1)S(1)}, u32[]{:S(2)}, u32[]{:S(2)}) collective-permute-start(bf16[128,1152]{1,0:T(8,128)(2,1)S(1)} %get-tuple-element.50), channel_id=1, source_target_pairs={{0,192},{192,0},{64,128},{128,64},{1,193},{193,1},{65,129},{129,65... | collective-permute-start | bytes 884744 | tf_op jit(solution)/shard_map/ppermute | solution.py:372
  47.1 2.3 %collective-permute-start.11 = (bf16[4,64,576]{2,1,0:T(8,128)(2,1)S(1)}, bf16[4,64,576]{2,1,0:T(8,128)(2,1)S(1)}, u32[]{:S(2)}, u32[]{:S(2)}) collective-permute-start(bf16[4,64,576]{2,1,0:T(8,128)(2,1)S(1)} %get-tuple-element.55), channel_id=1, source_target_pairs={{0,2},{1,3},{2,0},{3,1},{4,6},{5,7},{6,4},{7,5},{8,10},{9,11},{10,... | collective-permute-start | bytes 884744 | tf_op jit(solution)/shard_map/ppermute | solution.py:380
  49.4 0.0 collective-permute-start.12
  49.4 2.0 %collective-permute-start.13 = (bf16[4,64,576]{2,1,0:T(8,128)(2,1)S(1)}, bf16[4,64,576]{2,1,0:T(8,128)(2,1)S(1)}, u32[]{:S(2)}, u32[]{:S(2)}) collective-permute-start(bf16[4,64,576]{2,1,0:T(8,128)(2,1)S(1)} %get-tuple-element.57), channel_id=1, source_target_pairs={{0,3},{1,0},{2,1},{3,2},{4,7},{5,4},{6,5},{7,6},{8,11},{9,8},{10,9... | collective-permute-start | bytes 884744 | tf_op jit(solution)/shard_map/ppermute | solution.py:380
  51.4 0.6 shard_map.129
  52.0 6.0 %collective-permute-done.10.refs_2_.b0 = bf16[128,1152]{1,0:T(8,128)(2,1)S(1)} collective-permute-done((bf16[128,1152]{1,0:T(8,128)(2,1)S(1)}, bf16[128,1152]{1,0:T(8,128)(2,1)S(1)}, u32[]{:S(2)}, u32[]{:S(2)}) %collective-permute-start.10) | collective-permute-done | bytes 294944 | tf_op jit(solution)/shard_map/ppermute | solution.py:372
  58.1 3.9 %collective-permute-start.17 = (bf16[128,640]{1,0:T(8,128)(2,1)S(1)}, bf16[128,640]{1,0:T(8,128)(2,1)S(1)}, u32[]{:S(2)}, u32[]{:S(2)}) collective-permute-start(bf16[128,640]{1,0:T(8,128)(2,1)S(1)} %get-tuple-element.46), channel_id=1, source_target_pairs={{0,192},{192,0},{64,128},{128,64},{1,193},{193,1},{65,129},{129,65... | collective-permute-start | bytes 491528 | tf_op jit(solution)/shard_map/ppermute | solution.py:376
  62.0 0.0 copy-start.4
  62.0 0.0 copy-start.5
  62.1 0.0 collective-permute-done.12
  62.1 0.1 fusion.7
  62.3 6.9 %collective-permute-start.14 = (bf16[2,32,576]{2,1,0:T(8,128)(2,1)S(1)}, bf16[2,32,576]{2,1,0:T(8,128)(2,1)S(1)}, u32[]{:S(2)}, u32[]{:S(2)}) collective-permute-start(bf16[2,32,576]{2,1,0:T(8,128)(2,1)S(1)} %bitcast.28), channel_id=1, source_target_pairs={{0,128},{64,192},{128,0},{192,64},{1,129},{65,193},{129,1},{193,65... | collective-permute-start | bytes 221192 | tf_op jit(solution)/shard_map/ppermute | solution.py:387
  69.2 0.0 collective-permute-start.15
  69.2 4.1 %collective-permute-start.16 = (bf16[2,32,576]{2,1,0:T(8,128)(2,1)S(1)}, bf16[2,32,576]{2,1,0:T(8,128)(2,1)S(1)}, u32[]{:S(2)}, u32[]{:S(2)}) collective-permute-start(bf16[2,32,576]{2,1,0:T(8,128)(2,1)S(1)} %bitcast.26), channel_id=1, source_target_pairs={{0,192},{64,0},{128,64},{192,128},{1,193},{65,1},{129,65},{193,129... | collective-permute-start | bytes 221192 | tf_op jit(solution)/shard_map/ppermute | solution.py:387
  73.3 0.0 collective-permute-done.17.a1
  73.3 2.7 %collective-permute-done.18.b1 = bf16[128,640]{1,0:T(8,128)(2,1)S(1)} collective-permute-done((bf16[128,640]{1,0:T(8,128)(2,1)S(1)}, bf16[128,640]{1,0:T(8,128)(2,1)S(1)}, u32[]{:S(2)}, u32[]{:S(2)}) %collective-permute-start.18) | collective-permute-done | bytes 163872 | tf_op jit(solution)/shard_map/ppermute | solution.py:376
  76.1 2.9 %collective-permute-done.14 = bf16[2,32,576]{2,1,0:T(8,128)(2,1)S(1)} collective-permute-done((bf16[2,32,576]{2,1,0:T(8,128)(2,1)S(1)}, bf16[2,32,576]{2,1,0:T(8,128)(2,1)S(1)}, u32[]{:S(2)}, u32[]{:S(2)}) %collective-permute-start.14) | collective-permute-done | bytes 73760 | tf_op jit(solution)/shard_map/ppermute | solution.py:387
  79.1 0.1 collective-permute-start.20
  79.2 0.0 copy-start.7
  79.2 0.0 copy-start.8
  79.2 0.0 copy-start.9
  79.2 2.8 %shard_map.132 = f32[128,3584]{1,0:T(8,128)} custom-call(f32[2,128,1152]{2,1,0:T(8,128)S(1)} %get-tuple-element.41.keep0, f32[2,128,640]{2,1,0:T(8,128)S(1)} %get-tuple-element.58.keep1, bf16[128,1152]{1,0:T(8,128)(2,1)S(1)} %collective-permute-done.9.refs_1_.a0, bf16[128,640]{1,0:T(8,128)(2,1)S(1)} %collective-permute-done.17.a1, ...), custom_call_target="tpu_custom_call" | custom-call | flops 10000000000 | bytes 4000000 | tf_op jit(solution)/shard_map/pallas_call | solution.py:203
  82.1 1.1 %collective-permute-done.20 = bf16[32,576]{1,0:T(8,128)(2,1)S(1)} collective-permute-done((bf16[32,576]{1,0:T(8,128)(2,1)S(1)}, bf16[32,576]{1,0:T(8,128)(2,1)S(1)}, u32[]{:S(2)}, u32[]{:S(2)}) %collective-permute-start.20) | collective-permute-done | bytes 36896 | tf_op jit(solution)/shard_map/ppermute | solution.py:390
  83.2 0.7 multiply_subtract_fusion
  (33 shorter events, 0.2 us)
Async XLA Ops:
  0.6 3.3 %copy-start = (bf16[1,128,3584]{2,1,0:T(8,128)(2,1)S(1)}, bf16[1,128,3584]{2,1,0:T(8,128)(2,1)}, u32[]{:S(2)}) copy-start(bf16[1,128,3584]{2,1,0:T(8,128)(2,1)} %param.12) | copy-start | bytes 2752516
  0.6 3.3 %copy-start.3 = (bf16[1,128,1024]{2,1,0:T(8,128)(2,1)S(1)}, bf16[1,128,1024]{2,1,0:T(8,128)(2,1)}, u32[]{:S(2)}) copy-start(bf16[1,128,1024]{2,1,0:T(8,128)(2,1)} %param.11) | copy-start | bytes 786436
  0.7 11.4 %copy-start.1 = (bf16[128,7168]{1,0:T(8,128)(2,1)S(1)}, bf16[128,7168]{1,0:T(8,128)(2,1)}, u32[]{:S(2)}) copy-start(bf16[128,7168]{1,0:T(8,128)(2,1)} %lay_ref.3) | copy-start | bytes 5505028
  3.1 9.5 %copy-start.2 = (bf16[128,4224]{1,0:T(8,128)(2,1)S(1)}, bf16[128,4224]{1,0:T(8,128)(2,1)}, u32[]{:S(2)}) copy-start(bf16[128,4224]{1,0:T(8,128)(2,1)} %shard_map.126.to_core) | copy-start | bytes 3244036
  3.2 9.4 %collective-permute-start.3 = (bf16[128,4224]{1,0:T(8,128)(2,1)}, bf16[128,4224]{1,0:T(8,128)(2,1)S(1)}, u32[]{:S(2)}, u32[]{:S(2)}) collective-permute-start(bf16[128,4224]{1,0:T(8,128)(2,1)} %shard_map.126.to_core), channel_id=1, source_target_pairs={{0,32},{32,0},{1,33},{33,1},{2,34},{34,2},{3,35},{35,3},{4,36},{36... | collective-permute-start | bytes 3244040 | tf_op jit(solution)/shard_map/ppermute | solution.py:319
  4.2 30.0 %collective-permute-start.1 = (bf16[128,2304]{1,0:T(8,128)(2,1)S(1)}, bf16[128,2304]{1,0:T(8,128)(2,1)S(1)}, u32[]{:S(2)}, u32[]{:S(2)}) collective-permute-start(bf16[128,2304]{1,0:T(8,128)(2,1)S(1)} %get-tuple-element.32), channel_id=1, source_target_pairs={{0,64},{64,0},{128,192},{192,128},{1,65},{65,1},{129,193},{193,129... | collective-permute-start | bytes 1769480 | tf_op jit(solution)/shard_map/ppermute | solution.py:337
  7.6 30.1 %collective-permute-start.2 = (bf16[128,2304]{1,0:T(8,128)(2,1)S(1)}, bf16[128,2304]{1,0:T(8,128)(2,1)S(1)}, u32[]{:S(2)}, u32[]{:S(2)}) collective-permute-start(bf16[128,2304]{1,0:T(8,128)(2,1)S(1)} %get-tuple-element.33), channel_id=1, source_target_pairs={{0,192},{192,0},{64,128},{128,64},{1,193},{193,1},{65,129},{129,65... | collective-permute-start | bytes 1769480 | tf_op jit(solution)/shard_map/ppermute | solution.py:338
  15.0 22.8 %collective-permute-start.4 = (bf16[256,1664]{1,0:T(8,128)(2,1)S(1)}, bf16[256,1664]{1,0:T(8,128)(2,1)S(1)}, u32[]{:S(2)}, u32[]{:S(2)}) collective-permute-start(bf16[256,1664]{1,0:T(8,128)(2,1)S(1)} %get-tuple-element.37), channel_id=1, source_target_pairs={{0,8},{1,9},{2,10},{3,11},{4,12},{5,13},{6,14},{7,15},{8,0},{9,1},... | collective-permute-start | bytes 2555912 | tf_op jit(solution)/shard_map/ppermute | solution.py:355
  18.1 20.3 %collective-permute-start.5 = (bf16[256,1664]{1,0:T(8,128)(2,1)S(1)}, bf16[256,1664]{1,0:T(8,128)(2,1)S(1)}, u32[]{:S(2)}, u32[]{:S(2)}) collective-permute-start(bf16[256,1664]{1,0:T(8,128)(2,1)S(1)} %get-tuple-element.38), channel_id=1, source_target_pairs={{0,4},{1,5},{2,6},{3,7},{4,8},{5,9},{6,10},{7,11},{8,12},{9,13},{1... | collective-permute-start | bytes 2555912 | tf_op jit(solution)/shard_map/ppermute | solution.py:355
  18.7 19.8 %collective-permute-start.6 = (bf16[256,1664]{1,0:T(8,128)(2,1)S(1)}, bf16[256,1664]{1,0:T(8,128)(2,1)S(1)}, u32[]{:S(2)}, u32[]{:S(2)}) collective-permute-start(bf16[256,1664]{1,0:T(8,128)(2,1)S(1)} %get-tuple-element.39), channel_id=1, source_target_pairs={{0,12},{1,13},{2,14},{3,15},{4,0},{5,1},{6,2},{7,3},{8,4},{9,5},{1... | collective-permute-start | bytes 2555912 | tf_op jit(solution)/shard_map/ppermute | solution.py:355
  34.2 6.6 %collective-permute-start = (bf16[128,4096]{1,0:T(8,128)(2,1)S(1)}, bf16[128,4096]{1,0:T(8,128)(2,1)S(1)}, u32[]{:S(2)}, u32[]{:S(2)}) collective-permute-start(bf16[128,4096]{1,0:T(8,128)(2,1)S(1)} %shard_map.123), channel_id=1, source_target_pairs={{0,32},{32,0},{1,33},{33,1},{2,34},{34,2},{3,35},{35,3},{4,36},{36... | collective-permute-start | bytes 3145736 | tf_op jit(solution)/shard_map/ppermute | solution.py:348
  38.5 2.4 %collective-permute-start.7 = (bf16[128,2816]{1,0:T(8,128)(2,1)S(1)}, bf16[128,2816]{1,0:T(8,128)(2,1)S(1)}, u32[]{:S(2)}, u32[]{:S(2)}) collective-permute-start(bf16[128,2816]{1,0:T(8,128)(2,1)S(1)} %get-tuple-element.40), channel_id=1, source_target_pairs={{0,32},{32,0},{1,33},{33,1},{2,34},{34,2},{3,35},{35,3},{4,36},{36... | collective-permute-start | bytes 2162696 | tf_op jit(solution)/shard_map/ppermute | solution.py:368
  38.5 8.6 %collective-permute-start.8 = (bf16[128,1280]{1,0:T(8,128)(2,1)S(1)}, bf16[128,1280]{1,0:T(8,128)(2,1)S(1)}, u32[]{:S(2)}, u32[]{:S(2)}) collective-permute-start(bf16[128,1280]{1,0:T(8,128)(2,1)S(1)} %get-tuple-element.42), channel_id=1, source_target_pairs={{0,32},{32,0},{1,33},{33,1},{2,34},{34,2},{3,35},{35,3},{4,36},{36... | collective-permute-start | bytes 983048 | tf_op jit(solution)/shard_map/ppermute | solution.py:373
  41.7 16.3 %collective-permute-start.10 = (bf16[128,1152]{1,0:T(8,128)(2,1)S(1)}, bf16[128,1152]{1,0:T(8,128)(2,1)S(1)}, u32[]{:S(2)}, u32[]{:S(2)}) collective-permute-start(bf16[128,1152]{1,0:T(8,128)(2,1)S(1)} %get-tuple-element.51), channel_id=1, source_target_pairs={{0,64},{64,0},{128,192},{192,128},{1,65},{65,1},{129,193},{193,129... | collective-permute-start | bytes 884744 | tf_op jit(solution)/shard_map/ppermute | solution.py:372
  43.3 18.7 %collective-permute-start.9 = (bf16[128,1152]{1,0:T(8,128)(2,1)S(1)}, bf16[128,1152]{1,0:T(8,128)(2,1)S(1)}, u32[]{:S(2)}, u32[]{:S(2)}) collective-permute-start(bf16[128,1152]{1,0:T(8,128)(2,1)S(1)} %get-tuple-element.50), channel_id=1, source_target_pairs={{0,192},{192,0},{64,128},{128,64},{1,193},{193,1},{65,129},{129,65... | collective-permute-start | bytes 884744 | tf_op jit(solution)/shard_map/ppermute | solution.py:372
  47.1 15.0 %collective-permute-start.11 = (bf16[4,64,576]{2,1,0:T(8,128)(2,1)S(1)}, bf16[4,64,576]{2,1,0:T(8,128)(2,1)S(1)}, u32[]{:S(2)}, u32[]{:S(2)}) collective-permute-start(bf16[4,64,576]{2,1,0:T(8,128)(2,1)S(1)} %get-tuple-element.55), channel_id=1, source_target_pairs={{0,2},{1,3},{2,0},{3,1},{4,6},{5,7},{6,4},{7,5},{8,10},{9,11},{10,... | collective-permute-start | bytes 884744 | tf_op jit(solution)/shard_map/ppermute | solution.py:380
  49.4 12.7 %collective-permute-start.12 = (bf16[4,64,576]{2,1,0:T(8,128)(2,1)S(1)}, bf16[4,64,576]{2,1,0:T(8,128)(2,1)S(1)}, u32[]{:S(2)}, u32[]{:S(2)}) collective-permute-start(bf16[4,64,576]{2,1,0:T(8,128)(2,1)S(1)} %get-tuple-element.56), channel_id=1, source_target_pairs={{0,1},{1,2},{2,3},{3,0},{4,5},{5,6},{6,7},{7,4},{8,9},{9,10},{10,1... | collective-permute-start | bytes 884744 | tf_op jit(solution)/shard_map/ppermute | solution.py:380
  49.4 12.7 %collective-permute-start.13 = (bf16[4,64,576]{2,1,0:T(8,128)(2,1)S(1)}, bf16[4,64,576]{2,1,0:T(8,128)(2,1)S(1)}, u32[]{:S(2)}, u32[]{:S(2)}) collective-permute-start(bf16[4,64,576]{2,1,0:T(8,128)(2,1)S(1)} %get-tuple-element.57), channel_id=1, source_target_pairs={{0,3},{1,0},{2,1},{3,2},{4,7},{5,4},{6,5},{7,6},{8,11},{9,8},{10,9... | collective-permute-start | bytes 884744 | tf_op jit(solution)/shard_map/ppermute | solution.py:380
  58.1 15.2 %collective-permute-start.17 = (bf16[128,640]{1,0:T(8,128)(2,1)S(1)}, bf16[128,640]{1,0:T(8,128)(2,1)S(1)}, u32[]{:S(2)}, u32[]{:S(2)}) collective-permute-start(bf16[128,640]{1,0:T(8,128)(2,1)S(1)} %get-tuple-element.46), channel_id=1, source_target_pairs={{0,192},{192,0},{64,128},{128,64},{1,193},{193,1},{65,129},{129,65... | collective-permute-start | bytes 491528 | tf_op jit(solution)/shard_map/ppermute | solution.py:376
  62.0 14.0 %collective-permute-start.18 = (bf16[128,640]{1,0:T(8,128)(2,1)S(1)}, bf16[128,640]{1,0:T(8,128)(2,1)S(1)}, u32[]{:S(2)}, u32[]{:S(2)}) collective-permute-start(bf16[128,640]{1,0:T(8,128)(2,1)S(1)} %get-tuple-element.59), channel_id=1, source_target_pairs={{0,64},{64,0},{128,192},{192,128},{1,65},{65,1},{129,193},{193,129... | collective-permute-start | bytes 491528 | tf_op jit(solution)/shard_map/ppermute | solution.py:376
  62.0 17.2 %copy-start.6 = (f32[1,128,3584]{2,1,0:T(8,128)S(1)}, f32[1,128,3584]{2,1,0:T(8,128)}, u32[]{:S(2)}) copy-start(f32[1,128,3584]{2,1,0:T(8,128)} %param.16) | copy-start | bytes 5505028
  62.0 17.2 %copy-start.4 = (f32[1,128,3584]{2,1,0:T(8,128)S(1)}, f32[1,128,3584]{2,1,0:T(8,128)}, u32[]{:S(2)}) copy-start(f32[1,128,3584]{2,1,0:T(8,128)} %param.14) | copy-start | bytes 5505028
  62.0 17.2 %copy-start.5 = (f32[1,128,3584]{2,1,0:T(8,128)S(1)}, f32[1,128,3584]{2,1,0:T(8,128)}, u32[]{:S(2)}) copy-start(f32[1,128,3584]{2,1,0:T(8,128)} %param.15) | copy-start | bytes 5505028
  62.3 16.7 %collective-permute-start.14 = (bf16[2,32,576]{2,1,0:T(8,128)(2,1)S(1)}, bf16[2,32,576]{2,1,0:T(8,128)(2,1)S(1)}, u32[]{:S(2)}, u32[]{:S(2)}) collective-permute-start(bf16[2,32,576]{2,1,0:T(8,128)(2,1)S(1)} %bitcast.28), channel_id=1, source_target_pairs={{0,128},{64,192},{128,0},{192,64},{1,129},{65,193},{129,1},{193,65... | collective-permute-start | bytes 221192 | tf_op jit(solution)/shard_map/ppermute | solution.py:387
  69.2 9.8 %collective-permute-start.15 = (bf16[2,32,576]{2,1,0:T(8,128)(2,1)S(1)}, bf16[2,32,576]{2,1,0:T(8,128)(2,1)S(1)}, u32[]{:S(2)}, u32[]{:S(2)}) collective-permute-start(bf16[2,32,576]{2,1,0:T(8,128)(2,1)S(1)} %bitcast.27), channel_id=1, source_target_pairs={{0,64},{64,128},{128,192},{192,0},{1,65},{65,129},{129,193},{193,1... | collective-permute-start | bytes 221192 | tf_op jit(solution)/shard_map/ppermute | solution.py:387
  69.2 9.8 %collective-permute-start.16 = (bf16[2,32,576]{2,1,0:T(8,128)(2,1)S(1)}, bf16[2,32,576]{2,1,0:T(8,128)(2,1)S(1)}, u32[]{:S(2)}, u32[]{:S(2)}) collective-permute-start(bf16[2,32,576]{2,1,0:T(8,128)(2,1)S(1)} %bitcast.26), channel_id=1, source_target_pairs={{0,192},{64,0},{128,64},{192,128},{1,193},{65,1},{129,65},{193,129... | collective-permute-start | bytes 221192 | tf_op jit(solution)/shard_map/ppermute | solution.py:387
  76.0 3.1 %collective-permute-start.19 = (bf16[16,128]{1,0:T(8,128)(2,1)S(1)}, bf16[16,128]{1,0:T(8,128)(2,1)S(1)}, u32[]{:S(2)}, u32[]{:S(2)}) collective-permute-start(bf16[16,128]{1,0:T(8,128)(2,1)S(1)} %slice_add_fusion.1), channel_id=1, source_target_pairs={{0,32},{32,0},{1,33},{33,1},{2,34},{34,2},{3,35},{35,3},{4,36},{36... | collective-permute-start | bytes 12296 | tf_op jit(solution)/shard_map/ppermute | solution.py:393
  79.1 4.1 %collective-permute-start.20 = (bf16[32,576]{1,0:T(8,128)(2,1)S(1)}, bf16[32,576]{1,0:T(8,128)(2,1)S(1)}, u32[]{:S(2)}, u32[]{:S(2)}) collective-permute-start(bf16[32,576]{1,0:T(8,128)(2,1)S(1)} %fusion.6), channel_id=1, source_target_pairs={{0,16},{16,0},{1,17},{17,1},{2,18},{18,2},{3,19},{19,3},{4,20},{20... | collective-permute-start | bytes 110600 | tf_op jit(solution)/shard_map/ppermute | solution.py:390
  79.2 4.0 %copy-start.7 = (f32[28,576]{1,0:T(8,128)S(1)}, f32[28,576]{1,0:T(8,128)}, u32[]{:S(2)}) copy-start(f32[28,576]{1,0:T(8,128)} %param.19) | copy-start | bytes 193540
  79.2 3.9 %copy-start.8 = (f32[28,576]{1,0:T(8,128)S(1)}, f32[28,576]{1,0:T(8,128)}, u32[]{:S(2)}) copy-start(f32[28,576]{1,0:T(8,128)} %param.21) | copy-start | bytes 193540
  79.2 3.9 %copy-start.9 = (f32[28,576]{1,0:T(8,128)S(1)}, f32[28,576]{1,0:T(8,128)}, u32[]{:S(2)}) copy-start(f32[28,576]{1,0:T(8,128)} %param.20) | copy-start | bytes 193540

commit v5 on v4

--- a/solution.py
+++ b/solution.py
@@ -100,11 +100,15 @@
     copy.wait()
 
 
+def ring_place(me, step):
+    return (me + step * (1 + 2 * (me % 2))) % 4
+
+
 def part_copies(lay_ref, ref, side, sems):
     j = lax.axis_index("zh")
     copies = []
     for n in range(4):
-        start = pl.multiple_of((2 * lax.rem(j + n, 4) + side) * PART, 128)
+        start = pl.multiple_of((2 * ring_place(j, n) + side) * PART, 128)
         copies.append(
             pltpu.make_async_copy(
                 lay_ref.at[:, pl.ds(start, PART)],
@@ -221,8 +225,8 @@
     for copy in copies:
         copy.start()
     place = lax.broadcasted_iota(jnp.int32, (1, 1024), 1)
-    first = (place // 256 + x + core * (y - x)) % 4
-    second = (place // 64 % 4 + y + core * (x - y)) % 4
+    first = ring_place(x + core * (y - x), place // 256)
+    second = ring_place(y + core * (x - y), place // 64 % 4)
     half = (place // 32 % 2 + low) % 2
     row = place % PAD
     spot = half * 448 + first * (112 - 84 * core) + second * (28 + 84 * core) + row
@@ -278,7 +282,7 @@
         for x in range(4):
             for y in range(4):
                 along_x = (core + stage) % 2 == 0
-                to = ((x + step) % 4, y) if along_x else (x, (y + step) % 4)
+                to = (ring_place(x, step), y) if along_x else (x, ring_place(y, step))
                 pairs.append((core * 16 + x * 4 + y, core * 16 + to[0] * 4 + to[1]))
     return pairs
 
@@ -383,8 +387,8 @@
     line = add(after(keep, p_a, p_b), *terms).reshape(4, 2, PAD, KV)
 
     mine = line[0]
-    for step in (2, 1, 3):
-        term = lax.ppermute(line[step].astype(bf16), "zh", [(i, (i + step) % 4) for i in range(4)])
+    for step in (1, 3, 2):
+        term = lax.ppermute(line[step].astype(bf16), "zh", [(i, ring_place(i, step)) for i in range(4)])
         mine = mine + term.astype(f32)
     theirs = mine[1].astype(bf16)
     dense_grad = mine[0] + lax.ppermute(theirs, "zl", swap).astype(f32)

time: 84.3 us -> 83.5 us (level)
  starting transfers between devices: 39.5 us -> 33.6 us
  waiting for transfers between devices: 29.8 us -> 35.3 us
    ppermute x3, starting transfers between devices: 11 us -> 7.47 us  [on_device(): lax.ppermute(line[step].astype(bf16), 'zh', [(i, ring_place(i, step)) for...]
    ppermute x3, waiting for transfers between devices: 2.93 us -> 6.45 us  [on_device(): lax.ppermute(line[step].astype(bf16), 'zh', [(i, ring_place(i, step)) for...]
    ppermute x1, waiting for transfers between devices: 2.74 us -> 0.47 us  [on_device(): lax.ppermute(q_b, 'zh', PAIR_A)]
    ppermute x3, starting transfers between devices: 6.35 us -> 4.25 us  [on_device(): lax.ppermute(blocks[step], axes, plane_pairs(0, step))]
    ppermute x1, waiting for transfers between devices: 12.8 us -> 14.9 us  [on_device(): near_a = lax.ppermute(to_a, 'zh', PAIR_A)]
    ppermute x1, waiting for transfers between devices: 0.01 us -> 1.88 us  [on_device(): lax.ppermute(q_a, 'zh', PAIR_B)]
  transfers between devices with their start and end apart: 21 -> 21, of which waited for: 8 -> 9; matrix products, arithmetic and copies ran while one was open for 0% -> 0% of each run, Pallas kernels for 11% -> 11%
where the time goes in v5:
time: 83.5 us; the launch traced here: 83.4 us
  waiting for transfers between devices  35.3 us (42%)
  starting transfers between devices  33.6 us (40%)
  Pallas kernels  11.9 us (14%)
  between operations  1.67 us (2%)
  other arithmetic  0.9 us (1%)
    ppermute x1, waiting for transfers between devices, on_device(): near_a = lax.ppermute(to_a, 'zh', PAIR_A)  14.9 us
    pallas_call x9, Pallas kernels, in_vmem(): pl.pallas_call(kernel, out_shape=[jax.ShapeDtypeStruct(shape, dtype) for...  9.05 us
    ppermute x3, starting transfers between devices, on_device(): lax.ppermute(line[step].astype(bf16), 'zh', [(i, ring_place(i, step)) for...  7.47 us
    ppermute x3, waiting for transfers between devices, on_device(): lax.ppermute(line[step].astype(bf16), 'zh', [(i, ring_place(i, step)) for...  6.45 us
    ppermute x1, waiting for transfers between devices, on_device(): lax.ppermute(p_b, 'zh', PAIR_A)  6.29 us
    ppermute x1, starting transfers between devices, on_device(): near_b = lax.ppermute(to_b, 'zh', PAIR_B)  4.48 us
    ppermute x3, starting transfers between devices, on_device(): lax.ppermute(blocks[step], axes, plane_pairs(0, step))  4.25 us
    ppermute x3, starting transfers between devices, on_device(): lax.ppermute(block, axes, plane_pairs(1, step))  4.09 us
  transfers between devices with their start and end apart: 21, of which 9 were waited for; matrix products, arithmetic and copies ran while one was open for 0% of the time, Pallas kernels for 11%

profile of v5, /device:TPU:8, one launch (start us, length us, event | category | flops | bytes accessed | tf_op | source)
XLA Modules:
  0.0 83.4 jit_solution(3768110884285182029)
XLA Ops:
  0.7 2.5 %shard_map.126.to_core = bf16[128,4224]{1,0:T(8,128)(2,1)} custom-call(bf16[128,7168]{1,0:T(8,128)(2,1)} %lay_ref.3, bf16[576,128]{1,0:T(8,128)(2,1)} %bitcast.25), custom_call_target="tpu_custom_call" | custom-call | tf_op jit(solution)/shard_map/pallas_call | solution.py:146
  3.1 0.0 copy-start.2
  3.2 0.1 collective-permute-start.3
  4.0 0.2 shard_map.122
  4.2 3.4 %collective-permute-start.1 = (bf16[128,2304]{1,0:T(8,128)(2,1)S(1)}, bf16[128,2304]{1,0:T(8,128)(2,1)S(1)}, u32[]{:S(2)}, u32[]{:S(2)}) collective-permute-start(bf16[128,2304]{1,0:T(8,128)(2,1)S(1)} %get-tuple-element.32), channel_id=1, source_target_pairs={{0,64},{64,0},{128,192},{192,128},{1,65},{65,1},{129,193},{193,129... | collective-permute-start | bytes 1769480 | tf_op jit(solution)/shard_map/ppermute | solution.py:341
  7.6 4.5 %collective-permute-start.2 = (bf16[128,2304]{1,0:T(8,128)(2,1)S(1)}, bf16[128,2304]{1,0:T(8,128)(2,1)S(1)}, u32[]{:S(2)}, u32[]{:S(2)}) collective-permute-start(bf16[128,2304]{1,0:T(8,128)(2,1)S(1)} %get-tuple-element.33), channel_id=1, source_target_pairs={{0,192},{192,0},{64,128},{128,64},{1,193},{193,1},{65,129},{129,65... | collective-permute-start | bytes 1769480 | tf_op jit(solution)/shard_map/ppermute | solution.py:342
  12.0 0.5 shard_map.125
  12.6 0.0 collective-permute-done.3.got
  12.6 2.3 %shard_map.127 = (bf16[256,1664]{1,0:T(8,128)(2,1)S(1)}, bf16[256,1664]{1,0:T(8,128)(2,1)S(1)}, bf16[256,1664]{1,0:T(8,128)(2,1)S(1)}, bf16[256,1664]{1,0:T(8,128)(2,1)S(1)}) custom-call(bf16[896,1024]{1,0:T(8,128)(2,1)S(1)} %get-tuple-element.35.order, bf16[128,3584]{1,0:T(8,128)(2,1)S(1)} %get-tuple-element.36.own, bf16[128,4224]{1,0:T(8,128)(2,1)S(1)} %copy-done.2, ...), custom_call_target="tpu_custom_call" | custom-call | tf_op jit(solution)/shard_map/pallas_call | solution.py:146
  15.0 3.1 %collective-permute-start.4 = (bf16[256,1664]{1,0:T(8,128)(2,1)S(1)}, bf16[256,1664]{1,0:T(8,128)(2,1)S(1)}, u32[]{:S(2)}, u32[]{:S(2)}) collective-permute-start(bf16[256,1664]{1,0:T(8,128)(2,1)S(1)} %get-tuple-element.37), channel_id=1, source_target_pairs={{0,8},{1,9},{2,10},{3,11},{4,12},{5,13},{6,14},{7,15},{8,0},{9,1},... | collective-permute-start | bytes 2555912 | tf_op jit(solution)/shard_map/ppermute | solution.py:359
  18.1 0.6 collective-permute-start.5
  18.7 0.6 collective-permute-start.6
  19.2 0.1 shard_map.123
  19.3 14.9 %collective-permute-done.1.near_a = bf16[128,2304]{1,0:T(8,128)(2,1)S(1)} collective-permute-done((bf16[128,2304]{1,0:T(8,128)(2,1)S(1)}, bf16[128,2304]{1,0:T(8,128)(2,1)S(1)}, u32[]{:S(2)}, u32[]{:S(2)}) %collective-permute-start.1) | collective-permute-done | bytes 589856 | tf_op jit(solution)/shard_map/ppermute | solution.py:341
  34.2 3.4 %collective-permute-done.2.near_b = bf16[128,2304]{1,0:T(8,128)(2,1)S(1)} collective-permute-done((bf16[128,2304]{1,0:T(8,128)(2,1)S(1)}, bf16[128,2304]{1,0:T(8,128)(2,1)S(1)}, u32[]{:S(2)}, u32[]{:S(2)}) %collective-permute-start.2) | collective-permute-done | bytes 589856 | tf_op jit(solution)/shard_map/ppermute | solution.py:342
  37.6 0.1 shard_map.124
  37.7 0.8 collective-permute-done.5.b2
  38.5 0.0 collective-permute-done.6.b3
  38.5 0.5 collective-permute-start.8
  39.0 1.8 %shard_map.130 = (f32[4,64,576]{2,1,0:T(8,128)S(1)}, bf16[4,64,576]{2,1,0:T(8,128)(2,1)S(1)}, bf16[4,64,576]{2,1,0:T(8,128)(2,1)S(1)}, bf16[4,64,576]{2,1,0:T(8,128)(2,1)S(1)}) custom-call(bf16[256,1664]{1,0:T(8,128)(2,1)S(1)} %get-tuple-element.44.b0, bf16[256,1664]{1,0:T(8,128)(2,1)S(1)} %collective-permute-done.4.b1, ...), custom_call_target="tpu_custom_call" | custom-call | tf_op jit(solution)/shard_map/pallas_call | solution.py:146
  40.8 0.0 collective-permute-done.7.far.columns
  40.9 0.9 %shard_map.128 = (bf16[128,1152]{1,0:T(8,128)(2,1)S(1)}, bf16[128,1152]{1,0:T(8,128)(2,1)S(1)}, f32[2,128,1152]{2,1,0:T(8,128)S(1)}) custom-call(bf16[128,3584]{1,0:T(8,128)(2,1)S(1)} %bitcast.17, bf16[128,512]{1,0:T(8,128)(2,1)S(1)} %get-tuple-element.31.own, bf16[128,4096]{1,0:T(8,128)(2,1)S(1)} %collective-permute-done.sib, ...), custom_call_target="tpu_custom_call" | custom-call | tf_op jit(solution)/shard_map/pallas_call | solution.py:146
  41.7 1.6 %collective-permute-start.10 = (bf16[128,1152]{1,0:T(8,128)(2,1)S(1)}, bf16[128,1152]{1,0:T(8,128)(2,1)S(1)}, u32[]{:S(2)}, u32[]{:S(2)}) collective-permute-start(bf16[128,1152]{1,0:T(8,128)(2,1)S(1)} %get-tuple-element.51), channel_id=1, source_target_pairs={{0,64},{64,0},{128,192},{192,128},{1,65},{65,1},{129,193},{193,129... | collective-permute-start | bytes 884744 | tf_op jit(solution)/shard_map/ppermute | solution.py:376
  43.3 3.8 %collective-permute-start.9 = (bf16[128,1152]{1,0:T(8,128)(2,1)S(1)}, bf16[128,1152]{1,0:T(8,128)(2,1)S(1)}, u32[]{:S(2)}, u32[]{:S(2)}) collective-permute-start(bf16[128,1152]{1,0:T(8,128)(2,1)S(1)} %get-tuple-element.50), channel_id=1, source_target_pairs={{0,192},{192,0},{64,128},{128,64},{1,193},{193,1},{65,129},{129,65... | collective-permute-start | bytes 884744 | tf_op jit(solution)/shard_map/ppermute | solution.py:376
  47.1 2.3 %collective-permute-start.11 = (bf16[4,64,576]{2,1,0:T(8,128)(2,1)S(1)}, bf16[4,64,576]{2,1,0:T(8,128)(2,1)S(1)}, u32[]{:S(2)}, u32[]{:S(2)}) collective-permute-start(bf16[4,64,576]{2,1,0:T(8,128)(2,1)S(1)} %get-tuple-element.55), channel_id=1, source_target_pairs={{0,2},{1,3},{2,0},{3,1},{4,6},{5,7},{6,4},{7,5},{8,10},{9,11},{10,... | collective-permute-start | bytes 884744 | tf_op jit(solution)/shard_map/ppermute | solution.py:384
  49.4 1.3 %collective-permute-start.12 = (bf16[4,64,576]{2,1,0:T(8,128)(2,1)S(1)}, bf16[4,64,576]{2,1,0:T(8,128)(2,1)S(1)}, u32[]{:S(2)}, u32[]{:S(2)}) collective-permute-start(bf16[4,64,576]{2,1,0:T(8,128)(2,1)S(1)} %get-tuple-element.56), channel_id=1, source_target_pairs={{0,1},{1,0},{2,3},{3,2},{4,5},{5,4},{6,7},{7,6},{8,9},{9,8},{10,11... | collective-permute-start | bytes 884744 | tf_op jit(solution)/shard_map/ppermute | solution.py:384
  50.7 0.4 collective-permute-start.13
  51.2 0.6 shard_map.129
  51.8 6.3 %collective-permute-done.10.refs_2_.b0 = bf16[128,1152]{1,0:T(8,128)(2,1)S(1)} collective-permute-done((bf16[128,1152]{1,0:T(8,128)(2,1)S(1)}, bf16[128,1152]{1,0:T(8,128)(2,1)S(1)}, u32[]{:S(2)}, u32[]{:S(2)}) %collective-permute-start.10) | collective-permute-done | bytes 294944 | tf_op jit(solution)/shard_map/ppermute | solution.py:376
  58.1 3.9 %collective-permute-start.17 = (bf16[128,640]{1,0:T(8,128)(2,1)S(1)}, bf16[128,640]{1,0:T(8,128)(2,1)S(1)}, u32[]{:S(2)}, u32[]{:S(2)}) collective-permute-start(bf16[128,640]{1,0:T(8,128)(2,1)S(1)} %get-tuple-element.46), channel_id=1, source_target_pairs={{0,192},{192,0},{64,128},{128,64},{1,193},{193,1},{65,129},{129,65... | collective-permute-start | bytes 491528 | tf_op jit(solution)/shard_map/ppermute | solution.py:380
  62.0 0.0 copy-start.4
  62.0 0.0 copy-start.5
  62.1 0.0 collective-permute-done.12
  62.1 0.0 collective-permute-done.13
  62.1 0.1 fusion.7
  62.3 3.0 %collective-permute-start.14 = (bf16[2,32,576]{2,1,0:T(8,128)(2,1)S(1)}, bf16[2,32,576]{2,1,0:T(8,128)(2,1)S(1)}, u32[]{:S(2)}, u32[]{:S(2)}) collective-permute-start(bf16[2,32,576]{2,1,0:T(8,128)(2,1)S(1)} %bitcast.28), channel_id=1, source_target_pairs={{0,64},{64,0},{128,192},{192,128},{1,65},{65,1},{129,193},{193,129... | collective-permute-start | bytes 221192 | tf_op jit(solution)/shard_map/ppermute | solution.py:391
  65.2 4.5 %collective-permute-start.15 = (bf16[2,32,576]{2,1,0:T(8,128)(2,1)S(1)}, bf16[2,32,576]{2,1,0:T(8,128)(2,1)S(1)}, u32[]{:S(2)}, u32[]{:S(2)}) collective-permute-start(bf16[2,32,576]{2,1,0:T(8,128)(2,1)S(1)} %bitcast.27), channel_id=1, source_target_pairs={{0,192},{64,128},{128,64},{192,0},{1,193},{65,129},{129,65},{193,1... | collective-permute-start | bytes 221192 | tf_op jit(solution)/shard_map/ppermute | solution.py:391
  69.7 1.9 %collective-permute-done.17.a1 = bf16[128,640]{1,0:T(8,128)(2,1)S(1)} collective-permute-done((bf16[128,640]{1,0:T(8,128)(2,1)S(1)}, bf16[128,640]{1,0:T(8,128)(2,1)S(1)}, u32[]{:S(2)}, u32[]{:S(2)}) %collective-permute-start.17) | collective-permute-done | bytes 163872 | tf_op jit(solution)/shard_map/ppermute | solution.py:380
  71.6 0.5 collective-permute-done.18.b1
  72.1 5.5 %collective-permute-done.14 = bf16[2,32,576]{2,1,0:T(8,128)(2,1)S(1)} collective-permute-done((bf16[2,32,576]{2,1,0:T(8,128)(2,1)S(1)}, bf16[2,32,576]{2,1,0:T(8,128)(2,1)S(1)}, u32[]{:S(2)}, u32[]{:S(2)}) %collective-permute-start.14) | collective-permute-done | bytes 73760 | tf_op jit(solution)/shard_map/ppermute | solution.py:391
  77.7 0.9 %collective-permute-done.16 = bf16[2,32,576]{2,1,0:T(8,128)(2,1)S(1)} collective-permute-done((bf16[2,32,576]{2,1,0:T(8,128)(2,1)S(1)}, bf16[2,32,576]{2,1,0:T(8,128)(2,1)S(1)}, u32[]{:S(2)}, u32[]{:S(2)}) %collective-permute-start.16) | collective-permute-done | bytes 73760 | tf_op jit(solution)/shard_map/ppermute | solution.py:391
  78.6 0.1 collective-permute-start.20
  78.8 0.0 copy-start.7
  78.8 0.0 copy-start.8
  78.8 0.0 copy-start.9
  78.8 2.8 %shard_map.132 = f32[128,3584]{1,0:T(8,128)} custom-call(f32[2,128,1152]{2,1,0:T(8,128)S(1)} %get-tuple-element.41.keep0, f32[2,128,640]{2,1,0:T(8,128)S(1)} %get-tuple-element.58.keep1, bf16[128,1152]{1,0:T(8,128)(2,1)S(1)} %collective-permute-done.9.refs_1_.a0, bf16[128,640]{1,0:T(8,128)(2,1)S(1)} %collective-permute-done.17.a1, ...), custom_call_target="tpu_custom_call" | custom-call | flops 10000000000 | bytes 4000000 | tf_op jit(solution)/shard_map/pallas_call | solution.py:207
  81.6 1.1 %collective-permute-done.20 = bf16[32,576]{1,0:T(8,128)(2,1)S(1)} collective-permute-done((bf16[32,576]{1,0:T(8,128)(2,1)S(1)}, bf16[32,576]{1,0:T(8,128)(2,1)S(1)}, u32[]{:S(2)}, u32[]{:S(2)}) %collective-permute-start.20) | collective-permute-done | bytes 36896 | tf_op jit(solution)/shard_map/ppermute | solution.py:394
  82.7 0.7 multiply_subtract_fusion
  (33 shorter events, 0.2 us)
Async XLA Ops:
  0.6 3.3 %copy-start = (bf16[1,128,3584]{2,1,0:T(8,128)(2,1)S(1)}, bf16[1,128,3584]{2,1,0:T(8,128)(2,1)}, u32[]{:S(2)}) copy-start(bf16[1,128,3584]{2,1,0:T(8,128)(2,1)} %param.12) | copy-start | bytes 2752516
  0.6 3.3 %copy-start.3 = (bf16[1,128,1024]{2,1,0:T(8,128)(2,1)S(1)}, bf16[1,128,1024]{2,1,0:T(8,128)(2,1)}, u32[]{:S(2)}) copy-start(bf16[1,128,1024]{2,1,0:T(8,128)(2,1)} %param.11) | copy-start | bytes 786436
  0.7 11.4 %copy-start.1 = (bf16[128,7168]{1,0:T(8,128)(2,1)S(1)}, bf16[128,7168]{1,0:T(8,128)(2,1)}, u32[]{:S(2)}) copy-start(bf16[128,7168]{1,0:T(8,128)(2,1)} %lay_ref.3) | copy-start | bytes 5505028
  3.1 9.5 %copy-start.2 = (bf16[128,4224]{1,0:T(8,128)(2,1)S(1)}, bf16[128,4224]{1,0:T(8,128)(2,1)}, u32[]{:S(2)}) copy-start(bf16[128,4224]{1,0:T(8,128)(2,1)} %shard_map.126.to_core) | copy-start | bytes 3244036
  3.2 9.4 %collective-permute-start.3 = (bf16[128,4224]{1,0:T(8,128)(2,1)}, bf16[128,4224]{1,0:T(8,128)(2,1)S(1)}, u32[]{:S(2)}, u32[]{:S(2)}) collective-permute-start(bf16[128,4224]{1,0:T(8,128)(2,1)} %shard_map.126.to_core), channel_id=1, source_target_pairs={{0,32},{32,0},{1,33},{33,1},{2,34},{34,2},{3,35},{35,3},{4,36},{36... | collective-permute-start | bytes 3244040 | tf_op jit(solution)/shard_map/ppermute | solution.py:323
  4.2 30.0 %collective-permute-start.1 = (bf16[128,2304]{1,0:T(8,128)(2,1)S(1)}, bf16[128,2304]{1,0:T(8,128)(2,1)S(1)}, u32[]{:S(2)}, u32[]{:S(2)}) collective-permute-start(bf16[128,2304]{1,0:T(8,128)(2,1)S(1)} %get-tuple-element.32), channel_id=1, source_target_pairs={{0,64},{64,0},{128,192},{192,128},{1,65},{65,1},{129,193},{193,129... | collective-permute-start | bytes 1769480 | tf_op jit(solution)/shard_map/ppermute | solution.py:341
  7.6 30.1 %collective-permute-start.2 = (bf16[128,2304]{1,0:T(8,128)(2,1)S(1)}, bf16[128,2304]{1,0:T(8,128)(2,1)S(1)}, u32[]{:S(2)}, u32[]{:S(2)}) collective-permute-start(bf16[128,2304]{1,0:T(8,128)(2,1)S(1)} %get-tuple-element.33), channel_id=1, source_target_pairs={{0,192},{192,0},{64,128},{128,64},{1,193},{193,1},{65,129},{129,65... | collective-permute-start | bytes 1769480 | tf_op jit(solution)/shard_map/ppermute | solution.py:342
  15.0 22.8 %collective-permute-start.4 = (bf16[256,1664]{1,0:T(8,128)(2,1)S(1)}, bf16[256,1664]{1,0:T(8,128)(2,1)S(1)}, u32[]{:S(2)}, u32[]{:S(2)}) collective-permute-start(bf16[256,1664]{1,0:T(8,128)(2,1)S(1)} %get-tuple-element.37), channel_id=1, source_target_pairs={{0,8},{1,9},{2,10},{3,11},{4,12},{5,13},{6,14},{7,15},{8,0},{9,1},... | collective-permute-start | bytes 2555912 | tf_op jit(solution)/shard_map/ppermute | solution.py:359
  18.1 20.4 %collective-permute-start.5 = (bf16[256,1664]{1,0:T(8,128)(2,1)S(1)}, bf16[256,1664]{1,0:T(8,128)(2,1)S(1)}, u32[]{:S(2)}, u32[]{:S(2)}) collective-permute-start(bf16[256,1664]{1,0:T(8,128)(2,1)S(1)} %get-tuple-element.38), channel_id=1, source_target_pairs={{0,4},{1,5},{2,6},{3,7},{4,0},{5,1},{6,2},{7,3},{8,12},{9,13},{10,... | collective-permute-start | bytes 2555912 | tf_op jit(solution)/shard_map/ppermute | solution.py:359
  18.7 19.8 %collective-permute-start.6 = (bf16[256,1664]{1,0:T(8,128)(2,1)S(1)}, bf16[256,1664]{1,0:T(8,128)(2,1)S(1)}, u32[]{:S(2)}, u32[]{:S(2)}) collective-permute-start(bf16[256,1664]{1,0:T(8,128)(2,1)S(1)} %get-tuple-element.39), channel_id=1, source_target_pairs={{0,12},{1,13},{2,14},{3,15},{4,8},{5,9},{6,10},{7,11},{8,4},{9,5},... | collective-permute-start | bytes 2555912 | tf_op jit(solution)/shard_map/ppermute | solution.py:359
  34.2 6.6 %collective-permute-start = (bf16[128,4096]{1,0:T(8,128)(2,1)S(1)}, bf16[128,4096]{1,0:T(8,128)(2,1)S(1)}, u32[]{:S(2)}, u32[]{:S(2)}) collective-permute-start(bf16[128,4096]{1,0:T(8,128)(2,1)S(1)} %shard_map.123), channel_id=1, source_target_pairs={{0,32},{32,0},{1,33},{33,1},{2,34},{34,2},{3,35},{35,3},{4,36},{36... | collective-permute-start | bytes 3145736 | tf_op jit(solution)/shard_map/ppermute | solution.py:352
  38.5 2.4 %collective-permute-start.7 = (bf16[128,2816]{1,0:T(8,128)(2,1)S(1)}, bf16[128,2816]{1,0:T(8,128)(2,1)S(1)}, u32[]{:S(2)}, u32[]{:S(2)}) collective-permute-start(bf16[128,2816]{1,0:T(8,128)(2,1)S(1)} %get-tuple-element.40), channel_id=1, source_target_pairs={{0,32},{32,0},{1,33},{33,1},{2,34},{34,2},{3,35},{35,3},{4,36},{36... | collective-permute-start | bytes 2162696 | tf_op jit(solution)/shard_map/ppermute | solution.py:372
  38.5 8.6 %collective-permute-start.8 = (bf16[128,1280]{1,0:T(8,128)(2,1)S(1)}, bf16[128,1280]{1,0:T(8,128)(2,1)S(1)}, u32[]{:S(2)}, u32[]{:S(2)}) collective-permute-start(bf16[128,1280]{1,0:T(8,128)(2,1)S(1)} %get-tuple-element.42), channel_id=1, source_target_pairs={{0,32},{32,0},{1,33},{33,1},{2,34},{34,2},{3,35},{35,3},{4,36},{36... | collective-permute-start | bytes 983048 | tf_op jit(solution)/shard_map/ppermute | solution.py:377
  41.7 16.3 %collective-permute-start.10 = (bf16[128,1152]{1,0:T(8,128)(2,1)S(1)}, bf16[128,1152]{1,0:T(8,128)(2,1)S(1)}, u32[]{:S(2)}, u32[]{:S(2)}) collective-permute-start(bf16[128,1152]{1,0:T(8,128)(2,1)S(1)} %get-tuple-element.51), channel_id=1, source_target_pairs={{0,64},{64,0},{128,192},{192,128},{1,65},{65,1},{129,193},{193,129... | collective-permute-start | bytes 884744 | tf_op jit(solution)/shard_map/ppermute | solution.py:376
  43.3 18.7 %collective-permute-start.9 = (bf16[128,1152]{1,0:T(8,128)(2,1)S(1)}, bf16[128,1152]{1,0:T(8,128)(2,1)S(1)}, u32[]{:S(2)}, u32[]{:S(2)}) collective-permute-start(bf16[128,1152]{1,0:T(8,128)(2,1)S(1)} %get-tuple-element.50), channel_id=1, source_target_pairs={{0,192},{192,0},{64,128},{128,64},{1,193},{193,1},{65,129},{129,65... | collective-permute-start | bytes 884744 | tf_op jit(solution)/shard_map/ppermute | solution.py:376
  47.1 15.0 %collective-permute-start.11 = (bf16[4,64,576]{2,1,0:T(8,128)(2,1)S(1)}, bf16[4,64,576]{2,1,0:T(8,128)(2,1)S(1)}, u32[]{:S(2)}, u32[]{:S(2)}) collective-permute-start(bf16[4,64,576]{2,1,0:T(8,128)(2,1)S(1)} %get-tuple-element.55), channel_id=1, source_target_pairs={{0,2},{1,3},{2,0},{3,1},{4,6},{5,7},{6,4},{7,5},{8,10},{9,11},{10,... | collective-permute-start | bytes 884744 | tf_op jit(solution)/shard_map/ppermute | solution.py:384
  49.4 12.7 %collective-permute-start.12 = (bf16[4,64,576]{2,1,0:T(8,128)(2,1)S(1)}, bf16[4,64,576]{2,1,0:T(8,128)(2,1)S(1)}, u32[]{:S(2)}, u32[]{:S(2)}) collective-permute-start(bf16[4,64,576]{2,1,0:T(8,128)(2,1)S(1)} %get-tuple-element.56), channel_id=1, source_target_pairs={{0,1},{1,0},{2,3},{3,2},{4,5},{5,4},{6,7},{7,6},{8,9},{9,8},{10,11... | collective-permute-start | bytes 884744 | tf_op jit(solution)/shard_map/ppermute | solution.py:384
  50.7 11.3 %collective-permute-start.13 = (bf16[4,64,576]{2,1,0:T(8,128)(2,1)S(1)}, bf16[4,64,576]{2,1,0:T(8,128)(2,1)S(1)}, u32[]{:S(2)}, u32[]{:S(2)}) collective-permute-start(bf16[4,64,576]{2,1,0:T(8,128)(2,1)S(1)} %get-tuple-element.57), channel_id=1, source_target_pairs={{0,3},{1,2},{2,1},{3,0},{4,7},{5,6},{6,5},{7,4},{8,11},{9,10},{10,... | collective-permute-start | bytes 884744 | tf_op jit(solution)/shard_map/ppermute | solution.py:384
  58.1 13.5 %collective-permute-start.17 = (bf16[128,640]{1,0:T(8,128)(2,1)S(1)}, bf16[128,640]{1,0:T(8,128)(2,1)S(1)}, u32[]{:S(2)}, u32[]{:S(2)}) collective-permute-start(bf16[128,640]{1,0:T(8,128)(2,1)S(1)} %get-tuple-element.46), channel_id=1, source_target_pairs={{0,192},{192,0},{64,128},{128,64},{1,193},{193,1},{65,129},{129,65... | collective-permute-start | bytes 491528 | tf_op jit(solution)/shard_map/ppermute | solution.py:380
  62.0 10.1 %collective-permute-start.18 = (bf16[128,640]{1,0:T(8,128)(2,1)S(1)}, bf16[128,640]{1,0:T(8,128)(2,1)S(1)}, u32[]{:S(2)}, u32[]{:S(2)}) collective-permute-start(bf16[128,640]{1,0:T(8,128)(2,1)S(1)} %get-tuple-element.59), channel_id=1, source_target_pairs={{0,64},{64,0},{128,192},{192,128},{1,65},{65,1},{129,193},{193,129... | collective-permute-start | bytes 491528 | tf_op jit(solution)/shard_map/ppermute | solution.py:380
  62.0 16.7 %copy-start.6 = (f32[1,128,3584]{2,1,0:T(8,128)S(1)}, f32[1,128,3584]{2,1,0:T(8,128)}, u32[]{:S(2)}) copy-start(f32[1,128,3584]{2,1,0:T(8,128)} %param.16) | copy-start | bytes 5505028
  62.0 16.7 %copy-start.4 = (f32[1,128,3584]{2,1,0:T(8,128)S(1)}, f32[1,128,3584]{2,1,0:T(8,128)}, u32[]{:S(2)}) copy-start(f32[1,128,3584]{2,1,0:T(8,128)} %param.14) | copy-start | bytes 5505028
  62.0 16.7 %copy-start.5 = (f32[1,128,3584]{2,1,0:T(8,128)S(1)}, f32[1,128,3584]{2,1,0:T(8,128)}, u32[]{:S(2)}) copy-start(f32[1,128,3584]{2,1,0:T(8,128)} %param.15) | copy-start | bytes 5505028
  62.3 15.4 %collective-permute-start.14 = (bf16[2,32,576]{2,1,0:T(8,128)(2,1)S(1)}, bf16[2,32,576]{2,1,0:T(8,128)(2,1)S(1)}, u32[]{:S(2)}, u32[]{:S(2)}) collective-permute-start(bf16[2,32,576]{2,1,0:T(8,128)(2,1)S(1)} %bitcast.28), channel_id=1, source_target_pairs={{0,64},{64,0},{128,192},{192,128},{1,65},{65,1},{129,193},{193,129... | collective-permute-start | bytes 221192 | tf_op jit(solution)/shard_map/ppermute | solution.py:391
  65.2 12.4 %collective-permute-start.15 = (bf16[2,32,576]{2,1,0:T(8,128)(2,1)S(1)}, bf16[2,32,576]{2,1,0:T(8,128)(2,1)S(1)}, u32[]{:S(2)}, u32[]{:S(2)}) collective-permute-start(bf16[2,32,576]{2,1,0:T(8,128)(2,1)S(1)} %bitcast.27), channel_id=1, source_target_pairs={{0,192},{64,128},{128,64},{192,0},{1,193},{65,129},{129,65},{193,1... | collective-permute-start | bytes 221192 | tf_op jit(solution)/shard_map/ppermute | solution.py:391
  69.7 8.8 %collective-permute-start.16 = (bf16[2,32,576]{2,1,0:T(8,128)(2,1)S(1)}, bf16[2,32,576]{2,1,0:T(8,128)(2,1)S(1)}, u32[]{:S(2)}, u32[]{:S(2)}) collective-permute-start(bf16[2,32,576]{2,1,0:T(8,128)(2,1)S(1)} %bitcast.26), channel_id=1, source_target_pairs={{0,128},{64,192},{128,0},{192,64},{1,129},{65,193},{129,1},{193,65... | collective-permute-start | bytes 221192 | tf_op jit(solution)/shard_map/ppermute | solution.py:391
  72.1 6.6 %collective-permute-start.19 = (bf16[16,128]{1,0:T(8,128)(2,1)S(1)}, bf16[16,128]{1,0:T(8,128)(2,1)S(1)}, u32[]{:S(2)}, u32[]{:S(2)}) collective-permute-start(bf16[16,128]{1,0:T(8,128)(2,1)S(1)} %slice_add_fusion.1), channel_id=1, source_target_pairs={{0,32},{32,0},{1,33},{33,1},{2,34},{34,2},{3,35},{35,3},{4,36},{36... | collective-permute-start | bytes 12296 | tf_op jit(solution)/shard_map/ppermute | solution.py:397
  78.6 4.1 %collective-permute-start.20 = (bf16[32,576]{1,0:T(8,128)(2,1)S(1)}, bf16[32,576]{1,0:T(8,128)(2,1)S(1)}, u32[]{:S(2)}, u32[]{:S(2)}) collective-permute-start(bf16[32,576]{1,0:T(8,128)(2,1)S(1)} %fusion.6), channel_id=1, source_target_pairs={{0,16},{16,0},{1,17},{17,1},{2,18},{18,2},{3,19},{19,3},{4,20},{20... | collective-permute-start | bytes 110600 | tf_op jit(solution)/shard_map/ppermute | solution.py:394
  78.8 4.0 %copy-start.7 = (f32[28,576]{1,0:T(8,128)S(1)}, f32[28,576]{1,0:T(8,128)}, u32[]{:S(2)}) copy-start(f32[28,576]{1,0:T(8,128)} %param.19) | copy-start | bytes 193540
  78.8 3.9 %copy-start.8 = (f32[28,576]{1,0:T(8,128)S(1)}, f32[28,576]{1,0:T(8,128)}, u32[]{:S(2)}) copy-start(f32[28,576]{1,0:T(8,128)} %param.21) | copy-start | bytes 193540
  78.8 3.9 %copy-start.9 = (f32[28,576]{1,0:T(8,128)S(1)}, f32[28,576]{1,0:T(8,128)}, u32[]{:S(2)}) copy-start(f32[28,576]{1,0:T(8,128)} %param.20) | copy-start | bytes 193540
